TPU v7x, 128 devices: a whole 4x4x4 slice. The times are simulated.
128 devices in a mesh: expert: 8 (over z, core), dp: 16 (over y, x).
Axes of the slice: x: 4, y: 4, z: 4, core: 2. Of those that a mesh axis runs over, the one named last changes fastest.
Arguments:
- hidden_in: bfloat16 [2, 9216, 768], P(None, ('expert', 'dp')), may hold values from -6 to 6
- lengths: int32 [2, 8, 3], P(None, 'expert'), may hold values from 1 to 1116, as said below
- routes: int32 [2, 9216, 2], P(None, ('expert', 'dp')), may hold values from 0 to 7, all different within a row; in each aligned block of 72 rows (0 to 71, 72 to 143, ..., all dimensions but the last counted through in order) at most 20 rows name the same one
- norm_gains: bfloat16 [4, 768], P(None, ('expert', 'dp')), may hold values from 0.5 to 1.5
- qkv_weights: bfloat16 [2, 3, 768, 768], P(None, None, ('expert', 'dp')), may hold values from -0.21875 to 0.21875
- out_weights: bfloat16 [2, 768, 768], P(None, ('expert', 'dp')), may hold values from -0.4375 to 0.4375
- rel_table: bfloat16 [384], P(('expert', 'dp')), may hold values from -3 to 3
- ffn_in: bfloat16 [768, 3072], P(('expert', 'dp')), may hold values from -0.21875 to 0.21875
- ffn_out: bfloat16 [3072, 768], P(('expert', 'dp')), may hold values from -0.109375 to 0.109375
- router: bfloat16 [768, 8], P(('expert', 'dp')), may hold values from -0.15625 to 0.15625
- expert_in: bfloat16 [8, 768, 3072], P('expert', 'dp'), may hold values from -0.21875 to 0.21875
- expert_out: bfloat16 [8, 3072, 768], P('expert', 'dp'), may hold values from -0.109375 to 0.109375
- cotangent: bfloat16 [2, 9216, 768], P(None, ('expert', 'dp')), may hold values from -6 to 6
Outputs:
- hidden_out: float32 [2, 9216, 768], P(None, ('expert', 'dp'))
- grad_input: float32 [2, 9216, 768], P(None, ('expert', 'dp'))
- grad_gains: float32 [4, 768], P(None, ('expert', 'dp'))
- grad_qkv: float32 [2, 3, 768, 768], P(None, None, ('expert', 'dp'))
- grad_out_weights: float32 [2, 768, 768], P(None, ('expert', 'dp'))
- grad_rel_table: float32 [384], P(('expert', 'dp'))
- grad_ffn_in: float32 [768, 3072], P(('expert', 'dp'))
- grad_ffn_out: float32 [3072, 768], P(('expert', 'dp'))
- grad_router: float32 [768, 8], P(('expert', 'dp'))
- grad_expert_in: float32 [8, 768, 3072], P('expert', 'dp')
- grad_expert_out: float32 [8, 3072, 768], P('expert', 'dp')
Inputs may be any that keep to these rules, and one draw needn't show every extreme that they name: In each micro-batch and group the 3 lengths add up to 1152; one of them, at a place drawn from the seed, is 1116 and reaches from the group's first device to its last. `routes`: each token names two different experts. Among the 72 tokens of one device in one micro-batch no expert is named more than 20 times; in some devices' tokens one expert is named exactly 20 times.
All inputs are finite; a program needn't handle non-finite values.
Results may differ from a plain program's by a relative error of at most 0.04.
Values may be sent and summed in bfloat16 or wider, within the bound.
No kernel may reach another device: no remote copies, remote signals or barrier semaphores. Data moves between devices by JAX's collectives and lax.ppermute only.
A program may use at most 256 MiB of HBM per device.

v0:
```python
import jax
import jax.numpy as jnp
from jax import lax
from jax.sharding import PartitionSpec as P

HEADS = 12
HEAD_DIM = 64
BUCKETS = 16


EPSILON = 1e-06
NEGATIVE = -1e30


def normalize(values, scales):
    return values * lax.rsqrt(jnp.mean(values * values, axis=-1, keepdims=True) + EPSILON) * scales


def smooth_gate(values):
    return jax.nn.gelu(values, approximate=True)


def softmax_pair(values):
    return jax.nn.softmax(values, axis=-1)


def bucket_index(distance):
    distance = jnp.maximum(distance, 0)
    result = jnp.minimum(distance, 7)
    for exponent in range(3, 11):
        result = result + (distance >= 2**exponent).astype(jnp.int32)
    return result


def document_of(bounds, position):
    doc_ends = jnp.cumsum(bounds)
    return jnp.sum((position[:, None] >= doc_ends[None, :]).astype(jnp.int32), axis=1)


def project(operand, matrix):
    return jnp.dot(operand, matrix, preferred_element_type=jnp.float32)


def project_back(operand, matrix):
    return jnp.einsum("ta,ba->tb", operand, matrix, preferred_element_type=jnp.float32)


def outer_sum(operand, matrix):
    return jnp.einsum("ta,tb->ab", operand, matrix, preferred_element_type=jnp.float32)


def pair_layout(bounds, query_pos, key_pos):
    same_doc = document_of(bounds, query_pos)[:, None] == document_of(bounds, key_pos)[None, :]
    allowed = same_doc & (key_pos[None, :] <= query_pos[:, None])
    buckets = bucket_index(query_pos[:, None] - key_pos[None, :])
    one_hot = buckets[:, :, None] == jnp.arange(BUCKETS, dtype=jnp.int32)[None, None, :]
    return (allowed, one_hot.astype(jnp.float32), one_hot.astype(jnp.bfloat16))


def score_layout(bounds, my_rank, tok_count, group_count):
    query_pos = my_rank * tok_count + jnp.arange(tok_count, dtype=jnp.int32)
    key_pos = jnp.arange(group_count, dtype=jnp.int32)
    return pair_layout(bounds, query_pos, key_pos)


def attention_scores(query_heads, key_heads, bias_table, allowed, one_hot_f):
    raw_scores = jnp.einsum(
        "qhd,khd->hqk", query_heads, key_heads, preferred_element_type=jnp.float32
    ) * HEAD_DIM ** (-0.5)
    rel_bias = jnp.einsum("hb,qkb->hqk", bias_table, one_hot_f, precision=lax.Precision.HIGHEST)
    return jnp.where(allowed[None], raw_scores + rel_bias, NEGATIVE)


def attend_forward(stream, scales, weights, w_out, bias_table, layout):
    allowed, one_hot_f, one_hot_b = layout
    tok_count = stream.shape[0]
    normed = normalize(stream, scales).astype(jnp.bfloat16)
    queries = project(normed, weights[0]).astype(jnp.bfloat16)
    key_local = project(normed, weights[1]).astype(jnp.bfloat16)
    value_local = project(normed, weights[2]).astype(jnp.bfloat16)
    gathered_keys, gathered_values = (
        lax.all_gather(key_local, "dp", axis=0, tiled=True),
        lax.all_gather(value_local, "dp", axis=0, tiled=True),
    )
    query_heads = queries.reshape(tok_count, HEADS, HEAD_DIM)
    key_heads = gathered_keys.reshape(-1, HEADS, HEAD_DIM)
    value_heads = gathered_values.reshape(-1, HEADS, HEAD_DIM)
    scores = attention_scores(query_heads, key_heads, bias_table, allowed, one_hot_f)
    row_peak = jnp.max(scores, axis=-1, keepdims=True)
    weights_exp = jnp.exp(scores - row_peak)
    row_total = jnp.sum(weights_exp, axis=-1, keepdims=True)
    probability = (weights_exp / row_total).astype(jnp.bfloat16)
    log_total = row_peak + jnp.log(row_total)
    attended = jnp.einsum(
        "hqk,khd->qhd", probability, value_heads, preferred_element_type=jnp.float32
    )
    attended = attended.reshape(tok_count, -1).astype(jnp.bfloat16)
    saved = (normed, queries, gathered_keys, gathered_values, attended, log_total)
    return (stream + project(attended, w_out), saved)


def attend_backward(grad_stream, stream, scales, weights, w_out, bias_table, layout, saved):
    allowed, one_hot_f, one_hot_b = layout
    normed, queries, gathered_keys, gathered_values, attended, log_total = saved
    tok_count = stream.shape[0]
    score_scale = HEAD_DIM ** (-0.5)
    grad_branch = grad_stream.astype(jnp.bfloat16)
    grad_w_out = outer_sum(attended, grad_branch)
    grad_attended = project_back(grad_branch, w_out).astype(jnp.bfloat16)
    grad_heads = grad_attended.reshape(tok_count, HEADS, HEAD_DIM)
    query_heads = queries.reshape(tok_count, HEADS, HEAD_DIM)
    key_heads = gathered_keys.reshape(-1, HEADS, HEAD_DIM)
    value_heads = gathered_values.reshape(-1, HEADS, HEAD_DIM)
    scores = attention_scores(query_heads, key_heads, bias_table, allowed, one_hot_f)
    probability = jnp.exp(scores - log_total)
    grad_probs = jnp.einsum(
        "qhd,khd->hqk", grad_heads, value_heads, preferred_element_type=jnp.float32
    )
    row_inner = jnp.sum(probability * grad_probs, axis=-1, keepdims=True)
    grad_scores = (probability * (grad_probs - row_inner)).astype(jnp.bfloat16)
    grad_table = jnp.einsum(
        "hqk,qkb->hb", grad_scores, one_hot_b, preferred_element_type=jnp.float32
    )
    grad_query = (
        jnp.einsum("hqk,khd->qhd", grad_scores, key_heads, preferred_element_type=jnp.float32)
        * score_scale
    )
    grad_query = grad_query.reshape(tok_count, -1).astype(jnp.bfloat16)
    key_terms = jnp.einsum(
        "hqk,qhd->khd", grad_scores, query_heads, preferred_element_type=jnp.float32
    )
    key_terms = key_terms.reshape(gathered_keys.shape) * score_scale
    value_terms = jnp.einsum(
        "hqk,qhd->khd",
        probability.astype(jnp.bfloat16),
        grad_heads,
        preferred_element_type=jnp.float32,
    )
    value_terms = value_terms.reshape(gathered_values.shape)
    grad_key, grad_value = (
        lax.psum_scatter(key_terms, "dp", scatter_dimension=0, tiled=True),
        lax.psum_scatter(value_terms, "dp", scatter_dimension=0, tiled=True),
    )
    grad_key = grad_key.astype(jnp.bfloat16)
    grad_value = grad_value.astype(jnp.bfloat16)
    grad_weights = jnp.stack(
        [outer_sum(normed, grad_query), outer_sum(normed, grad_key), outer_sum(normed, grad_value)]
    )
    grad_normed = (
        project_back(grad_query, weights[0])
        + project_back(grad_key, weights[1])
        + project_back(grad_value, weights[2])
    )
    unused_norm, pullback = jax.vjp(normalize, stream, scales)
    grad_inner, grad_scales = pullback(grad_normed)
    return (grad_stream + grad_inner, grad_scales, grad_weights, grad_w_out, grad_table)


def dense_forward(stream, scales, w_first, w_second):
    normed = normalize(stream, scales).astype(jnp.bfloat16)
    pre_gate = project(normed, w_first)
    hidden = smooth_gate(pre_gate).astype(jnp.bfloat16)
    return (stream + project(hidden, w_second), (normed, pre_gate, hidden))


def dense_backward(grad_stream, stream, scales, w_first, w_second, saved):
    normed, pre_gate, hidden = saved
    grad_branch = grad_stream.astype(jnp.bfloat16)
    grad_second = outer_sum(hidden, grad_branch)
    grad_hidden = project_back(grad_branch, w_second)
    unused_gate, gate_pullback = jax.vjp(smooth_gate, pre_gate)
    grad_pre = gate_pullback(grad_hidden)[0].astype(jnp.bfloat16)
    grad_first = outer_sum(normed, grad_pre)
    grad_normed = project_back(grad_pre, w_first)
    unused_norm, pullback = jax.vjp(normalize, stream, scales)
    grad_inner, grad_scales = pullback(grad_normed)
    return (grad_stream + grad_inner, grad_scales, grad_first, grad_second)


def slot_plan(choice_ids, expert_count):
    flat_ids = choice_ids.reshape(-1)
    route_marks = (flat_ids[:, None] == jnp.arange(expert_count, dtype=jnp.int32)[None, :]).astype(
        jnp.int32
    )
    slot_ranks = jnp.sum((jnp.cumsum(route_marks, axis=0) - route_marks) * route_marks, axis=1)
    return (flat_ids, slot_ranks)


def expert_forward(stream, scales, router_w, w_first, w_second, choice_ids):
    tok_count, width_count = stream.shape
    expert_count = router_w.shape[1]
    capacity = 9 * tok_count // (4 * expert_count)
    normed = normalize(stream, scales).astype(jnp.bfloat16)
    logits = jnp.dot(normed.astype(jnp.float32), router_w, precision=lax.Precision.HIGHEST)
    pick_table = (
        choice_ids[:, :, None] == jnp.arange(expert_count, dtype=jnp.int32)[None, None, :]
    ).astype(jnp.float32)
    chosen = jnp.einsum("tke,te->tk", pick_table, logits, precision=lax.Precision.HIGHEST)
    gate_weights = softmax_pair(chosen)
    flat_ids, slot_ranks = slot_plan(choice_ids, expert_count)
    outbound = jnp.zeros((expert_count, capacity, width_count), jnp.bfloat16)
    outbound = outbound.at[flat_ids, slot_ranks].set(jnp.repeat(normed, 2, axis=0))
    arrived = lax.all_to_all(outbound, "expert", split_axis=0, concat_axis=0, tiled=True)
    expert_rows = arrived.reshape(-1, width_count)
    pre_gate = project(expert_rows, w_first[0])
    hidden = smooth_gate(pre_gate).astype(jnp.bfloat16)
    produced = project(hidden, w_second[0]).astype(jnp.bfloat16).reshape(arrived.shape)
    returned = lax.all_to_all(produced, "expert", split_axis=0, concat_axis=0, tiled=True)
    picked = returned[flat_ids, slot_ranks].astype(jnp.float32).reshape(tok_count, 2, width_count)
    combined = jnp.sum(gate_weights[:, :, None] * picked, axis=1)
    saved = (
        normed,
        pick_table,
        chosen,
        gate_weights,
        flat_ids,
        slot_ranks,
        expert_rows,
        pre_gate,
        hidden,
        picked,
    )
    return (stream + combined, saved)


def expert_backward(grad_stream, stream, scales, router_w, w_first, w_second, saved):
    (
        normed,
        pick_table,
        chosen,
        gate_weights,
        flat_ids,
        slot_ranks,
        expert_rows,
        pre_gate,
        hidden,
        picked,
    ) = saved
    tok_count, width_count = stream.shape
    expert_count = router_w.shape[1]
    capacity = 9 * tok_count // (4 * expert_count)
    grad_gates = jnp.sum(grad_stream[:, None, :] * picked, axis=-1)
    grad_picked = (
        (gate_weights[:, :, None] * grad_stream[:, None, :])
        .astype(jnp.bfloat16)
        .reshape(-1, width_count)
    )
    outbound = (
        jnp.zeros((expert_count, capacity, width_count), jnp.bfloat16)
        .at[flat_ids, slot_ranks]
        .set(grad_picked)
    )
    arrived = lax.all_to_all(outbound, "expert", split_axis=0, concat_axis=0, tiled=True)
    grad_rows = arrived.reshape(-1, width_count)
    grad_second = outer_sum(hidden, grad_rows)[None]
    grad_hidden = project_back(grad_rows, w_second[0])
    unused_gate, gate_pullback = jax.vjp(smooth_gate, pre_gate)
    grad_pre = gate_pullback(grad_hidden)[0].astype(jnp.bfloat16)
    grad_first = outer_sum(expert_rows, grad_pre)[None]
    grad_sent = project_back(grad_pre, w_first[0]).reshape(arrived.shape)
    came_back = lax.all_to_all(grad_sent, "expert", split_axis=0, concat_axis=0, tiled=True)
    grad_normed = jnp.sum(
        came_back[flat_ids, slot_ranks].reshape(tok_count, 2, width_count), axis=1
    )
    unused_soft, soft_pullback = jax.vjp(softmax_pair, chosen)
    grad_chosen = soft_pullback(grad_gates)[0]
    grad_logits = jnp.einsum("tke,tk->te", pick_table, grad_chosen, precision=lax.Precision.HIGHEST)
    grad_router = jnp.einsum(
        "td,te->de", normed.astype(jnp.float32), grad_logits, precision=lax.Precision.HIGHEST
    )
    grad_normed = grad_normed + jnp.einsum(
        "te,de->td", grad_logits, router_w, precision=lax.Precision.HIGHEST
    )
    unused_norm, pullback = jax.vjp(normalize, stream, scales)
    grad_inner, grad_scales = pullback(grad_normed)
    return (grad_stream + grad_inner, grad_scales, grad_router, grad_first, grad_second)


def unpack_dense(parts):
    gain_rows, qkv_all, out_all, table_flat, first_dense, second_dense, router_w = parts
    bias_table = table_flat.astype(jnp.float32).reshape(2, HEADS, BUCKETS)
    return (
        gain_rows.astype(jnp.float32),
        qkv_all,
        out_all,
        bias_table,
        first_dense,
        second_dense,
        router_w.astype(jnp.float32),
    )


def on_device(
    hidden_in,
    lengths,
    routes,
    norm_gains,
    qkv_weights,
    out_weights,
    rel_table,
    ffn_in,
    ffn_out,
    router,
    expert_in,
    expert_out,
    cotangent,
):
    tok_count = hidden_in.shape[1]
    group_count = tok_count * lax.axis_size("dp")
    my_rank = lax.axis_index("dp")
    outputs_all = []
    grad_inputs_all = []
    totals = None
    for micro_index in range(hidden_in.shape[0]):
        forward_parts = (
            lax.all_gather(norm_gains, ("expert", "dp"), axis=1, tiled=True),
            lax.all_gather(qkv_weights, ("expert", "dp"), axis=2, tiled=True),
            lax.all_gather(out_weights, ("expert", "dp"), axis=1, tiled=True),
            lax.all_gather(rel_table, ("expert", "dp"), axis=0, tiled=True),
            lax.all_gather(ffn_in, ("expert", "dp"), axis=0, tiled=True),
            lax.all_gather(ffn_out, ("expert", "dp"), axis=0, tiled=True),
            lax.all_gather(router, ("expert", "dp"), axis=0, tiled=True),
        )
        forward_experts = (
            lax.all_gather(expert_in, "dp", axis=1, tiled=True),
            lax.all_gather(expert_out, "dp", axis=1, tiled=True),
        )
        gain_rows, qkv_all, out_all, bias_table, first_dense, second_dense, router_w = unpack_dense(
            forward_parts
        )
        bounds = lengths[micro_index, 0]
        layout = score_layout(bounds, my_rank, tok_count, group_count)
        stream_zero = hidden_in[micro_index].astype(jnp.float32)
        stream_one, saved_one = attend_forward(
            stream_zero, gain_rows[0], qkv_all[0], out_all[0], bias_table[0], layout
        )
        stream_two, saved_two = dense_forward(stream_one, gain_rows[1], first_dense, second_dense)
        stream_three, saved_three = attend_forward(
            stream_two, gain_rows[2], qkv_all[1], out_all[1], bias_table[1], layout
        )
        stream_four, saved_four = expert_forward(
            stream_three,
            gain_rows[3],
            router_w,
            forward_experts[0],
            forward_experts[1],
            routes[micro_index],
        )
        outputs_all.append(stream_four)
        backward_parts = (
            lax.all_gather(norm_gains, ("expert", "dp"), axis=1, tiled=True),
            lax.all_gather(qkv_weights, ("expert", "dp"), axis=2, tiled=True),
            lax.all_gather(out_weights, ("expert", "dp"), axis=1, tiled=True),
            lax.all_gather(rel_table, ("expert", "dp"), axis=0, tiled=True),
            lax.all_gather(ffn_in, ("expert", "dp"), axis=0, tiled=True),
            lax.all_gather(ffn_out, ("expert", "dp"), axis=0, tiled=True),
            lax.all_gather(router, ("expert", "dp"), axis=0, tiled=True),
        )
        backward_experts = (
            lax.all_gather(expert_in, "dp", axis=1, tiled=True),
            lax.all_gather(expert_out, "dp", axis=1, tiled=True),
        )
        gain_rows, qkv_all, out_all, bias_table, first_dense, second_dense, router_w = unpack_dense(
            backward_parts
        )
        grad_four = cotangent[micro_index].astype(jnp.float32)
        grad_three, gain_four, grad_route, expert_first_grad, expert_second_grad = expert_backward(
            grad_four,
            stream_three,
            gain_rows[3],
            router_w,
            backward_experts[0],
            backward_experts[1],
            saved_four,
        )
        grad_two, gain_three, qkv_two, out_two, table_two = attend_backward(
            grad_three,
            stream_two,
            gain_rows[2],
            qkv_all[1],
            out_all[1],
            bias_table[1],
            layout,
            saved_three,
        )
        grad_one, gain_two, dense_first_grad, dense_second_grad = dense_backward(
            grad_two, stream_one, gain_rows[1], first_dense, second_dense, saved_two
        )
        grad_zero, gain_one, qkv_one, out_one, table_one = attend_backward(
            grad_one,
            stream_zero,
            gain_rows[0],
            qkv_all[0],
            out_all[0],
            bias_table[0],
            layout,
            saved_one,
        )
        grad_inputs_all.append(grad_zero)
        contribution = (
            jnp.stack([gain_one, gain_two, gain_three, gain_four]),
            jnp.stack([qkv_one, qkv_two]),
            jnp.stack([out_one, out_two]),
            jnp.stack([table_one, table_two]).reshape(-1),
            dense_first_grad,
            dense_second_grad,
            grad_route,
            expert_first_grad,
            expert_second_grad,
        )
        totals = contribution if totals is None else jax.tree.map(jnp.add, totals, contribution)
    (
        gain_sum,
        qkv_sum,
        out_sum,
        table_sum,
        first_sum,
        second_sum,
        router_sum,
        expert_first_sum,
        expert_second_sum,
    ) = totals
    gain_part, qkv_part, out_part, table_part, first_part, second_part, router_part = (
        lax.psum_scatter(gain_sum, ("expert", "dp"), scatter_dimension=1, tiled=True),
        lax.psum_scatter(qkv_sum, ("expert", "dp"), scatter_dimension=2, tiled=True),
        lax.psum_scatter(out_sum, ("expert", "dp"), scatter_dimension=1, tiled=True),
        lax.psum_scatter(table_sum, ("expert", "dp"), scatter_dimension=0, tiled=True),
        lax.psum_scatter(first_sum, ("expert", "dp"), scatter_dimension=0, tiled=True),
        lax.psum_scatter(second_sum, ("expert", "dp"), scatter_dimension=0, tiled=True),
        lax.psum_scatter(router_sum, ("expert", "dp"), scatter_dimension=0, tiled=True),
    )
    expert_first_part, expert_second_part = (
        lax.psum_scatter(expert_first_sum, "dp", scatter_dimension=1, tiled=True),
        lax.psum_scatter(expert_second_sum, "dp", scatter_dimension=1, tiled=True),
    )
    return (
        jnp.stack(outputs_all),
        jnp.stack(grad_inputs_all),
        gain_part,
        qkv_part,
        out_part,
        table_part,
        first_part,
        second_part,
        router_part,
        expert_first_part,
        expert_second_part,
    )


def solution(mesh):
    return jax.shard_map(
        on_device,
        mesh=mesh,
        in_specs=(
            P(None, ("expert", "dp"), None),
            P(None, "expert", None),
            P(None, ("expert", "dp"), None),
            P(None, ("expert", "dp")),
            P(None, None, ("expert", "dp"), None),
            P(None, ("expert", "dp"), None),
            P(("expert", "dp")),
            P(("expert", "dp"), None),
            P(("expert", "dp"), None),
            P(("expert", "dp"), None),
            P("expert", "dp", None),
            P("expert", "dp", None),
            P(None, ("expert", "dp"), None),
        ),
        out_specs=(
            P(None, ("expert", "dp"), None),
            P(None, ("expert", "dp"), None),
            P(None, ("expert", "dp")),
            P(None, None, ("expert", "dp"), None),
            P(None, ("expert", "dp"), None),
            P(("expert", "dp")),
            P(("expert", "dp"), None),
            P(("expert", "dp"), None),
            P(("expert", "dp"), None),
            P("expert", "dp", None),
            P("expert", "dp", None),
        ),
        check_vma=False,
    )
```

profile of v0, /device:TPU:0, one launch (start us, length us, event | category | flops | bytes accessed | tf_op | source)
XLA Modules:
  0.0 2366.2 jit_solution(2925303248600283625)
XLA Ops:
  10.3 58.7 %all-gather = bf16[128,6,4]{1,2,0:T(4,128)(2,1)S(1)} all-gather(bf16[1,6,4]{1,2,0:T(4,128)(2,1)} %bitcast.611), channel_id=1, replica_groups=mesh['expert'=8,'dp'=16] {'expert','dp'}, dimensions={0}, use_global_device_ids=true | all-gather | bytes 6192 | tf_op jit(solution)/shard_map/all_gather | solution.py:316
  71.2 11.9 all-gather.18.cloned.1.call-done
  83.1 15.9 fusion.249
  107.6 63.7 %all-reduce.2 = bf16[384]{0:T(512)(128)(2,1)S(1)} all-reduce(bf16[384]{0:T(512)(128)(2,1)S(1)} %dynamic-update-slice), channel_id=1, replica_groups=mesh['expert'=8,'dp'=16] {'expert','dp'}, use_global_device_ids=true, to_apply=%add.2 | all-reduce | flops 384 | bytes 1536
  176.7 7.8 fusion.250
  184.7 32.8 %all-gather.44.cloned.1.call-done = bf16[128,6,3072]{2,1,0:T(8,128)(2,1)} async-done(((bf16[1,6,3072]{2,1,0:T(8,128)(2,1)}), bf16[128,6,3072]{2,1,0:T(8,128)(2,1)}) %all-gather.44.cloned.1.call-update) | async-done | bytes 4718608 | tf_op jit(solution)/shard_map/all_gather | solution.py:320
  217.5 7.8 reshape.1014
  234.2 28.0 %all-gather.38.cloned.1.call-done = bf16[1152,768]{1,0:T(8,128)(2,1)} async-done(((bf16[72,768]{1,0:T(8,128)(2,1)}), bf16[1152,768]{1,0:T(8,128)(2,1)}) %all-gather.38.cloned.1.call-update) | async-done | bytes 1769488 | tf_op jit(solution)/shard_map/all_gather | solution.py:82
  266.0 7.0 fusion.253
  273.1 35.5 %all-gather.36.cloned.1.call-done = bf16[1152,768]{1,0:T(8,128)(2,1)} async-done(((bf16[72,768]{1,0:T(8,128)(2,1)}), bf16[1152,768]{1,0:T(8,128)(2,1)}) %all-gather.36.cloned.1.call-update) | async-done | bytes 1769488 | tf_op jit(solution)/shard_map/all_gather | solution.py:83
  312.5 42.5 %all-gather.22.cloned.1.call-done = bf16[1152,768]{1,0:T(8,128)(2,1)} async-done(((bf16[72,768]{1,0:T(8,128)(2,1)}), bf16[1152,768]{1,0:T(8,128)(2,1)}) %all-gather.22.cloned.1.call-update) | async-done | bytes 1769488 | tf_op jit(solution)/shard_map/all_gather | solution.py:82
  367.4 56.9 %all-gather.26.cloned.1.call-done = bf16[3072,768]{1,0:T(8,128)(2,1)} async-done(((bf16[24,768]{1,0:T(8,128)(2,1)}), bf16[3072,768]{1,0:T(8,128)(2,1)}) %all-gather.26.cloned.1.call-update) | async-done | bytes 4718608 | tf_op jit(solution)/shard_map/all_gather | solution.py:321
  436.6 32.4 %all-gather.20.cloned.1.call-done = bf16[1152,768]{1,0:T(8,128)(2,1)} async-done(((bf16[72,768]{1,0:T(8,128)(2,1)}), bf16[1152,768]{1,0:T(8,128)(2,1)}) %all-gather.20.cloned.1.call-update) | async-done | bytes 1769488 | tf_op jit(solution)/shard_map/all_gather | solution.py:83
  494.1 60.1 %all-gather.2 = bf16[128,6,8]{2,1,0:T(8,128)(2,1)S(1)} all-gather(bf16[1,6,8]{2,1,0:T(8,128)(2,1)S(1)} %bitcast.606), channel_id=1, replica_groups=mesh['expert'=8,'dp'=16] {'expert','dp'}, dimensions={0}, use_global_device_ids=true | all-gather | bytes 12384 | tf_op jit(solution)/shard_map/all_gather | solution.py:322
  609.8 20.6 scatter_fusion.2
  636.3 20.5 scatter_fusion
  689.2 33.5 %all-gather.32.cloned.1.call-done = bf16[1,768,3072]{2,1,0:T(8,128)(2,1)} async-done(((bf16[1,48,3072]{2,1,0:T(8,128)(2,1)}), bf16[1,768,3072]{2,1,0:T(8,128)(2,1)}) %all-gather.32.cloned.1.call-update) | async-done | bytes 4718608 | tf_op jit(solution)/shard_map/all_gather | solution.py:325
  727.3 51.0 %all-gather.34.cloned.1.call-done = bf16[1,3072,768]{2,1,0:T(8,128)(2,1)} async-done(((bf16[1,192,768]{2,1,0:T(8,128)(2,1)}), bf16[1,3072,768]{2,1,0:T(8,128)(2,1)}) %all-gather.34.cloned.1.call-update) | async-done | bytes 4718608 | tf_op jit(solution)/shard_map/all_gather | solution.py:326
  828.4 8.8 scatter_fusion.3
  838.2 8.8 scatter_fusion.1
  853.0 7.4 all-to-all-done.2
  954.0 308.2 %all-reduce.27 = (bf16[1152,768]{0,1:T(8,128)(2,1)}, bf16[1152,768]{0,1:T(8,128)(2,1)}, bf16[1152,768]{0,1:T(8,128)(2,1)}, bf16[1152,768]{0,1:T(8,128)(2,1)}) all-reduce(f32[1152,768]{0,1:T(8,128)} %bitcast.543, f32[1152,768]{0,1:T(8,128)} %bitcast.539, f32[1152,768]{0,1:T(8,128)} %bitcast.541, ...), channel_id=6, replica_groups=mesh['expert'=8,'dp'=16] {'dp'}, use_global_device_ids=true, to_apply=%region_56.57.clone | all-reduce | flops 3538944 | bytes 21233664
  1328.2 5.9 copy.267
  1334.0 308.0 %all-reduce.28 = (bf16[1152,768]{0,1:T(8,128)(2,1)}, bf16[1152,768]{0,1:T(8,128)(2,1)S(1)}, bf16[1152,768]{0,1:T(8,128)(2,1)}, bf16[1152,768]{0,1:T(8,128)(2,1)}) all-reduce(f32[1152,768]{0,1:T(8,128)} %bitcast.542, f32[1152,768]{0,1:T(8,128)} %bitcast.537, ...), channel_id=8, replica_groups=mesh['expert'=8,'dp'=16] {'dp'}, use_global_device_ids=true, to_apply=%region_61.62.clone | all-reduce | flops 3538944 | bytes 21233664
  1654.6 6.5 maximum_bitcast_fusion
  1670.6 7.8 maximum_add_fusion
  1678.4 18.0 copy.266
  1729.4 396.7 %fusion = f32[8,3072]{1,0:T(8,128)S(1)} fusion(f32[768,3072]{1,0:T(8,128)} %convolution_add_fusion.1), kind=kCustom, calls=%all-reduce-scatter | all-reduce-scatter fusion | flops 3145729 | bytes 9535488
  2156.0 11.8 collective-permute-start.17
  2173.1 68.1 %all-reduce.18 = (f32[4,768]{1,0:T(4,128)S(1)}, f32[384]{0:T(512)S(1)}, f32[768,8]{1,0:T(8,128)S(1)}) all-reduce(f32[4,768]{1,0:T(4,128)S(1)} %maximum_add_fusion.3, f32[384]{0:T(512)S(1)} %add.516, f32[768,8]{1,0:T(8,128)S(1)} %convolution_add_fusion.2), channel_id=10, replica_groups=mesh['expert'=8,'dp'=16] {'expert','dp'}, use_global_device_ids=true, to_apply=%region_72.73.clone | all-reduce | flops 9600 | bytes 76800
  2261.8 6.2 collective-permute-start.23
  2318.5 31.5 %concatenate.30 = f32[262,3072]{1,0:T(8,128)S(1)} concatenate(f32[6,3072]{1,0:T(8,128)S(1)} %copy-done.167, f32[8,3072]{1,0:T(8,128)} %copy-done.188, f32[8,3072]{1,0:T(8,128)} %copy-done.186, f32[8,3072]{1,0:T(8,128)} %copy-done.185, f32[8,3072]{1,0:T(8,128)} %copy-done.184, f32[8,3072]{1,0:T(8,128)} %copy-done.183, f32[8,3072]{1,0:T(8,128)} %copy-done.182, ...), dimensions={0} | concatenate | bytes 6438912
  (943 shorter events, 566.7 us)
Async XLA Ops:
  7.2 75.9 %all-gather.18.cloned.1.call-start = ((), (), s32[]{:S(2)}) async-start(), calls=%async_computation.11 | async-start | bytes 7133184 | tf_op jit(solution)/shard_map/all_gather | solution.py:317
  8.7 167.9 %all-gather.24.cloned.1.call-start = ((), (), s32[]{:S(2)}) async-start(), calls=%async_computation.14 | async-start | bytes 2377728 | tf_op jit(solution)/shard_map/all_gather | solution.py:318
  9.5 208.1 %all-gather.44.cloned.1.call-start = ((), (), s32[]{:S(2)}) async-start(), calls=%async_computation.27 | async-start | bytes 6340608 | tf_op jit(solution)/shard_map/all_gather | solution.py:320
  10.2 251.9 %all-gather.38.cloned.1.call-start = ((), (), s32[]{:S(2)}) async-start(), calls=%async_computation.21 | async-start | bytes 1880064 | tf_op jit(solution)/shard_map/all_gather | solution.py:82
  101.0 207.5 %all-gather.36.cloned.1.call-start = ((), (), s32[]{:S(2)}) async-start(), calls=%async_computation.20 | async-start | bytes 1880064 | tf_op jit(solution)/shard_map/all_gather | solution.py:83
  105.0 250.0 %all-gather.22.cloned.1.call-start = ((), (), s32[]{:S(2)}) async-start(), calls=%async_computation.13 | async-start | bytes 1880064 | tf_op jit(solution)/shard_map/all_gather | solution.py:82
  106.2 318.2 %all-gather.26.cloned.1.call-start = ((), (), s32[]{:S(2)}) async-start(), calls=%async_computation.15 | async-start | bytes 4755456 | tf_op jit(solution)/shard_map/all_gather | solution.py:321
  106.9 362.0 %all-gather.20.cloned.1.call-start = ((), (), s32[]{:S(2)}) async-start(), calls=%async_computation.12 | async-start | bytes 1880064 | tf_op jit(solution)/shard_map/all_gather | solution.py:83
  233.9 347.4 %all-gather.30.cloned.1.call-start = ((), (), s32[]{:S(2)}) async-start(), calls=%async_computation.17 | async-start | bytes 1880064 | tf_op jit(solution)/shard_map/all_gather | solution.py:82
  484.9 100.3 %all-gather.28.cloned.1.call-start = ((), (), s32[]{:S(2)}) async-start(), calls=%async_computation.16 | async-start | bytes 1880064 | tf_op jit(solution)/shard_map/all_gather | solution.py:83
  488.0 175.0 %all-gather.42.cloned.1.call-start = ((), (), s32[]{:S(2)}) async-start(), calls=%async_computation.23 | async-start | bytes 1880064 | tf_op jit(solution)/shard_map/all_gather | solution.py:82
  489.9 177.3 %all-gather.40.cloned.1.call-start = ((), (), s32[]{:S(2)}) async-start(), calls=%async_computation.22 | async-start | bytes 1880064 | tf_op jit(solution)/shard_map/all_gather | solution.py:83
  491.9 230.8 %all-gather.32.cloned.1.call-start = ((), (), s32[]{:S(2)}) async-start(), calls=%async_computation.18 | async-start | bytes 5013504 | tf_op jit(solution)/shard_map/all_gather | solution.py:325
  492.6 285.7 %all-gather.34.cloned.1.call-start = ((), (), s32[]{:S(2)}) async-start(), calls=%async_computation.19 | async-start | bytes 5013504 | tf_op jit(solution)/shard_map/all_gather | solution.py:326
  658.5 25.3 %all-to-all-start = ((bf16[8,20,768]{2,1,0:T(8,128)(2,1)}), bf16[8,20,768]{2,1,0:T(8,128)(2,1)}, u32[]{:S(2)}, u32[]{:S(2)}) async-start(bf16[8,20,768]{2,1,0:T(8,128)(2,1)} %copy.243), calls=%async_computation | async-start | bytes 589824 | tf_op jit(solution)/shard_map/all_to_all | solution.py:203
  683.8 99.5 %all-to-all-start.4 = ((bf16[8,20,768]{2,1,0:T(8,128)(2,1)}), bf16[8,20,768]{2,1,0:T(8,128)(2,1)S(1)}, u32[]{:S(2)}, u32[]{:S(2)}) async-start(bf16[8,20,768]{2,1,0:T(8,128)(2,1)} %copy.258), calls=%async_computation.4 | async-start | bytes 589824 | tf_op jit(solution)/shard_map/all_to_all | solution.py:253
  895.0 1455.7 %all-reduce.26.cloned.1.call-start = ((), (), s32[]{:S(2)}) async-start(), calls=%async_computation.28 | async-start | bytes 37748736
  1696.4 657.2 %reduce-scatter.15.cloned.1.call-start = ((), (), s32[]{:S(2)}) async-start(), calls=%async_computation.24 | async-start | bytes 9510912 | tf_op jit(solution)/shard_map/reduce_scatter | solution.py:429
  1704.4 649.3 %reduce-scatter.19.cloned.1.call-start = ((), (), s32[]{:S(2)}) async-start(), calls=%async_computation.26 | async-start | bytes 10027008 | tf_op jit(solution)/shard_map/reduce_scatter | solution.py:434
  1713.3 645.6 %reduce-scatter.17.cloned.1.call-start = ((), (), s32[]{:S(2)}) async-start(), calls=%async_computation.25 | async-start | bytes 10027008 | tf_op jit(solution)/shard_map/reduce_scatter | solution.py:433
  2126.1 24.4 %collective-permute-start = (f32[8,3072]{1,0:T(8,128)S(1)}, f32[8,3072]{1,0:T(8,128)S(1)}, u32[]{:S(2)}, u32[]{:S(2)}) collective-permute-start(f32[8,3072]{1,0:T(8,128)S(1)} %fusion), channel_id=1, source_target_pairs={{0,1},{1,2},{2,3},{3,4},{4,5},{5,6},{6,7},{7,8},{8,9},{9,10},{10,1... | collective-permute-start | bytes 294920
  2127.8 24.2 %collective-permute-start.1 = (f32[8,3072]{1,0:T(8,128)S(1)}, f32[8,3072]{1,0:T(8,128)}, u32[]{:S(2)}, u32[]{:S(2)}) collective-permute-start(f32[8,3072]{1,0:T(8,128)S(1)} %fusion), channel_id=1, source_target_pairs={{0,2},{1,3},{2,4},{3,5},{4,6},{5,7},{6,8},{7,9},{8,10},{9,11},{10,... | collective-permute-start | bytes 294920
  2129.8 23.6 collective-permute-start.10
  2131.7 23.0 collective-permute-start.11
  2152.1 89.7 %collective-permute-start.14 = (f32[8,3072]{1,0:T(8,128)S(1)}, f32[8,3072]{1,0:T(8,128)S(1)}, u32[]{:S(2)}, u32[]{:S(2)}) collective-permute-start(f32[8,3072]{1,0:T(8,128)S(1)} %fusion), channel_id=1, source_target_pairs={{0,15},{1,16},{2,17},{3,18},{4,19},{5,20},{6,21},{7,22},{8,23},{9,... | collective-permute-start | bytes 294920
  2153.4 91.3 %collective-permute-start.15 = (f32[8,3072]{1,0:T(8,128)S(1)}, f32[8,3072]{1,0:T(8,128)S(1)}, u32[]{:S(2)}, u32[]{:S(2)}) collective-permute-start(f32[8,3072]{1,0:T(8,128)S(1)} %fusion), channel_id=1, source_target_pairs={{0,16},{1,17},{2,18},{3,19},{4,20},{5,21},{6,22},{7,23},{8,24},{9,... | collective-permute-start | bytes 294920
  2154.7 94.7 %collective-permute-start.16 = (f32[8,3072]{1,0:T(8,128)S(1)}, f32[8,3072]{1,0:T(8,128)S(1)}, u32[]{:S(2)}, u32[]{:S(2)}) collective-permute-start(f32[8,3072]{1,0:T(8,128)S(1)} %fusion), channel_id=1, source_target_pairs={{0,17},{1,18},{2,19},{3,20},{4,21},{5,22},{6,23},{7,24},{8,25},{9,... | collective-permute-start | bytes 294920
  2156.0 95.5 %collective-permute-start.17 = (f32[8,3072]{1,0:T(8,128)S(1)}, f32[8,3072]{1,0:T(8,128)S(1)}, u32[]{:S(2)}, u32[]{:S(2)}) collective-permute-start(f32[8,3072]{1,0:T(8,128)S(1)} %fusion), channel_id=1, source_target_pairs={{0,18},{1,19},{2,20},{3,21},{4,22},{5,23},{6,24},{7,25},{8,26},{9,... | collective-permute-start | bytes 294920
  2167.8 89.1 %collective-permute-start.18 = (f32[8,3072]{1,0:T(8,128)S(1)}, f32[8,3072]{1,0:T(8,128)S(1)}, u32[]{:S(2)}, u32[]{:S(2)}) collective-permute-start(f32[8,3072]{1,0:T(8,128)S(1)} %fusion), channel_id=1, source_target_pairs={{0,19},{1,20},{2,21},{3,22},{4,23},{5,24},{6,25},{7,26},{8,27},{9,... | collective-permute-start | bytes 294920
  2244.7 23.3 collective-permute-start.2
  2251.6 21.9 collective-permute-start.21
  2295.5 21.7 collective-permute-start.5
  (285 other events, 7732.0 us)
Sparse Core Ops, SparseCore 0:
  11.6 71.4 all-gather.17
  86.1 62.7 all-gather.23
  151.9 65.6 all-gather.43
  220.1 42.0 all-gather.37
  264.7 43.8 all-gather.35
  311.1 43.8 all-gather.21
  357.8 66.4 all-gather.25
  427.0 41.8 all-gather.19
  485.0 43.7 all-gather.29
  531.4 43.9 all-gather.27
  577.5 43.7 all-gather.41
  623.3 43.8 all-gather.39
  669.3 53.2 all-gather.31
  724.7 53.5 all-gather.33
  1696.5 234.2 all-reduce.25
  1937.0 219.2 reduce-scatter.14
  2160.6 86.5 reduce-scatter.18
  2251.2 107.6 reduce-scatter.16
where the time goes:
time: 2380 us; the launch traced here: 2370 us
  blocking collectives  1260 us (53%)
  waiting for transfers between devices  341 us (14%)
  local copies, waits for them, and re-layouts  286 us (12%)
  matrix products  251 us (11%)
  starting transfers between devices  142 us (6%)
  other arithmetic  63.2 us (3%)
    unnamed x5, blocking collectives  1140 us
    unnamed x33, starting transfers between devices  105 us
    unnamed x541, local copies, waits for them, and re-layouts  86.5 us
    all_gather x4, waiting for transfers between devices, attend_forward(): lax.all_gather(key_local, 'dp', axis=0, tiled=True)  70.5 us
    all_gather x4, waiting for transfers between devices, attend_forward(): lax.all_gather(value_local, 'dp', axis=0, tiled=True)  68.3 us
    dot_general x24, matrix products, outer_sum(): jnp.einsum('ta,tb->ab', operand, matrix, preferred_element_type=jnp.float32)  63.6 us
    all_gather x1, blocking collectives, on_device(): lax.all_gather(router, ('expert', 'dp'), axis=0, tiled=True)  60.1 us
    all_gather x1, blocking collectives, on_device(): lax.all_gather(norm_gains, ('expert', 'dp'), axis=1, tiled=True)  58.7 us
  transfers between devices with their start and end apart: 58, of which 13 were waited for; matrix products, arithmetic and copies ran while one was open for 32% of the time, Pallas kernels for 0%

commit v1 on v0

v1 whole, which is shorter than its diff:
```python
import jax
import jax.numpy as jnp
from jax import lax
from jax.experimental import pallas as pl
from jax.experimental.pallas import tpu as pltpu
from jax.sharding import Mesh
from jax.sharding import PartitionSpec as P

WIDTH = 768
HEADS = 12
HEAD_DIM = 64
BUCKETS = 16
EXPERTS = 8
MICRO = 2
TOK = 72
ROWS = MICRO * TOK
GROUP = 1152
CAP = 20
FF = 3072
BLOCK = 128
SLOTS = 16
EPSILON = 1e-06
NEGATIVE = -1e30
SCALE = HEAD_DIM ** (-0.5)
LINE = ("y", "x")
ROW = ("z", "c")
ALL = ("z", "c", "y", "x")

bf16 = jnp.bfloat16
f32 = jnp.float32


def dot(a, b):
    return lax.dot_general(a, b, (((1,), (0,)), ((), ())), preferred_element_type=f32)


def dot_back(a, b):
    return lax.dot_general(a, b, (((1,), (1,)), ((), ())), preferred_element_type=f32)


def dot_outer(a, b):
    return lax.dot_general(a, b, (((0,), (0,)), ((), ())), preferred_element_type=f32)


def normalize(x, scales):
    inv = lax.rsqrt(jnp.mean(x * x, axis=-1, keepdims=True) + EPSILON)
    return (x * inv * scales).astype(bf16), inv


def normalize_back(grad, x, inv, scales):
    scaled = grad * scales
    mean = jnp.mean(scaled * x, axis=-1, keepdims=True)
    grad_x = inv * scaled - x * (inv * inv * inv) * mean
    grad_scales = jnp.sum(grad * x * inv, axis=0)
    return grad_x, grad_scales


def gelu(u):
    return jax.nn.gelu(u, approximate=True)


def forward_kernel(qk0_ref, qk1_ref, v_ref, bias_ref, start_ref, o_ref, lse_ref):
    for m, qk_ref in enumerate((qk0_ref, qk1_ref)):
        lanes = slice(m * HEAD_DIM, (m + 1) * HEAD_DIM)
        keys = qk_ref[:, HEAD_DIM:]
        values = v_ref[:, lanes]
        for i in range(GROUP // BLOCK):
            rows = slice(i * BLOCK, (i + 1) * BLOCK)
            width = (i + 1) * BLOCK
            scores = dot_back(qk_ref[rows, :HEAD_DIM], keys[:width])
            scores = scores + bias_ref[:, GROUP - width :]
            column = lax.broadcasted_iota(jnp.int32, (BLOCK, width), 1)
            scores = jnp.where(column >= start_ref[rows, m : m + 1], scores, NEGATIVE)
            peak = jnp.max(scores, axis=-1, keepdims=True)
            weights = jnp.exp(scores - peak)
            total = jnp.sum(weights, axis=-1, keepdims=True)
            probs = (weights * (1.0 / total)).astype(bf16)
            o_ref[rows, lanes] = dot(probs, values[:width]).astype(bf16)
            lse_ref[rows, m : m + 1] = peak + jnp.log(total)


def backward_kernel(
    qk0_ref, qk1_ref, v_ref, do_ref, bias_ref, start_ref, lse_ref,
    dqk0_ref, dqk1_ref, dv_ref, table_ref, dk_acc, dv_acc,
):
    table_ref[...] = jnp.zeros_like(table_ref)
    for m, (qk_ref, dqk_ref) in enumerate(((qk0_ref, dqk0_ref), (qk1_ref, dqk1_ref))):
        lanes = slice(m * HEAD_DIM, (m + 1) * HEAD_DIM)
        keys = qk_ref[:, HEAD_DIM:]
        values = v_ref[:, lanes]
        dk_acc[...] = jnp.zeros_like(dk_acc)
        dv_acc[...] = jnp.zeros_like(dv_acc)
        for i in range(GROUP // BLOCK):
            rows = slice(i * BLOCK, (i + 1) * BLOCK)
            width = (i + 1) * BLOCK
            query = qk_ref[rows, :HEAD_DIM]
            grad_o = do_ref[rows, lanes]
            scores = dot_back(query, keys[:width]) + bias_ref[:, GROUP - width :]
            column = lax.broadcasted_iota(jnp.int32, (BLOCK, width), 1)
            scores = jnp.where(column >= start_ref[rows, m : m + 1], scores, NEGATIVE)
            probs = jnp.exp(scores - lse_ref[rows, m : m + 1])
            grad_probs = dot_back(grad_o, values[:width])
            weighted = probs * grad_probs
            inner = jnp.sum(weighted, axis=-1, keepdims=True)
            grad_scores = (weighted - probs * inner).astype(bf16)
            table_ref[:, GROUP - width :] += grad_scores.astype(f32)
            dqk_ref[rows, :HEAD_DIM] = (dot(grad_scores, keys[:width]) * SCALE).astype(bf16)
            dk_acc[:width] += dot_outer(grad_scores, query)
            dv_acc[:width] += dot_outer(probs.astype(bf16), grad_o)
        dqk_ref[:, HEAD_DIM:] = dk_acc[...].astype(bf16)
        dv_ref[:, lanes] = dv_acc[...].astype(bf16)


LIMIT = pltpu.CompilerParams(vmem_limit_bytes=48 * 1024 * 1024)


def head_forward(qk0, qk1, v, bias, start):
    return pl.pallas_call(
        forward_kernel,
        out_shape=(
            jax.ShapeDtypeStruct((GROUP, 2 * HEAD_DIM), bf16),
            jax.ShapeDtypeStruct((GROUP, MICRO), f32),
        ),
        compiler_params=LIMIT,
        cost_estimate=pl.CostEstimate(
            flops=4 * MICRO * GROUP * GROUP * HEAD_DIM // 2,
            bytes_accessed=6 * GROUP * 256,
            transcendentals=MICRO * GROUP * GROUP // 2,
        ),
    )(qk0, qk1, v, bias, start)


def head_backward(qk0, qk1, v, grad_o, bias, start, lse):
    shape = jax.ShapeDtypeStruct((GROUP, 2 * HEAD_DIM), bf16)
    return pl.pallas_call(
        backward_kernel,
        out_shape=(shape, shape, shape, jax.ShapeDtypeStruct((BLOCK, GROUP), f32)),
        scratch_shapes=[pltpu.VMEM((GROUP, HEAD_DIM), f32), pltpu.VMEM((GROUP, HEAD_DIM), f32)],
        compiler_params=LIMIT,
        cost_estimate=pl.CostEstimate(
            flops=10 * MICRO * GROUP * GROUP * HEAD_DIM // 2,
            bytes_accessed=12 * GROUP * 256,
            transcendentals=MICRO * GROUP * GROUP // 2,
        ),
    )(qk0, qk1, v, grad_o, bias, start, lse)


def tile_distance():
    row = lax.broadcasted_iota(jnp.int32, (BLOCK, GROUP), 0)
    column = lax.broadcasted_iota(jnp.int32, (BLOCK, GROUP), 1)
    return row - column + (GROUP - BLOCK)


def bucket_starts():
    return [0, 1, 2, 3, 4, 5, 6, 7] + [2**t for t in range(3, 11)]


def bias_tile(entries):
    distance = tile_distance()
    result = jnp.full((BLOCK, GROUP), NEGATIVE, f32)
    for b, first in enumerate(bucket_starts()):
        result = jnp.where(distance >= first, entries[b], result)
    return result


def table_sums(tile):
    distance = tile_distance()
    above = [jnp.sum(jnp.where(distance >= first, tile, 0.0)) for first in bucket_starts()]
    above.append(jnp.zeros((), f32))
    return jnp.stack([above[b] - above[b + 1] for b in range(BUCKETS)])


def exchange(blocks, axes):
    return lax.all_to_all(blocks, axes, split_axis=0, concat_axis=0, tiled=True)


def pad_heads(blocks):
    return jnp.pad(blocks, ((0, SLOTS - HEADS), (0, 0), (0, 0)))


def by_head_single(values):
    parts = values.reshape(MICRO, TOK, HEADS, HEAD_DIM).transpose(2, 1, 0, 3)
    return parts.reshape(HEADS, TOK, MICRO * HEAD_DIM)


def from_head_single(blocks):
    parts = blocks.reshape(HEADS, TOK, MICRO, HEAD_DIM).transpose(2, 1, 0, 3)
    return parts.reshape(ROWS, WIDTH)


def send_heads(q, k, v):
    pair = jnp.stack([q.reshape(ROWS, HEADS, HEAD_DIM), k.reshape(ROWS, HEADS, HEAD_DIM)], axis=2)
    pair = pair.reshape(ROWS, HEADS, 2 * HEAD_DIM).transpose(1, 0, 2)
    blocks = exchange(pad_heads(jnp.concatenate([pair, by_head_single(v)], axis=1)), LINE)
    return tuple(
        blocks[:, j * TOK : (j + 1) * TOK].reshape(GROUP, 2 * HEAD_DIM) for j in range(3)
    )


def return_heads(dqk0, dqk1, dv):
    blocks = jnp.concatenate([a.reshape(SLOTS, TOK, 2 * HEAD_DIM) for a in (dqk0, dqk1, dv)], axis=1)
    blocks = exchange(blocks, LINE)[:HEADS]
    pair = blocks[:, :ROWS].reshape(HEADS, ROWS, 2, HEAD_DIM).transpose(2, 1, 0, 3)
    pair = pair.reshape(2, ROWS, WIDTH)
    return pair[0], pair[1], from_head_single(blocks[:, ROWS:])


def attend_forward(x, scales, weights, bias, start):
    normed, inv = normalize(x, scales)
    q = (dot(normed, weights[0]) * SCALE).astype(bf16)
    k = dot(normed, weights[1]).astype(bf16)
    v = dot(normed, weights[2]).astype(bf16)
    qk0, qk1, vv = send_heads(q, k, v)
    o, lse = head_forward(qk0, qk1, vv, bias, start)
    attended = from_head_single(exchange(o.reshape(SLOTS, TOK, 2 * HEAD_DIM), LINE)[:HEADS])
    return x + dot(attended, weights[3]), (normed, inv, qk0, qk1, vv, lse, attended)


def attend_backward(grad, x, scales, weights, bias, start, saved):
    normed, inv, qk0, qk1, vv, lse, attended = saved
    branch = grad.astype(bf16)
    grad_attended = dot_back(branch, weights[3]).astype(bf16)
    grad_o = exchange(pad_heads(by_head_single(grad_attended)), LINE).reshape(GROUP, 2 * HEAD_DIM)
    dqk0, dqk1, dv, tile = head_backward(qk0, qk1, vv, grad_o, bias, start, lse)
    dq, dk, dv = return_heads(dqk0, dqk1, dv)
    grad_normed = dot_back(dq, weights[0]) + dot_back(dk, weights[1]) + dot_back(dv, weights[2])
    grad_x, grad_scales = normalize_back(grad_normed, x, inv, scales)
    return grad + grad_x, grad_scales, branch, (dq, dk, dv), tile


def other_core(value):
    return lax.ppermute(value, "c", [(0, 1), (1, 0)])


def select_columns(core):
    out = lax.broadcasted_iota(jnp.int32, (WIDTH, WIDTH // 2), 1)
    source = lax.broadcasted_iota(jnp.int32, (WIDTH, WIDTH // 2), 0)
    line, rest = out // 24, out % 24
    z, i = rest // 6, rest % 6
    return (source == ((z * 2 + core) * 16 + line) * 6 + i).astype(bf16)


def pick(a, selector):
    return dot(a, selector).astype(bf16)


def on_device(
    hidden_in, lengths, routes, norm_gains, qkv_weights, out_weights, rel_table,
    ffn_in, ffn_out, router, expert_in, expert_out, cotangent,
):
    core = lax.axis_index("c")
    line_rank = lax.axis_index("y") * 4 + lax.axis_index("x")

    first_pack = jnp.concatenate([qkv_weights[0], out_weights[:1]], axis=0)
    second_pack = jnp.concatenate(
        [
            ffn_in.reshape(6, 4, WIDTH).transpose(1, 0, 2),
            ffn_out.reshape(4, 6, WIDTH),
            qkv_weights[1],
            out_weights[1:],
        ],
        axis=0,
    )
    first = lax.all_gather(first_pack, ALL, axis=1, tiled=True)
    second = lax.all_gather(second_pack, ALL, axis=1, tiled=True)
    w_expert_in = lax.all_gather(expert_in[0], LINE, axis=0, tiled=True)
    w_expert_out = lax.all_gather(expert_out[0], LINE, axis=0, tiled=True)
    w_in = [second[j] for j in range(4)]
    w_out = second[4:8].reshape(4, 128, 6, WIDTH).transpose(1, 0, 2, 3).reshape(FF, WIDTH)
    weights_one = second[8:]

    small = jnp.concatenate([norm_gains.reshape(24), router.reshape(48), rel_table])
    small = jnp.pad(small, (0, 128 - 75))[None, None, :]
    small = jnp.broadcast_to(small, (SLOTS, 8, 128))
    small = exchange(small, LINE).reshape(1, 128, 128)
    small = exchange(jnp.broadcast_to(small, (EXPERTS, 128, 128)), ROW)
    small = small.reshape(128, 8, 128)[:, 0]
    gains = small[:, :24].reshape(128, 4, 6).transpose(1, 0, 2).reshape(4, WIDTH).astype(f32)
    w_router = small[:, 24:72].reshape(WIDTH, EXPERTS)
    table = small[:, 72:75].reshape(2, HEADS, BUCKETS).astype(f32)
    head = jnp.minimum(line_rank, HEADS - 1)
    entries = lax.dynamic_index_in_dim(table, head, axis=1, keepdims=False)
    bias = [bias_tile(entries[layer]) for layer in range(2)]

    ends = jnp.cumsum(lengths[:, 0], axis=1)
    position = jnp.arange(GROUP, dtype=jnp.int32)[:, None, None]
    start = jnp.max(jnp.where(position >= ends[None], ends[None], 0), axis=2)

    x0 = hidden_in.reshape(ROWS, WIDTH).astype(f32)
    x1, saved_one = attend_forward(x0, gains[0], first, bias[0], start)
    c, inv_c = normalize(x1, gains[1])
    u = jnp.concatenate([dot(c, w) for w in w_in], axis=1)
    h = gelu(u).astype(bf16)
    x2 = x1 + dot(h, w_out)
    x3, saved_three = attend_forward(x2, gains[2], weights_one, bias[1], start)

    e, inv_e = normalize(x3, gains[3])
    logits = dot(e, w_router)
    choice = routes.reshape(ROWS, 2)
    marks = (choice[:, :, None] == jnp.arange(EXPERTS, dtype=jnp.int32)).astype(f32)
    chosen = jnp.sum(marks * logits[:, None, :], axis=-1)
    gates = jax.nn.softmax(chosen, axis=-1)
    pair_marks = marks.reshape(MICRO, TOK * 2, EXPERTS)
    earlier = jnp.cumsum(pair_marks, axis=1) - pair_marks
    slots = jnp.sum(earlier * pair_marks, axis=-1).astype(jnp.int32).reshape(ROWS, 2)
    micro = (jnp.arange(ROWS, dtype=jnp.int32) // TOK)[:, None]
    target = choice * 80 + micro * CAP + slots
    target_k = target.T
    row_id = jnp.arange(EXPERTS * 80, dtype=jnp.int32)
    place = [row_id[:, None] == target_k[k][None, :] for k in range(2)]
    place_back = [row_id[:, None] == target_k[k][None, :] + 40 for k in range(2)]
    scatter = jnp.concatenate([place[0] | place[1], place_back[0], place_back[1]], axis=1).astype(bf16)
    collect = jnp.concatenate([place_back[0] | place_back[1], place[0], place[1]], axis=1).astype(bf16)
    grad_four = cotangent.reshape(ROWS, WIDTH).astype(f32)
    picked_grads = [(gates[:, k : k + 1] * grad_four).astype(bf16) for k in range(2)]
    sent = dot(scatter, jnp.concatenate([e] + picked_grads, axis=0)).astype(bf16)
    arrived = exchange(sent.reshape(EXPERTS, 80, WIDTH), ROW)
    expert_rows = arrived[:, :40].reshape(320, WIDTH)
    grad_rows = arrived[:, 40:].reshape(320, WIDTH)
    ue = dot(expert_rows, w_expert_in)
    he, gelu_back = jax.vjp(gelu, ue)
    he = he.astype(bf16)
    ye = dot(he, w_expert_out).astype(bf16)
    due = gelu_back(dot_back(grad_rows, w_expert_out))[0].astype(bf16)
    grad_sent = dot_back(due, w_expert_in).astype(bf16)
    produced = jnp.concatenate([ye.reshape(EXPERTS, 40, WIDTH), grad_sent.reshape(EXPERTS, 40, WIDTH)], axis=1)
    returned = exchange(produced, ROW).reshape(EXPERTS * 80, WIDTH)
    collected = dot_outer(collect, returned)
    picked = [collected[ROWS : 2 * ROWS], collected[2 * ROWS :]]
    hidden_out = x3 + gates[:, :1] * picked[0] + gates[:, 1:] * picked[1]

    expert_parts = [
        dot_outer(expert_rows, due[:, j * WIDTH : (j + 1) * WIDTH]).astype(bf16).reshape(SLOTS, 48, WIDTH)
        for j in range(4)
    ] + [dot_outer(he, grad_rows).astype(bf16).reshape(SLOTS, 192, WIDTH)]
    expert_sum = lax.psum_scatter(
        jnp.concatenate(expert_parts, axis=1), LINE, scatter_dimension=0, tiled=False
    ).astype(f32)

    dgates = jnp.stack([jnp.sum(grad_four * p, axis=-1) for p in picked], axis=1)
    dchosen = gates * (dgates - jnp.sum(gates * dgates, axis=-1, keepdims=True))
    dlogits = jnp.sum(marks * dchosen[:, :, None], axis=1)
    grad_router = dot_outer(e, dlogits.astype(bf16))
    grad_e = collected[:ROWS] + dot_back(dlogits.astype(bf16), w_router)
    grad_x, gain_four = normalize_back(grad_e, x3, inv_e, gains[3])
    grad_three = grad_four + grad_x

    selector = select_columns(core)
    selector_other = select_columns(1 - core)

    def share(a, b):
        mine, theirs = pick(a, selector), pick(a, selector_other)
        got = other_core(jnp.concatenate([theirs, b], axis=1))
        return (
            jnp.concatenate([mine, got[:, : WIDTH // 2]], axis=0),
            jnp.concatenate([b, got[:, WIDTH // 2 :]], axis=0),
        )

    def chunks(a, b):
        return [
            dot_outer(a, b[:, j * WIDTH : (j + 1) * WIDTH]).astype(bf16).reshape(SLOTS, 24, WIDTH)
            for j in range(b.shape[1] // WIDTH)
        ]

    grad_two, gain_three, branch_three, heads_three, tile_three = attend_backward(
        grad_three, x2, gains[2], weights_one, bias[1], start, saved_three
    )
    parts = chunks(*share(saved_three[0], jnp.concatenate(heads_three, axis=1)))
    parts += chunks(*share(saved_three[6], branch_three))

    branch_two = grad_two.astype(bf16)
    grad_h = dot_back(branch_two, w_out)
    gelu_back_two = jax.vjp(gelu, u)[1]
    du = gelu_back_two(grad_h)[0].astype(bf16)
    grad_c = sum(dot_back(du[:, j * WIDTH : (j + 1) * WIDTH], w_in[j]) for j in range(4))
    grad_x, gain_two = normalize_back(grad_c, x1, inv_c, gains[1])
    grad_one = grad_two + grad_x
    parts += chunks(*share(c, du))
    halves = h.reshape(ROWS, 4, 2, FF // 8)
    mine = lax.dynamic_index_in_dim(halves, core, axis=2, keepdims=False).reshape(ROWS, FF // 2)
    theirs = lax.dynamic_index_in_dim(halves, 1 - core, axis=2, keepdims=False).reshape(ROWS, FF // 2)
    got = other_core(jnp.concatenate([theirs, branch_two], axis=1))
    mine = jnp.concatenate([mine, got[:, : FF // 2]], axis=0)
    second_grad = dot_outer(mine, jnp.concatenate([branch_two, got[:, FF // 2 :]], axis=0))
    second_grad = second_grad.astype(bf16).reshape(4, SLOTS, 24, WIDTH)
    parts += [second_grad[z] for z in range(4)]
    early_sum = lax.psum_scatter(
        jnp.concatenate(parts, axis=1), LINE, scatter_dimension=0, tiled=False
    )

    grad_zero, gain_one, branch_one, heads_one, tile_one = attend_backward(
        grad_one, x0, gains[0], first, bias[0], start, saved_one
    )
    late = chunks(*share(saved_one[0], jnp.concatenate(heads_one, axis=1)))
    late += chunks(*share(saved_one[6], branch_one))

    own_head = (jnp.arange(HEADS, dtype=jnp.int32) == line_rank).astype(f32)
    table_grad = jnp.stack([table_sums(tile_one), table_sums(tile_three)])
    table_grad = (own_head[None, :, None] * table_grad[:, None, :]).reshape(128, 3)
    gain_grad = jnp.stack([gain_one, gain_two, gain_three, gain_four])
    gain_grad = gain_grad.reshape(4, 128, 6).transpose(1, 0, 2).reshape(128, 24)
    tiny = jnp.concatenate([gain_grad, grad_router.reshape(128, 48), table_grad], axis=1)
    tiny = jnp.pad(tiny, ((0, 0), (0, 128 - 75))).reshape(4, 2, SLOTS, 128)
    tiny_mine = lax.dynamic_index_in_dim(tiny, core, axis=1, keepdims=False)
    tiny_theirs = lax.dynamic_index_in_dim(tiny, 1 - core, axis=1, keepdims=False)
    tiny_sum = tiny_mine + other_core(tiny_theirs)
    tiny_sum = tiny_sum.transpose(1, 0, 2).reshape(SLOTS, 1, 512)
    tiny_sum = jnp.pad(tiny_sum, ((0, 0), (0, 7), (0, 256))).astype(bf16)
    late_blocks = exchange(jnp.concatenate(late + [tiny_sum], axis=1), LINE)
    late_sum = jnp.sum(late_blocks.astype(f32), axis=0)

    tiny_rows = late_sum[96, :512].reshape(4, 1, 128)
    tiny_rows = jnp.pad(tiny_rows, ((0, 0), (0, 7), (0, WIDTH - 128)))
    late_rows = late_sum[:96].reshape(4, 4, 6, WIDTH)
    early = early_sum.astype(f32)
    early_rows = early[:192].reshape(8, 4, 6, WIDTH)
    ffn_out_rows = early[192:].reshape(4, 24, WIDTH)
    six = jnp.concatenate([late_rows, early_rows], axis=0).transpose(1, 0, 2, 3).reshape(4, 72, WIDTH)
    last = exchange(jnp.concatenate([six, ffn_out_rows, tiny_rows], axis=1).astype(bf16), ("z",))
    last = jnp.sum(last.astype(f32), axis=0)
    six = last[:72].reshape(12, 6, WIDTH)
    tiny = last[96, :75]
    out_shape = hidden_in.shape
    return (
        hidden_out.reshape(out_shape),
        grad_zero.reshape(out_shape),
        tiny[:24].reshape(4, 6),
        jnp.stack([six[0:3], six[4:7]]),
        jnp.stack([six[3], six[7]]),
        tiny[72:75],
        six[8:12].transpose(1, 0, 2).reshape(6, FF),
        last[72:96],
        tiny[24:72].reshape(6, EXPERTS),
        expert_sum[:192].reshape(4, 48, WIDTH).transpose(1, 0, 2).reshape(1, 48, FF),
        expert_sum[192:].reshape(1, 192, WIDTH),
    )


def solution(mesh):
    fine = Mesh(mesh.devices.reshape(4, 2, 4, 4), ALL)
    return jax.shard_map(
        on_device,
        mesh=fine,
        in_specs=(
            P(None, ALL, None),
            P(None, ROW, None),
            P(None, ALL, None),
            P(None, ALL),
            P(None, None, ALL, None),
            P(None, ALL, None),
            P(ALL),
            P(ALL, None),
            P(ALL, None),
            P(ALL, None),
            P(ROW, LINE, None),
            P(ROW, LINE, None),
            P(None, ALL, None),
        ),
        out_specs=(
            P(None, ALL, None),
            P(None, ALL, None),
            P(None, ALL),
            P(None, None, ALL, None),
            P(None, ALL, None),
            P(ALL),
            P(ALL, None),
            P(ALL, None),
            P(ALL, None),
            P(ROW, LINE, None),
            P(ROW, LINE, None),
        ),
        check_vma=False,
    )
```

time: 2380 us -> 754 us (0.32)
  blocking collectives: 1260 us -> 0 us
  matrix products: 251 us -> 107 us
  waiting for transfers between devices: 341 us -> 212 us
  starting transfers between devices: 142 us -> 70.7 us
  local copies, waits for them, and re-layouts: 286 us -> 217 us
  between operations: 19.2 us -> 54.7 us
  Pallas kernels: 0 us -> 34.8 us
    unnamed x5 -> x0, blocking collectives: 1140 us -> none
    all_gather x14 -> x4, waiting for transfers between devices: 325 us -> 48.7 us  [the longest x1 38.4 us: on_device(): first = lax.all_gather(first_pack, ALL, axis=1, tiled=True)]
    dot_general x112 -> x63, matrix products: 251 us -> 107 us  [the longest x27 50.7 us: dot(): lax.dot_general(a, b, (((1,), (0,)), ((), ())), preferred_element_type=f32)]
    all_to_all x8 -> x14, waiting for transfers between devices: 7.5 us -> 131 us  [exchange(): return lax.all_to_all(blocks, axes, split_axis=0, concat_axis=0, tiled=True)]
    all_gather x2 -> x0, blocking collectives: 119 us -> none  [the longest x1 60.1 us: on_device(): lax.all_gather(router, ('expert', 'dp'), axis=0, tiled=True)]
    unnamed x33 -> x2, starting transfers between devices: 105 us -> 0.29 us
    scatter x8 -> x0, local copies, waits for them, and re-layouts: 63.5 us -> none  [the longest x4 31.8 us: expert_backward(): outbound = jnp.zeros((expert_count, capacity, width_count), jnp.bfloat16)...]
    slice x7 -> x55, local copies, waits for them, and re-layouts: 25.4 us -> 85 us  [the longest x2 50.8 us: attend_forward(): weights[3]]
  transfers between devices with their start and end apart: 58 -> 27, of which waited for: 13 -> 18; matrix products, arithmetic and copies ran while one was open for 32% -> 37% of each run, Pallas kernels for 0% -> 3%
where the time goes in v1:
time: 754 us; the launch traced here: 745 us
  local copies, waits for them, and re-layouts  217 us (29%)
  waiting for transfers between devices  212 us (28%)
  matrix products  107 us (14%)
  starting transfers between devices  70.7 us (9%)
  between operations  54.7 us (7%)
  other arithmetic  48.4 us (6%)
  Pallas kernels  34.8 us (5%)
    all_to_all x14, waiting for transfers between devices, exchange(): return lax.all_to_all(blocks, axes, split_axis=0, concat_axis=0, tiled=True)  131 us
    all_to_all x14, starting transfers between devices, exchange(): return lax.all_to_all(blocks, axes, split_axis=0, concat_axis=0, tiled=True)  68.3 us
    slice x2, local copies, waits for them, and re-layouts, attend_forward(): weights[3]  50.8 us
    dot_general x27, matrix products, dot(): lax.dot_general(a, b, (((1,), (0,)), ((), ())), preferred_element_type=f32)  50.7 us
    unnamed x299, local copies, waits for them, and re-layouts  43.6 us
    all_gather x1, waiting for transfers between devices, on_device(): first = lax.all_gather(first_pack, ALL, axis=1, tiled=True)  38.4 us
    dot_general x16, matrix products, dot_back(): lax.dot_general(a, b, (((1,), (1,)), ((), ())), preferred_element_type=f32)  35.5 us
    unnamed x8, waiting for transfers between devices  29.4 us
  transfers between devices with their start and end apart: 27, of which 18 were waited for; matrix products, arithmetic and copies ran while one was open for 37% of the time, Pallas kernels for 3%

profile of v1, /device:TPU:0, one launch (start us, length us, event | category | flops | bytes accessed | tf_op | source)
XLA Modules:
  0.0 744.8 jit_solution(15065433061470972951)
XLA Ops:
  13.9 7.1 all-to-all-start
  29.4 5.3 all-to-all-start.1
  35.0 7.2 all-to-all-done.1
  42.8 38.4 %all-gather.7.cloned.1.call-done = bf16[4,768,768]{2,0,1:T(4,128)(2,1)} async-done(((bf16[4,6,768]{2,0,1:T(4,128)(2,1)}), bf16[4,768,768]{2,0,1:T(4,128)(2,1)}) %all-gather.7.cloned.1.call-update) | async-done | bytes 4718608 | tf_op jit(solution)/shard_map/all_gather | solution.py:264
  81.2 16.0 %fusion.202 = (bf16[1,768,768]{2,0,1:T(2,128)(2,1)}, bf16[1,768,768]{2,0,1:T(2,128)(2,1)S(1)}, bf16[1,768,768]{2,0,1:T(2,128)(2,1)}, bf16[1,768,768]{2,0,1:T(2,128)(2,1)}) fusion(bf16[4,768,768]{2,0,1:T(4,128)(2,1)} %all-gather.7.cloned.1.call-done), kind=kLoop, calls=%fused_computation.459 | loop fusion | bytes 9437184 | tf_op jit(solution)/shard_map/slice | solution.py:216
  112.5 10.1 %select_select_fusion.1.bias_ref = f32[128,1152]{1,0:T(8,128)S(1)} fusion(f32[]{:T(128)} %bitcast.31, f32[]{:T(128)} %bitcast.30, f32[]{:T(128)} %bitcast.29, f32[]{:T(128)} %bitcast.28, f32[]{:T(128)} %bitcast.27, f32[]{:T(128)} %bitcast.26, f32[]{:T(128)} %bitcast.25, f32[]{:T(128)} %bitcast.24, f32[]{:T(128)} %bitcast.23, f32[]{:T(128)} %bitcast.22, ...), kind=kLoop, calls=%fused_computation.216 | loop fusion | flops 5013504 | bytes 589888 | tf_op jit(solution)/shard_map/jit(_where)/select_n | solution.py:162
  122.6 8.3 %all-to-all-done.2 = bf16[16,216,128]{2,1,0:T(8,128)(2,1)S(1)} async-done(((bf16[16,216,128]{2,1,0:T(8,128)(2,1)}), bf16[16,216,128]{2,1,0:T(8,128)(2,1)S(1)}, u32[]{:S(2)}, u32[]{:S(2)}) %all-to-all-start.2) | async-done | bytes 884768 | tf_op jit(solution)/shard_map/all_to_all | solution.py:174
  131.0 8.1 %shard_map.212 = (bf16[1152,128]{1,0:T(8,128)(2,1)}, f32[1152,2]{1,0:T(8,128)S(1)}) custom-call(bf16[1152,128]{1,0:T(8,128)(2,1)S(1)} %bitcast.369, bf16[1152,128]{1,0:T(8,128)(2,1)S(1)} %bitcast.367, bf16[1152,128]{1,0:T(8,128)(2,1)S(1)} %bitcast.365, f32[128,1152]{1,0:T(8,128)S(1)} %select_select_fusion.1.bias_ref, s32[1152,2]{1,0:T(8,128)S(1)} %copy.509.start_ref), custom_call_target="tpu_custom_call" | custom-call | flops 339738624 | bytes 1769472 | tf_op jit(solution)/shard_map/pallas_call | solution.py:118
  144.4 11.2 %all-to-all-done.3 = bf16[16,72,128]{2,1,0:T(8,128)(2,1)S(1)} async-done(((bf16[16,72,128]{2,1,0:T(8,128)(2,1)}), bf16[16,72,128]{2,1,0:T(8,128)(2,1)S(1)}, u32[]{:S(2)}, u32[]{:S(2)}) %all-to-all-start.3) | async-done | bytes 294944 | tf_op jit(solution)/shard_map/all_to_all | solution.py:174
  164.7 10.3 %all-gather.9.cloned.1.call-done = bf16[12,768,768]{2,0,1:T(8,128)(2,1)} async-done(((bf16[12,6,768]{2,0,1:T(8,128)(2,1)}), bf16[12,768,768]{2,0,1:T(8,128)(2,1)}) %all-gather.9.cloned.1.call-update) | async-done | bytes 14155792 | tf_op jit(solution)/shard_map/all_gather | solution.py:265
  175.0 34.9 %fusion.201 = (bf16[1,768,768]{2,0,1:T(2,128)(2,1)}, bf16[1,768,768]{2,0,1:T(2,128)(2,1)}, bf16[1,768,768]{2,0,1:T(2,128)(2,1)}, bf16[1,768,768]{2,0,1:T(2,128)(...) fusion(bf16[12,768,768]{2,0,1:T(8,128)(2,1)} %all-gather.9.clon, ...), kind=kLoop, calls=%fused_computation.458 | loop fusion | bytes 18874368 | tf_op jit(solution)/shard_map/slice | solution.py:216
  209.9 6.1 slice.698
  220.3 9.1 %reshape.677 = bf16[3072,768]{1,0:T(8,128)(2,1)} reshape(bf16[128,4,6,768]{3,2,1,0:T(8,128)(2,1)} %copy.520) | data formatting | bytes 9437184 | tf_op jit(solution)/shard_map/reshape | solution.py:269
  251.9 5.5 all-to-all-start.4
  260.1 10.2 %select_select_fusion.bias_ref = f32[128,1152]{1,0:T(8,128)S(1)} fusion(f32[]{:T(128)} %bitcast.70, f32[]{:T(128)} %bitcast.69, f32[]{:T(128)} %bitcast.68, f32[]{:T(128)} %bitcast.67, f32[]{:T(128)} %bitcast.66, f32[]{:T(128)} %bitcast.65, f32[]{:T(128)} %bitcast.64, f32[]{:T(128)} %bitcast.63, f32[]{:T(128)} %bitcast.62, f32[]{:T(128)} %bitcast.61, ...), kind=kLoop, calls=%fused_computation.215 | loop fusion | flops 5013504 | bytes 589888 | tf_op jit(solution)/shard_map/jit(_where)/select_n | solution.py:162
  270.3 8.0 %all-to-all-done.4 = bf16[16,216,128]{2,1,0:T(8,128)(2,1)} async-done(((bf16[16,216,128]{2,1,0:T(8,128)(2,1)}), bf16[16,216,128]{2,1,0:T(8,128)(2,1)}, u32[]{:S(2)}, u32[]{:S(2)}) %all-to-all-start.4) | async-done | bytes 884768 | tf_op jit(solution)/shard_map/all_to_all | solution.py:174
  279.6 8.2 %shard_map.213 = (bf16[1152,128]{1,0:T(8,128)(2,1)}, f32[1152,2]{1,0:T(8,128)S(1)}) custom-call(bf16[1152,128]{1,0:T(8,128)(2,1)S(1)} %bitcast.375, bf16[1152,128]{1,0:T(8,128)(2,1)S(1)} %bitcast.373, bf16[1152,128]{1,0:T(8,128)(2,1)S(1)} %bitcast.371, f32[128,1152]{1,0:T(8,128)S(1)} %select_select_fusion.bias_ref, s32[1152,2]{1,0:T(8,128)S(1)} %copy.509.start_ref), custom_call_target="tpu_custom_call" | custom-call | flops 339738624 | bytes 1769472 | tf_op jit(solution)/shard_map/pallas_call | solution.py:118
  295.0 6.8 all-to-all-done.5
  336.7 6.1 fusion.6
  342.8 6.1 fusion.54
  355.6 4.6 all-to-all-start.7
  367.2 8.2 %all-to-all-done.7 = bf16[8,80,768]{2,1,0:T(8,128)(2,1)} async-done(((bf16[8,80,768]{2,1,0:T(8,128)(2,1)}), bf16[8,80,768]{2,1,0:T(8,128)(2,1)}, u32[]{:S(2)}, u32[]{:S(2)}) %all-to-all-start.7) | async-done | bytes 983072 | tf_op jit(solution)/shard_map/all_to_all | solution.py:174
  395.6 7.1 all-to-all-done.8
  407.4 9.2 %shard_map.214 = (bf16[1152,128]{1,0:T(8,128)(2,1)S(1)}, bf16[1152,128]{1,0:T(8,128)(2,1)S(1)}, bf16[1152,128]{1,0:T(8,128)(2,1)S(1)}, f32[128,1152]{1,0:T(8,128)S(1)}) custom-call(bf16[1152,128]{1,0:T(8,128)(2,1)S(1)} %bitcast.376, bf16[1152,128]{1,0:T(8,128)(2,1)S(1)} %bitcast.374, bf16[1152,128]{1,0:T(8,128)(2,1)S(1)} %bitcast.372, ...), custom_call_target="tpu_custom_call" | custom-call | flops 849346560 | bytes 3538944 | tf_op jit(solution)/shard_map/pallas_call | solution.py:135
  426.0 9.9 %all-to-all-done.9 = bf16[16,216,128]{2,1,0:T(8,128)(2,1)S(1)} async-done(((bf16[16,216,128]{2,1,0:T(8,128)(2,1)}), bf16[16,216,128]{2,1,0:T(8,128)(2,1)S(1)}, u32[]{:S(2)}, u32[]{:S(2)}) %all-to-all-start.9) | async-done | bytes 884768 | tf_op jit(solution)/shard_map/all_to_all | solution.py:174
  468.1 4.5 fusion.27
  558.8 9.2 %shard_map.215 = (bf16[1152,128]{1,0:T(8,128)(2,1)S(1)}, bf16[1152,128]{1,0:T(8,128)(2,1)S(1)}, bf16[1152,128]{1,0:T(8,128)(2,1)S(1)}, f32[128,1152]{1,0:T(8,128)S(1)}) custom-call(bf16[1152,128]{1,0:T(8,128)(2,1)S(1)} %bitcast.370, bf16[1152,128]{1,0:T(8,128)(2,1)S(1)} %bitcast.368, bf16[1152,128]{1,0:T(8,128)(2,1)S(1)} %bitcast.366, ...), custom_call_target="tpu_custom_call" | custom-call | flops 849346560 | bytes 3538944 | tf_op jit(solution)/shard_map/pallas_call | solution.py:135
  569.1 7.4 all-to-all-start.11
  622.2 7.4 all-to-all-start.12
  630.2 51.8 %all-to-all-done.12 = bf16[16,104,768]{2,1,0:T(8,128)(2,1)} async-done(((bf16[16,104,768]{2,1,0:T(8,128)(2,1)}), bf16[16,104,768]{2,1,0:T(8,128)(2,1)}, u32[]{:S(2)}, u32[]{:S(2)}) %all-to-all-start.12) | async-done | bytes 2555936 | tf_op jit(solution)/shard_map/all_to_all | solution.py:174
  693.8 7.7 %all-to-all-done.13 = bf16[4,104,768]{2,1,0:T(8,128)(2,1)S(1)} async-done(((bf16[4,104,768]{2,1,0:T(8,128)(2,1)}), bf16[4,104,768]{2,1,0:T(8,128)(2,1)S(1)}, u32[]{:S(2)}, u32[]{:S(2)}) %all-to-all-start.13) | async-done | bytes 639008 | tf_op jit(solution)/shard_map/all_to_all | solution.py:174
  706.3 28.1 %reduce-scatter.4.cloned.1.call-done = bf16[1,384,768]{2,1,0:T(8,128)(2,1)} async-done(((bf16[16,384,768]{2,1,0:T(8,128)(2,1)}), bf16[1,384,768]{2,1,0:T(8,128)(2,1)}) %reduce-scatter.4.cloned.1.call-update) | async-done | bytes 589840
  (641 shorter events, 311.7 us)
Async XLA Ops:
  7.2 73.9 %all-gather.7.cloned.1.call-start = ((), (), s32[]{:S(2)}) async-start(), calls=%async_computation.15 | async-start | bytes 4755456 | tf_op jit(solution)/shard_map/all_gather | solution.py:264
  9.8 165.2 %all-gather.9.cloned.1.call-start = ((), (), s32[]{:S(2)}) async-start(), calls=%async_computation.16 | async-start | bytes 19021824 | tf_op jit(solution)/shard_map/all_gather | solution.py:265
  12.3 324.4 %all-gather.11.cloned.1.call-start = ((), (), s32[]{:S(2)}) async-start(), calls=%async_computation.17 | async-start | bytes 5013504 | tf_op jit(solution)/shard_map/all_gather | solution.py:266
  13.9 14.7 %all-to-all-start = ((bf16[16,8,128]{2,1,0:T(8,128)(2,1)}), bf16[16,8,128]{2,1,0:T(8,128)(2,1)S(1)}, u32[]{:S(2)}, u32[]{:S(2)}) async-start(bf16[16,8,128]{2,1,0:T(8,128)(2,1)} %broadcast_in_dim.179), calls=%async_computation | async-start | bytes 65536 | tf_op jit(solution)/shard_map/all_to_all | solution.py:174
  21.0 321.8 %all-gather.13.cloned.1.call-start = ((), (), s32[]{:S(2)}) async-start(), calls=%async_computation.18 | async-start | bytes 5013504 | tf_op jit(solution)/shard_map/all_gather | solution.py:267
  29.4 12.9 %all-to-all-start.1 = ((bf16[8,128,128]{2,1,0:T(8,128)(2,1)}), bf16[8,128,128]{2,1,0:T(8,128)(2,1)S(1)}, u32[]{:S(2)}, u32[]{:S(2)}) async-start(bf16[8,128,128]{2,1,0:T(8,128)(2,1)} %broadcast_in_dim.181), calls=%async_computation.1 | async-start | bytes 524288 | tf_op jit(solution)/shard_map/all_to_all | solution.py:174
  34.7 62.4 %copy-start.81 = (f32[2,8,3]{1,2,0:T(4,128)}, f32[2,8,3]{1,2,0:T(4,128)S(1)}, u32[]{:S(2)}) copy-start(f32[2,8,3]{1,2,0:T(4,128)S(1)} %reduce-window.9) | copy-start | bytes 580
  35.0 62.1 %copy-start.79 = (f32[2,72]{1,0:T(2,128)}, f32[2,72]{1,0:T(2,128)S(1)}, u32[]{:S(2)}) copy-start(f32[2,72]{1,0:T(2,128)S(1)} %add_rsqrt_fusion.3) | copy-start | bytes 1732
  106.8 24.1 %all-to-all-start.2 = ((bf16[16,216,128]{2,1,0:T(8,128)(2,1)}), bf16[16,216,128]{2,1,0:T(8,128)(2,1)S(1)}, u32[]{:S(2)}, u32[]{:S(2)}) async-start(bf16[16,216,128]{2,1,0:T(8,128)(2,1)} %fusion.70), calls=%async_computation.2 | async-start | bytes 1769472 | tf_op jit(solution)/shard_map/all_to_all | solution.py:174
  139.1 16.5 %all-to-all-start.3 = ((bf16[16,72,128]{2,1,0:T(8,128)(2,1)}), bf16[16,72,128]{2,1,0:T(8,128)(2,1)S(1)}, u32[]{:S(2)}, u32[]{:S(2)}) async-start(bf16[16,72,128]{2,1,0:T(8,128)(2,1)} %bitcast.33), calls=%async_computation.3 | async-start | bytes 589824 | tf_op jit(solution)/shard_map/all_to_all | solution.py:174
  143.9 166.8 %copy-start.71 = (s32[144,2]{0,1:T(2,128)}, s32[144,2]{0,1:T(2,128)S(1)}, u32[]{:S(2)}) copy-start(s32[144,2]{0,1:T(2,128)S(1)} %eq.112) | copy-start | bytes 3460
  163.9 70.7 %copy-start.19 = (f32[144,768]{1,0:T(8,128)}, f32[144,768]{1,0:T(8,128)S(1)}, u32[]{:S(2)}) copy-start(f32[144,768]{1,0:T(8,128)S(1)} %get-tuple-element.272) | copy-start | bytes 1327108
  164.7 69.5 %copy-start.15 = (bf16[144,768]{1,0:T(8,128)(2,1)}, bf16[144,768]{1,0:T(8,128)(2,1)S(1)}, u32[]{:S(2)}) copy-start(bf16[144,768]{1,0:T(8,128)(2,1)S(1)} %multiply_convert_fusion.6) | copy-start | bytes 663556
  251.9 26.5 %all-to-all-start.4 = ((bf16[16,216,128]{2,1,0:T(8,128)(2,1)}), bf16[16,216,128]{2,1,0:T(8,128)(2,1)}, u32[]{:S(2)}, u32[]{:S(2)}) async-start(bf16[16,216,128]{2,1,0:T(8,128)(2,1)} %fusion.71), calls=%async_computation.4 | async-start | bytes 1769472 | tf_op jit(solution)/shard_map/all_to_all | solution.py:174
  289.3 12.5 %all-to-all-start.5 = ((bf16[16,72,128]{2,1,0:T(8,128)(2,1)}), bf16[16,72,128]{2,1,0:T(8,128)(2,1)S(1)}, u32[]{:S(2)}, u32[]{:S(2)}) async-start(bf16[16,72,128]{2,1,0:T(8,128)(2,1)} %bitcast.71), calls=%async_computation.5 | async-start | bytes 589824 | tf_op jit(solution)/shard_map/all_to_all | solution.py:174
  315.0 19.5 %all-to-all-start.6 = ((bf16[8,80,768]{2,1,0:T(8,128)(2,1)}), bf16[8,80,768]{2,1,0:T(8,128)(2,1)}, u32[]{:S(2)}, u32[]{:S(2)}) async-start(bf16[8,80,768]{2,1,0:T(8,128)(2,1)} %bitcast.431), calls=%async_computation.6 | async-start | bytes 1966080 | tf_op jit(solution)/shard_map/all_to_all | solution.py:174
  355.6 19.9 %all-to-all-start.7 = ((bf16[8,80,768]{2,1,0:T(8,128)(2,1)}), bf16[8,80,768]{2,1,0:T(8,128)(2,1)}, u32[]{:S(2)}, u32[]{:S(2)}) async-start(bf16[8,80,768]{2,1,0:T(8,128)(2,1)} %pad_maximum_fusion.4), calls=%async_computation.7 | async-start | bytes 1966080 | tf_op jit(solution)/shard_map/all_to_all | solution.py:174
  390.1 12.6 %all-to-all-start.8 = ((bf16[16,72,128]{2,1,0:T(8,128)(2,1)}), bf16[16,72,128]{2,1,0:T(8,128)(2,1)S(1)}, u32[]{:S(2)}, u32[]{:S(2)}) async-start(bf16[16,72,128]{2,1,0:T(8,128)(2,1)} %pad.40), calls=%async_computation.8 | async-start | bytes 589824 | tf_op jit(solution)/shard_map/all_to_all | solution.py:174
  417.6 18.3 %all-to-all-start.9 = ((bf16[16,216,128]{2,1,0:T(8,128)(2,1)}), bf16[16,216,128]{2,1,0:T(8,128)(2,1)S(1)}, u32[]{:S(2)}, u32[]{:S(2)}) async-start(bf16[16,216,128]{2,1,0:T(8,128)(2,1)} %pad_maximum_fusion.5), calls=%async_computation.9 | async-start | bytes 1769472 | tf_op jit(solution)/shard_map/all_to_all | solution.py:174
  421.2 263.1 %all-reduce.13.cloned.1.call-start = ((), (), s32[]{:S(2)}) async-start(), calls=%async_computation.19 | async-start | bytes 14155776
  422.9 1.7 collective-permute-start.4
  472.7 2.2 collective-permute-start.6
  472.9 3.6 collective-permute-start.3
  473.6 9.0 %collective-permute-start.5 = (bf16[144,3456]{1,0:T(8,128)(2,1)S(1)}, bf16[144,3456]{1,0:T(8,128)(2,1)S(1)}, u32[]{:S(2)}, u32[]{:S(2)}) collective-permute-start(bf16[144,3456]{1,0:T(8,128)(2,1)S(1)} %pad_maximum_fusion.3), channel_id=1, source_target_pairs={{0,16},{16,0},{1,17},{17,1},{2,18},{18,2},{3,19},{19,3},{4,20},{20... | collective-permute-start | bytes 2985992 | tf_op jit(solution)/shard_map/ppermute | solution.py:232
  491.9 242.5 %reduce-scatter.4.cloned.1.call-start = ((), (), s32[]{:S(2)}) async-start(), calls=%async_computation.20 | async-start | bytes 10027008
  533.3 24.5 %all-to-all-start.10 = ((bf16[16,72,128]{2,1,0:T(8,128)(2,1)}), bf16[16,72,128]{2,1,0:T(8,128)(2,1)S(1)}, u32[]{:S(2)}, u32[]{:S(2)}) async-start(bf16[16,72,128]{2,1,0:T(8,128)(2,1)} %pad.41), calls=%async_computation.10 | async-start | bytes 589824 | tf_op jit(solution)/shard_map/all_to_all | solution.py:174
  569.1 30.6 %all-to-all-start.11 = ((bf16[16,216,128]{2,1,0:T(8,128)(2,1)}), bf16[16,216,128]{2,1,0:T(8,128)(2,1)S(1)}, u32[]{:S(2)}, u32[]{:S(2)}) async-start(bf16[16,216,128]{2,1,0:T(8,128)(2,1)} %pad_maximum_fusion.6), calls=%async_computation.11 | async-start | bytes 1769472 | tf_op jit(solution)/shard_map/all_to_all | solution.py:174
  576.6 21.7 %collective-permute-start.1 = (bf16[144,1152]{1,0:T(8,128)(2,1)S(1)}, bf16[144,1152]{1,0:T(8,128)(2,1)S(1)}, u32[]{:S(2)}, u32[]{:S(2)}) collective-permute-start(bf16[144,1152]{1,0:T(8,128)(2,1)S(1)} %pad_maximum_fusion.14), channel_id=1, source_target_pairs={{0,16},{16,0},{1,17},{17,1},{2,18},{18,2},{3,19},{19,3},{4,20},{20... | collective-permute-start | bytes 995336 | tf_op jit(solution)/shard_map/ppermute | solution.py:232
  613.7 2.6 collective-permute-start
  614.8 1.4 collective-permute-start.2
  622.2 59.8 %all-to-all-start.12 = ((bf16[16,104,768]{2,1,0:T(8,128)(2,1)}), bf16[16,104,768]{2,1,0:T(8,128)(2,1)}, u32[]{:S(2)}, u32[]{:S(2)}) async-start(bf16[16,104,768]{2,1,0:T(8,128)(2,1)} %pad_dynamic-update-slice_fusion), calls=%async_computation.12 | async-start | bytes 5111808 | tf_op jit(solution)/shard_map/all_to_all | solution.py:174
  689.3 12.2 %all-to-all-start.13 = ((bf16[4,104,768]{2,1,0:T(8,128)(2,1)}), bf16[4,104,768]{2,1,0:T(8,128)(2,1)S(1)}, u32[]{:S(2)}, u32[]{:S(2)}) async-start(bf16[4,104,768]{2,1,0:T(8,128)(2,1)} %copy.578), calls=%async_computation.13 | async-start | bytes 1277952 | tf_op jit(solution)/shard_map/all_to_all | solution.py:174
  (129 other events, 570.3 us)
Sparse Core Ops, SparseCore 0:
  11.5 69.6 all-gather.6
  84.6 90.4 all-gather.8
  177.2 53.0 all-gather.10
  232.3 58.4 all-gather.12
  492.0 129.2 all-reduce.12
  625.0 109.2 reduce-scatter.3

commit v2 on v1

--- a/solution.py
+++ b/solution.py
@@ -165,9 +165,10 @@
 
 def table_sums(tile):
     distance = tile_distance()
-    above = [jnp.sum(jnp.where(distance >= first, tile, 0.0)) for first in bucket_starts()]
-    above.append(jnp.zeros((), f32))
-    return jnp.stack([above[b] - above[b + 1] for b in range(BUCKETS)])
+    first = jnp.array(bucket_starts(), jnp.int32)[:, None, None]
+    last = jnp.array(bucket_starts()[1:] + [GROUP], jnp.int32)[:, None, None]
+    inside = (distance[None] >= first) & (distance[None] < last)
+    return jnp.sum(jnp.where(inside, tile[None], 0.0), axis=(1, 2))
 
 
 def exchange(blocks, axes):
@@ -205,39 +206,55 @@
     return pair[0], pair[1], from_head_single(blocks[:, ROWS:])
 
 
-def attend_forward(x, scales, weights, bias, start):
+def spread_matrix():
+    out = lax.broadcasted_iota(jnp.int32, (WIDTH, 1024), 1)
+    source = lax.broadcasted_iota(jnp.int32, (WIDTH, 1024), 0)
+    return ((out % 8 < 6) & (source == out // 8 * 6 + out % 8)).astype(bf16)
+
+
+def spread(values, places):
+    return dot(values, places).astype(bf16)
+
+
+def gather_back(values, places):
+    return dot_back(values.astype(bf16), places)
+
+
+def attend_forward(x, scales, w_qkv, w_out, places, bias, start):
     normed, inv = normalize(x, scales)
-    q = (dot(normed, weights[0]) * SCALE).astype(bf16)
-    k = dot(normed, weights[1]).astype(bf16)
-    v = dot(normed, weights[2]).astype(bf16)
+    qkv = dot(spread(normed, places), w_qkv)
+    q = (qkv[:, :WIDTH] * SCALE).astype(bf16)
+    k = qkv[:, WIDTH : 2 * WIDTH].astype(bf16)
+    v = qkv[:, 2 * WIDTH :].astype(bf16)
     qk0, qk1, vv = send_heads(q, k, v)
     o, lse = head_forward(qk0, qk1, vv, bias, start)
     attended = from_head_single(exchange(o.reshape(SLOTS, TOK, 2 * HEAD_DIM), LINE)[:HEADS])
-    return x + dot(attended, weights[3]), (normed, inv, qk0, qk1, vv, lse, attended)
-
-
-def attend_backward(grad, x, scales, weights, bias, start, saved):
+    x = x + dot(spread(attended, places), w_out)
+    return x, (normed, inv, qk0, qk1, vv, lse, attended)
+
+
+def attend_backward(grad, x, scales, w_qkv, w_out, places, bias, start, saved):
     normed, inv, qk0, qk1, vv, lse, attended = saved
     branch = grad.astype(bf16)
-    grad_attended = dot_back(branch, weights[3]).astype(bf16)
+    grad_attended = gather_back(dot_back(branch, w_out), places).astype(bf16)
     grad_o = exchange(pad_heads(by_head_single(grad_attended)), LINE).reshape(GROUP, 2 * HEAD_DIM)
     dqk0, dqk1, dv, tile = head_backward(qk0, qk1, vv, grad_o, bias, start, lse)
-    dq, dk, dv = return_heads(dqk0, dqk1, dv)
-    grad_normed = dot_back(dq, weights[0]) + dot_back(dk, weights[1]) + dot_back(dv, weights[2])
+    heads = jnp.concatenate(return_heads(dqk0, dqk1, dv), axis=1)
+    grad_normed = gather_back(dot_back(heads, w_qkv), places)
     grad_x, grad_scales = normalize_back(grad_normed, x, inv, scales)
-    return grad + grad_x, grad_scales, branch, (dq, dk, dv), tile
+    return grad + grad_x, grad_scales, branch, heads, tile
 
 
 def other_core(value):
     return lax.ppermute(value, "c", [(0, 1), (1, 0)])
 
 
-def select_columns(core):
+def select_columns(core, line_first):
     out = lax.broadcasted_iota(jnp.int32, (WIDTH, WIDTH // 2), 1)
     source = lax.broadcasted_iota(jnp.int32, (WIDTH, WIDTH // 2), 0)
-    line, rest = out // 24, out % 24
-    z, i = rest // 6, rest % 6
-    return (source == ((z * 2 + core) * 16 + line) * 6 + i).astype(bf16)
+    outer, i = out // 6, out % 6
+    z, line = (outer % 4, outer // 4) if line_first else (outer // SLOTS, outer % SLOTS)
+    return (source == ((z * 2 + core) * SLOTS + line) * 6 + i).astype(bf16)
 
 
 def pick(a, selector):
@@ -251,23 +268,23 @@
     core = lax.axis_index("c")
     line_rank = lax.axis_index("y") * 4 + lax.axis_index("x")
 
-    first_pack = jnp.concatenate([qkv_weights[0], out_weights[:1]], axis=0)
-    second_pack = jnp.concatenate(
-        [
-            ffn_in.reshape(6, 4, WIDTH).transpose(1, 0, 2),
-            ffn_out.reshape(4, 6, WIDTH),
-            qkv_weights[1],
-            out_weights[1:],
-        ],
-        axis=0,
-    )
-    first = lax.all_gather(first_pack, ALL, axis=1, tiled=True)
-    second = lax.all_gather(second_pack, ALL, axis=1, tiled=True)
+    places = spread_matrix()
+    ffn_in_units = ffn_in.reshape(6, 128, 3, 8).transpose(0, 2, 1, 3).reshape(6, FF)
+    attention = [
+        jnp.concatenate([qkv_weights[l, 0], qkv_weights[l, 1], qkv_weights[l, 2], out_weights[l]], axis=1)
+        for l in range(2)
+    ]
+    first_pack = jnp.pad(jnp.concatenate([attention[0], ffn_in_units], axis=1), ((0, 2), (0, 0)))
+    first_pack = jnp.concatenate([first_pack, ffn_out[:8], ffn_out[8:16], ffn_out[16:]], axis=1)
+    second_pack = jnp.pad(attention[1], ((0, 2), (0, 0)))
+    first = lax.all_gather(first_pack, ALL, axis=0, tiled=True)
+    second = lax.all_gather(second_pack, ALL, axis=0, tiled=True)
     w_expert_in = lax.all_gather(expert_in[0], LINE, axis=0, tiled=True)
     w_expert_out = lax.all_gather(expert_out[0], LINE, axis=0, tiled=True)
-    w_in = [second[j] for j in range(4)]
-    w_out = second[4:8].reshape(4, 128, 6, WIDTH).transpose(1, 0, 2, 3).reshape(FF, WIDTH)
-    weights_one = second[8:]
+    qkv_zero, out_zero = first[:, : 3 * WIDTH], first[:, 3 * WIDTH : 4 * WIDTH]
+    qkv_one, out_one = second[:, : 3 * WIDTH], second[:, 3 * WIDTH :]
+    w_in = first[:, 4 * WIDTH : 8 * WIDTH]
+    w_out = [first[:, (8 + g) * WIDTH : (9 + g) * WIDTH] for g in range(3)]
 
     small = jnp.concatenate([norm_gains.reshape(24), router.reshape(48), rel_table])
     small = jnp.pad(small, (0, 128 - 75))[None, None, :]
@@ -287,12 +304,12 @@
     start = jnp.max(jnp.where(position >= ends[None], ends[None], 0), axis=2)
 
     x0 = hidden_in.reshape(ROWS, WIDTH).astype(f32)
-    x1, saved_one = attend_forward(x0, gains[0], first, bias[0], start)
+    x1, saved_one = attend_forward(x0, gains[0], qkv_zero, out_zero, places, bias[0], start)
     c, inv_c = normalize(x1, gains[1])
-    u = jnp.concatenate([dot(c, w) for w in w_in], axis=1)
+    u = dot(spread(c, places), w_in)
     h = gelu(u).astype(bf16)
-    x2 = x1 + dot(h, w_out)
-    x3, saved_three = attend_forward(x2, gains[2], weights_one, bias[1], start)
+    x2 = x1 + sum(dot(h[:, g * 1024 : (g + 1) * 1024], w_out[g]) for g in range(3))
+    x3, saved_three = attend_forward(x2, gains[2], qkv_one, out_one, places, bias[1], start)
 
     e, inv_e = normalize(x3, gains[3])
     logits = dot(e, w_router)
@@ -333,9 +350,6 @@
         dot_outer(expert_rows, due[:, j * WIDTH : (j + 1) * WIDTH]).astype(bf16).reshape(SLOTS, 48, WIDTH)
         for j in range(4)
     ] + [dot_outer(he, grad_rows).astype(bf16).reshape(SLOTS, 192, WIDTH)]
-    expert_sum = lax.psum_scatter(
-        jnp.concatenate(expert_parts, axis=1), LINE, scatter_dimension=0, tiled=False
-    ).astype(f32)
 
     dgates = jnp.stack([jnp.sum(grad_four * p, axis=-1) for p in picked], axis=1)
     dchosen = gates * (dgates - jnp.sum(gates * dgates, axis=-1, keepdims=True))
@@ -345,54 +359,56 @@
     grad_x, gain_four = normalize_back(grad_e, x3, inv_e, gains[3])
     grad_three = grad_four + grad_x
 
-    selector = select_columns(core)
-    selector_other = select_columns(1 - core)
-
-    def share(a, b):
-        mine, theirs = pick(a, selector), pick(a, selector_other)
+
+    def share(a, b, line_first):
+        mine = pick(a, select_columns(core, line_first))
+        theirs = pick(a, select_columns(1 - core, line_first))
         got = other_core(jnp.concatenate([theirs, b], axis=1))
         return (
             jnp.concatenate([mine, got[:, : WIDTH // 2]], axis=0),
             jnp.concatenate([b, got[:, WIDTH // 2 :]], axis=0),
         )
 
-    def chunks(a, b):
+    def chunks(a, b, count):
         return [
-            dot_outer(a, b[:, j * WIDTH : (j + 1) * WIDTH]).astype(bf16).reshape(SLOTS, 24, WIDTH)
+            dot_outer(a, b[:, j * WIDTH : (j + 1) * WIDTH]).astype(bf16).reshape(count, -1, WIDTH)
             for j in range(b.shape[1] // WIDTH)
         ]
 
     grad_two, gain_three, branch_three, heads_three, tile_three = attend_backward(
-        grad_three, x2, gains[2], weights_one, bias[1], start, saved_three
-    )
-    parts = chunks(*share(saved_three[0], jnp.concatenate(heads_three, axis=1)))
-    parts += chunks(*share(saved_three[6], branch_three))
+        grad_three, x2, gains[2], qkv_one, out_one, places, bias[1], start, saved_three
+    )
+    parts = chunks(*share(saved_three[0], heads_three, True), SLOTS)
+    parts += chunks(*share(saved_three[6], branch_three, True), SLOTS)
 
     branch_two = grad_two.astype(bf16)
-    grad_h = dot_back(branch_two, w_out)
+    grad_h = jnp.concatenate([dot_back(branch_two, w) for w in w_out], axis=1)
     gelu_back_two = jax.vjp(gelu, u)[1]
     du = gelu_back_two(grad_h)[0].astype(bf16)
-    grad_c = sum(dot_back(du[:, j * WIDTH : (j + 1) * WIDTH], w_in[j]) for j in range(4))
+    grad_c = gather_back(dot_back(du, w_in), places)
     grad_x, gain_two = normalize_back(grad_c, x1, inv_c, gains[1])
     grad_one = grad_two + grad_x
-    parts += chunks(*share(c, du))
-    halves = h.reshape(ROWS, 4, 2, FF // 8)
+    parts += chunks(*share(c, du, True), SLOTS)
+    parts += chunks(*share(saved_one[6], grad_one.astype(bf16), True), SLOTS)
+    halves = h.reshape(ROWS, 12, 2, BLOCK)
     mine = lax.dynamic_index_in_dim(halves, core, axis=2, keepdims=False).reshape(ROWS, FF // 2)
     theirs = lax.dynamic_index_in_dim(halves, 1 - core, axis=2, keepdims=False).reshape(ROWS, FF // 2)
     got = other_core(jnp.concatenate([theirs, branch_two], axis=1))
     mine = jnp.concatenate([mine, got[:, : FF // 2]], axis=0)
     second_grad = dot_outer(mine, jnp.concatenate([branch_two, got[:, FF // 2 :]], axis=0))
-    second_grad = second_grad.astype(bf16).reshape(4, SLOTS, 24, WIDTH)
-    parts += [second_grad[z] for z in range(4)]
-    early_sum = lax.psum_scatter(
-        jnp.concatenate(parts, axis=1), LINE, scatter_dimension=0, tiled=False
-    )
+    second_grad = second_grad.astype(bf16).reshape(12, SLOTS, 8, WIDTH).transpose(1, 0, 2, 3)
+    parts.append(second_grad.reshape(SLOTS, 96, WIDTH))
+    early_sum = lax.optimization_barrier(
+        lax.psum_scatter(
+            jnp.concatenate(parts + expert_parts, axis=1), LINE, scatter_dimension=0, tiled=False
+        )
+    )
+    expert_sum = early_sum[312:]
 
     grad_zero, gain_one, branch_one, heads_one, tile_one = attend_backward(
-        grad_one, x0, gains[0], first, bias[0], start, saved_one
-    )
-    late = chunks(*share(saved_one[0], jnp.concatenate(heads_one, axis=1)))
-    late += chunks(*share(saved_one[6], branch_one))
+        grad_one, x0, gains[0], qkv_zero, out_zero, places, bias[0], start, saved_one
+    )
+    late = chunks(*share(saved_one[0], heads_one, False), 64)
 
     own_head = (jnp.arange(HEADS, dtype=jnp.int32) == line_rank).astype(f32)
     table_grad = jnp.stack([table_sums(tile_one), table_sums(tile_three)])
@@ -404,35 +420,31 @@
     tiny_mine = lax.dynamic_index_in_dim(tiny, core, axis=1, keepdims=False)
     tiny_theirs = lax.dynamic_index_in_dim(tiny, 1 - core, axis=1, keepdims=False)
     tiny_sum = tiny_mine + other_core(tiny_theirs)
-    tiny_sum = tiny_sum.transpose(1, 0, 2).reshape(SLOTS, 1, 512)
-    tiny_sum = jnp.pad(tiny_sum, ((0, 0), (0, 7), (0, 256))).astype(bf16)
-    late_blocks = exchange(jnp.concatenate(late + [tiny_sum], axis=1), LINE)
+    tiny_sum = jnp.pad(tiny_sum.reshape(64, 1, 128), ((0, 0), (0, 5), (0, WIDTH - 128)))
+    late_blocks = exchange(jnp.concatenate(late + [tiny_sum.astype(bf16)], axis=1), ("z", "y", "x"))
     late_sum = jnp.sum(late_blocks.astype(f32), axis=0)
-
-    tiny_rows = late_sum[96, :512].reshape(4, 1, 128)
-    tiny_rows = jnp.pad(tiny_rows, ((0, 0), (0, 7), (0, WIDTH - 128)))
-    late_rows = late_sum[:96].reshape(4, 4, 6, WIDTH)
-    early = early_sum.astype(f32)
-    early_rows = early[:192].reshape(8, 4, 6, WIDTH)
-    ffn_out_rows = early[192:].reshape(4, 24, WIDTH)
-    six = jnp.concatenate([late_rows, early_rows], axis=0).transpose(1, 0, 2, 3).reshape(4, 72, WIDTH)
-    last = exchange(jnp.concatenate([six, ffn_out_rows, tiny_rows], axis=1).astype(bf16), ("z",))
+    tiny = late_sum[18, :75]
+
+    early_rows = early_sum[:216].reshape(9, 4, 6, WIDTH).transpose(1, 0, 2, 3).reshape(4, 54, WIDTH)
+    ffn_out_rows = early_sum[216:312].reshape(3, 4, 8, WIDTH).transpose(1, 0, 2, 3).reshape(4, 24, WIDTH)
+    last = jnp.concatenate([ffn_out_rows, early_rows], axis=1)
+    last = exchange(jnp.pad(last, ((0, 0), (0, 2), (0, 0))), ("z",))
     last = jnp.sum(last.astype(f32), axis=0)
-    six = last[:72].reshape(12, 6, WIDTH)
-    tiny = last[96, :75]
+    six = last[24:78].reshape(9, 6, WIDTH)
+    ffn_in_part = six[4:8].transpose(1, 0, 2).reshape(6, 3, 128, 8).transpose(0, 2, 1, 3)
     out_shape = hidden_in.shape
     return (
         hidden_out.reshape(out_shape),
         grad_zero.reshape(out_shape),
         tiny[:24].reshape(4, 6),
-        jnp.stack([six[0:3], six[4:7]]),
-        jnp.stack([six[3], six[7]]),
+        jnp.stack([late_sum[:18].reshape(3, 6, WIDTH), six[0:3]]),
+        jnp.stack([six[8], six[3]]),
         tiny[72:75],
-        six[8:12].transpose(1, 0, 2).reshape(6, FF),
-        last[72:96],
+        ffn_in_part.reshape(6, FF),
+        last[:24],
         tiny[24:72].reshape(6, EXPERTS),
-        expert_sum[:192].reshape(4, 48, WIDTH).transpose(1, 0, 2).reshape(1, 48, FF),
-        expert_sum[192:].reshape(1, 192, WIDTH),
+        expert_sum[:192].astype(f32).reshape(4, 48, WIDTH).transpose(1, 0, 2).reshape(1, 48, FF),
+        expert_sum[192:].astype(f32).reshape(1, 192, WIDTH),
     )
 
 

time: 754 us -> 648 us (0.86)
  local copies, waits for them, and re-layouts: 217 us -> 132 us
  between operations: 54.7 us -> 16.7 us
  matrix products: 107 us -> 129 us
  waiting for transfers between devices: 212 us -> 197 us
  other arithmetic: 48.4 us -> 56.9 us
    slice x17, local copies, waits for them, and re-layouts: 65.9 us -> 8.15 us  [the longest x4 2.17 us: attend_forward(): k = qkv[:, WIDTH:2 * WIDTH].astype(bf16)]
    unnamed x8 -> x6, waiting for transfers between devices: 29.4 us -> 1.25 us
    concatenate x11 -> x2, local copies, waits for them, and re-layouts: 16.3 us -> 2.58 us  [the longest x1 2.57 us: on_device(): jnp.concatenate(parts + expert_parts, axis=1)]
    unnamed x299 -> x319, local copies, waits for them, and re-layouts: 43.6 us -> 29.9 us
    dot_general x20, matrix products: 20.5 us -> 33.3 us  [dot_outer(): lax.dot_general(a, b, (((0,), (0,)), ((), ())), preferred_element_type=f32)]
    all_to_all x14, waiting for transfers between devices: 131 us -> 141 us  [exchange(): return lax.all_to_all(blocks, axes, split_axis=0, concat_axis=0, tiled=True)]
    dot_general x27 -> x22, matrix products: 50.7 us -> 56.7 us  [dot(): lax.dot_general(a, b, (((1,), (0,)), ((), ())), preferred_element_type=f32)]
    dot_general x16 -> x11, matrix products: 35.5 us -> 38.6 us  [dot_back(): lax.dot_general(a, b, (((1,), (1,)), ((), ())), preferred_element_type=f32)]
  transfers between devices with their start and end apart: 27 -> 26, of which waited for: 18 -> 16; matrix products, arithmetic and copies ran while one was open for 37% -> 31% of each run, Pallas kernels for 3% -> 4%
where the time goes in v2:
time: 648 us; the launch traced here: 639 us
  waiting for transfers between devices  197 us (30%)
  local copies, waits for them, and re-layouts  132 us (20%)
  matrix products  129 us (20%)
  starting transfers between devices  73.1 us (11%)
  other arithmetic  56.9 us (9%)
  Pallas kernels  34.8 us (5%)
  between operations  16.7 us (3%)
    all_to_all x14, waiting for transfers between devices, exchange(): return lax.all_to_all(blocks, axes, split_axis=0, concat_axis=0, tiled=True)  141 us
    all_to_all x14, starting transfers between devices, exchange(): return lax.all_to_all(blocks, axes, split_axis=0, concat_axis=0, tiled=True)  70.3 us
    dot_general x22, matrix products, dot(): lax.dot_general(a, b, (((1,), (0,)), ((), ())), preferred_element_type=f32)  56.7 us
    all_gather x1, waiting for transfers between devices, on_device(): first = lax.all_gather(first_pack, ALL, axis=0, tiled=True)  52.4 us
    dot_general x11, matrix products, dot_back(): lax.dot_general(a, b, (((1,), (1,)), ((), ())), preferred_element_type=f32)  38.6 us
    dot_general x20, matrix products, dot_outer(): lax.dot_general(a, b, (((0,), (0,)), ((), ())), preferred_element_type=f32)  33.3 us
    unnamed x319, local copies, waits for them, and re-layouts  29.9 us
    select_n x2, other arithmetic, bias_tile(): result = jnp.where(distance >= first, entries[b], result)  20.2 us
  transfers between devices with their start and end apart: 26, of which 16 were waited for; matrix products, arithmetic and copies ran while one was open for 31% of the time, Pallas kernels for 4%

profile of v2, /device:TPU:0, one launch (start us, length us, event | category | flops | bytes accessed | tf_op | source)
XLA Modules:
  0.0 638.8 jit_solution(1432623383977273185)
XLA Ops:
  14.6 7.1 %all-to-all-start = ((bf16[16,8,128]{2,1,0:T(8,128)(2,1)}), bf16[16,8,128]{2,1,0:T(8,128)(2,1)S(1)}, u32[]{:S(2)}, u32[]{:S(2)}) async-start(bf16[16,8,128]{2,1,0:T(8,128)(2,1)} %broadcast_in_dim.172), calls=%async_computation | async-start | bytes 65536 | tf_op jit(solution)/shard_map/all_to_all | solution.py:175
  30.1 5.4 all-to-all-start.1
  36.4 6.6 %all-to-all-done.1 = bf16[8,128,128]{2,1,0:T(8,128)(2,1)S(1)} async-done(((bf16[8,128,128]{2,1,0:T(8,128)(2,1)}), bf16[8,128,128]{2,1,0:T(8,128)(2,1)S(1)}, u32[]{:S(2)}, u32[]{:S(2)}) %all-to-all-start.1) | async-done | bytes 262176 | tf_op jit(solution)/shard_map/all_to_all | solution.py:175
  43.6 52.4 %all-gather.7.cloned.1.call-done = bf16[1024,8448]{1,0:T(8,128)(2,1)} async-done(((bf16[8,8448]{1,0:T(8,128)(2,1)}), bf16[1024,8448]{1,0:T(8,128)(2,1)}) %all-gather.7.cloned.1.call-update) | async-done | bytes 17301520 | tf_op jit(solution)/shard_map/all_gather | solution.py:280
  96.0 5.0 fusion.361
  105.9 7.3 %all-to-all-start.2 = ((bf16[16,216,128]{2,1,0:T(8,128)(2,1)}), bf16[16,216,128]{2,1,0:T(8,128)(2,1)S(1)}, u32[]{:S(2)}, u32[]{:S(2)}) async-start(bf16[16,216,128]{2,1,0:T(8,128)(2,1)} %fusion.147), calls=%async_computation.2 | async-start | bytes 1769472 | tf_op jit(solution)/shard_map/all_to_all | solution.py:175
  117.4 10.0 %select_select_fusion.2.bias_ref = f32[128,1152]{1,0:T(8,128)S(1)} fusion(f32[]{:T(128)} %bitcast.31, f32[]{:T(128)} %bitcast.30, f32[]{:T(128)} %bitcast.29, f32[]{:T(128)} %bitcast.28, f32[]{:T(128)} %bitcast.27, f32[]{:T(128)} %bitcast.26, f32[]{:T(128)} %bitcast.25, f32[]{:T(128)} %bitcast.24, f32[]{:T(128)} %bitcast.23, f32[]{:T(128)} %bitcast.22, ...), kind=kLoop, calls=%fused_computation.233 | loop fusion | flops 5013504 | bytes 589888 | tf_op jit(solution)/shard_map/jit(_where)/select_n | solution.py:162
  129.4 8.1 %shard_map.248 = (bf16[1152,128]{1,0:T(8,128)(2,1)}, f32[1152,2]{1,0:T(8,128)S(1)}) custom-call(bf16[1152,128]{1,0:T(8,128)(2,1)S(1)} %bitcast.286, bf16[1152,128]{1,0:T(8,128)(2,1)S(1)} %bitcast.284, bf16[1152,128]{1,0:T(8,128)(2,1)S(1)} %bitcast.282, f32[128,1152]{1,0:T(8,128)S(1)} %select_select_fusion.2.bias_ref, s32[1152,2]{1,0:T(8,128)S(1)} %copy.348.start_ref), custom_call_target="tpu_custom_call" | custom-call | flops 339738624 | bytes 1769472 | tf_op jit(solution)/shard_map/pallas_call | solution.py:118
  137.6 5.6 all-to-all-start.3
  143.2 10.1 %select_select_fusion.1.bias_ref = f32[128,1152]{1,0:T(8,128)S(1)} fusion(f32[]{:T(128)} %bitcast.61, f32[]{:T(128)} %bitcast.60, f32[]{:T(128)} %bitcast.59, f32[]{:T(128)} %bitcast.58, f32[]{:T(128)} %bitcast.57, f32[]{:T(128)} %bitcast.56, f32[]{:T(128)} %bitcast.55, f32[]{:T(128)} %bitcast.54, f32[]{:T(128)} %bitcast.53, f32[]{:T(128)} %bitcast.52, ...), kind=kLoop, calls=%fused_computation.232 | loop fusion | flops 5013504 | bytes 589888 | tf_op jit(solution)/shard_map/jit(_where)/select_n | solution.py:162
  162.5 6.7 %multiply_convert_fusion.1 = (bf16[144,3072]{1,0:T(8,128)(2,1)}, f32[144,3072]{1,0:T(8,128)}) fusion(bf16[1024,8448]{1,0:T(8,128)(2,1)} %all-gather.7.cloned.1.call-done, bf16[144,768]{1,0:T(8,128)(2,1)S(1)} %multiply_convert_fusion.4, s32[1024]{0:T(1024)S(1)} %get-tuple-element.233, s32[1024]{0:T(1024)S(1)} %get-tuple-element.236, ...), kind=kOutput, calls=%fused_computation.73 | convolution fusion | flops 1142095872 | bytes 9185280 | tf_op jit(solution)/shard_map/dot_general | solution.py:34
  176.0 5.3 fusion.368
  199.0 7.9 %all-to-all-start.4 = ((bf16[16,216,128]{2,1,0:T(8,128)(2,1)}), bf16[16,216,128]{2,1,0:T(8,128)(2,1)}, u32[]{:S(2)}, u32[]{:S(2)}) async-start(bf16[16,216,128]{2,1,0:T(8,128)(2,1)} %fusion.148), calls=%async_computation.4 | async-start | bytes 1769472 | tf_op jit(solution)/shard_map/all_to_all | solution.py:175
  215.6 16.9 %all-to-all-done.4 = bf16[16,216,128]{2,1,0:T(8,128)(2,1)} async-done(((bf16[16,216,128]{2,1,0:T(8,128)(2,1)}), bf16[16,216,128]{2,1,0:T(8,128)(2,1)}, u32[]{:S(2)}, u32[]{:S(2)}) %all-to-all-start.4) | async-done | bytes 884768 | tf_op jit(solution)/shard_map/all_to_all | solution.py:175
  233.7 8.2 %shard_map.249 = (bf16[1152,128]{1,0:T(8,128)(2,1)}, f32[1152,2]{1,0:T(8,128)S(1)}) custom-call(bf16[1152,128]{1,0:T(8,128)(2,1)S(1)} %bitcast.292, bf16[1152,128]{1,0:T(8,128)(2,1)S(1)} %bitcast.290, bf16[1152,128]{1,0:T(8,128)(2,1)S(1)} %bitcast.288, f32[128,1152]{1,0:T(8,128)S(1)} %select_select_fusion.1.bias_ref, s32[1152,2]{1,0:T(8,128)S(1)} %copy.348.start_ref), custom_call_target="tpu_custom_call" | custom-call | flops 339738624 | bytes 1769472 | tf_op jit(solution)/shard_map/pallas_call | solution.py:118
  248.9 8.5 %all-to-all-done.5 = bf16[16,72,128]{2,1,0:T(8,128)(2,1)S(1)} async-done(((bf16[16,72,128]{2,1,0:T(8,128)(2,1)}), bf16[16,72,128]{2,1,0:T(8,128)(2,1)S(1)}, u32[]{:S(2)}, u32[]{:S(2)}) %all-to-all-start.5) | async-done | bytes 294944 | tf_op jit(solution)/shard_map/all_to_all | solution.py:175
  276.8 6.8 %dynamic-slice_reduce_fusion.1 = (bf16[144,12,128]{2,1,0:T(8,128)(2,1)S(1)}, bf16[144,12,128]{2,1,0:T(8,128)(2,1)S(1)}) fusion(bf16[144,12,2,128]{3,2,1,0:T(2,128)(2,1)} %reshape.697, s32[]{:T(128)S(6)} %select_n.328, s32[]{:T(128)S(6)} %select_n.329), kind=kLoop, calls=%fused_computation.196 | loop fusion | bytes 1769480 | tf_op jit(solution)/shard_map/jit(dynamic_index_in_dim)/dynamic_slice | solution.py:394
  294.3 6.1 fusion.10
  300.4 6.1 fusion.78
  320.7 7.2 %convolution_convert_fusion = bf16[3072,768]{1,0:T(8,128)(2,1)} fusion(bf16[320,768]{1,0:T(8,128)(2,1)S(1)} %bitcast.365, f32[320,3072]{1,0:T(8,128)} %fusion.10), kind=kOutput, calls=%fused_computation.9 | convolution fusion | flops 1521156096 | bytes 9142272 | tf_op jit(solution)/shard_map/dot_general | solution.py:42
  356.0 6.0 all-to-all-done.8
  366.7 9.2 %shard_map.250 = (bf16[1152,128]{1,0:T(8,128)(2,1)S(1)}, bf16[1152,128]{1,0:T(8,128)(2,1)S(1)}, bf16[1152,128]{1,0:T(8,128)(2,1)S(1)}, f32[128,1152]{1,0:T(8,128)S(1)}) custom-call(bf16[1152,128]{1,0:T(8,128)(2,1)S(1)} %bitcast.293, bf16[1152,128]{1,0:T(8,128)(2,1)S(1)} %bitcast.291, bf16[1152,128]{1,0:T(8,128)(2,1)S(1)} %bitcast.289, ...), custom_call_target="tpu_custom_call" | custom-call | flops 849346560 | bytes 3538944 | tf_op jit(solution)/shard_map/pallas_call | solution.py:135
  389.1 6.8 %all-to-all-done.9 = bf16[16,216,128]{2,1,0:T(8,128)(2,1)} async-done(((bf16[16,216,128]{2,1,0:T(8,128)(2,1)}), bf16[16,216,128]{2,1,0:T(8,128)(2,1)}, u32[]{:S(2)}, u32[]{:S(2)}) %all-to-all-start.9) | async-done | bytes 884768 | tf_op jit(solution)/shard_map/all_to_all | solution.py:175
  415.6 6.2 multiply_reduce_fusion.1
  432.5 7.4 %multiply_reduce_fusion.2 = (f32[768]{0:T(1024)}, f32[144]{0:T(256)S(1)}, f32[144,768]{1,0:T(8,128)}) fusion(f32[144,768]{1,0:T(8,128)} %copy-done.11, f32[144]{0:T(256)S(1)} %copy-done.70, f32[768]{0:T(1024)S(1)} %mul.597, s32[1024]{0:T(1024)S(1)} %copy-done.80, s32[1024]{0:T(1024)S(1)} %copy-done.92, s32[1024]{0:T(1024)S(1)} %copy-done.84, ...), kind=kOutput, calls=%fused_computation.290 | convolution fusion | flops 1138777216 | bytes 8086656 | tf_op jit(solution)/shard_map/dot_general | solution.py:38
  487.7 7.7 %all-to-all-done.10 = bf16[16,72,128]{2,1,0:T(8,128)(2,1)S(1)} async-done(((bf16[16,72,128]{2,1,0:T(8,128)(2,1)}), bf16[16,72,128]{2,1,0:T(8,128)(2,1)S(1)}, u32[]{:S(2)}, u32[]{:S(2)}) %all-to-all-start.10) | async-done | bytes 294944 | tf_op jit(solution)/shard_map/all_to_all | solution.py:175
  496.4 9.2 %shard_map.251 = (bf16[1152,128]{1,0:T(8,128)(2,1)S(1)}, bf16[1152,128]{1,0:T(8,128)(2,1)S(1)}, bf16[1152,128]{1,0:T(8,128)(2,1)S(1)}, f32[128,1152]{1,0:T(8,128)S(1)}) custom-call(bf16[1152,128]{1,0:T(8,128)(2,1)S(1)} %bitcast.287, bf16[1152,128]{1,0:T(8,128)(2,1)S(1)} %bitcast.285, bf16[1152,128]{1,0:T(8,128)(2,1)S(1)} %bitcast.283, ...), custom_call_target="tpu_custom_call" | custom-call | flops 849346560 | bytes 3538944 | tf_op jit(solution)/shard_map/pallas_call | solution.py:135
  514.9 20.6 %all-to-all-done.11 = bf16[16,216,128]{2,1,0:T(8,128)(2,1)S(1)} async-done(((bf16[16,216,128]{2,1,0:T(8,128)(2,1)}), bf16[16,216,128]{2,1,0:T(8,128)(2,1)S(1)}, u32[]{:S(2)}, u32[]{:S(2)}) %all-to-all-start.11) | async-done | bytes 884768 | tf_op jit(solution)/shard_map/all_to_all | solution.py:175
  539.5 5.9 multiply_reduce_fusion.3
  555.9 5.2 all-to-all-start.12
  562.1 47.4 %all-to-all-done.12 = bf16[64,24,768]{2,1,0:T(8,128)(2,1)S(1)} async-done(((bf16[64,24,768]{2,1,0:T(8,128)(2,1)}), bf16[64,24,768]{2,1,0:T(8,128)(2,1)S(1)}, u32[]{:S(2)}, u32[]{:S(2)}) %all-to-all-start.12) | async-done | bytes 2359328 | tf_op jit(solution)/shard_map/all_to_all | solution.py:175
  621.3 5.4 all-to-all-done.13
  (644 shorter events, 287.7 us)
Async XLA Ops:
  7.2 88.8 %all-gather.7.cloned.1.call-start = ((), (), s32[]{:S(2)}) async-start(), calls=%async_computation.15 | async-start | bytes 17436672 | tf_op jit(solution)/shard_map/all_gather | solution.py:280
  12.3 163.7 %all-gather.9.cloned.1.call-start = ((), (), s32[]{:S(2)}) async-start(), calls=%async_computation.16 | async-start | bytes 6340608 | tf_op jit(solution)/shard_map/all_gather | solution.py:281
  13.0 281.3 %all-gather.11.cloned.1.call-start = ((), (), s32[]{:S(2)}) async-start(), calls=%async_computation.17 | async-start | bytes 5013504 | tf_op jit(solution)/shard_map/all_gather | solution.py:282
  14.6 14.7 %all-to-all-start = ((bf16[16,8,128]{2,1,0:T(8,128)(2,1)}), bf16[16,8,128]{2,1,0:T(8,128)(2,1)S(1)}, u32[]{:S(2)}, u32[]{:S(2)}) async-start(bf16[16,8,128]{2,1,0:T(8,128)(2,1)} %broadcast_in_dim.172), calls=%async_computation | async-start | bytes 65536 | tf_op jit(solution)/shard_map/all_to_all | solution.py:175
  21.8 278.6 %all-gather.13.cloned.1.call-start = ((), (), s32[]{:S(2)}) async-start(), calls=%async_computation.18 | async-start | bytes 5013504 | tf_op jit(solution)/shard_map/all_gather | solution.py:283
  22.5 153.5 %copy-start.78 = (s32[1024]{0:T(1024)}, s32[1024]{0:T(1024)S(1)}, u32[]{:S(2)}) copy-start(s32[1024]{0:T(1024)S(1)} %get-tuple-element.233) | copy-start | bytes 12292
  22.6 191.9 %copy-start.95 = (s32[384]{0:T(512)}, s32[384]{0:T(512)S(1)}, u32[]{:S(2)}) copy-start(s32[384]{0:T(512)S(1)} %get-tuple-element.240) | copy-start | bytes 4612
  22.6 191.9 %copy-start.99 = (s32[384]{0:T(512)}, s32[384]{0:T(512)S(1)}, u32[]{:S(2)}) copy-start(s32[384]{0:T(512)S(1)} %get-tuple-element.241) | copy-start | bytes 4612
  22.6 191.9 %copy-start.103 = (s32[384]{0:T(512)}, s32[384]{0:T(512)S(1)}, u32[]{:S(2)}) copy-start(s32[384]{0:T(512)S(1)} %get-tuple-element.242) | copy-start | bytes 4612
  22.6 191.9 %copy-start.107 = (s32[384]{0:T(512)}, s32[384]{0:T(512)S(1)}, u32[]{:S(2)}) copy-start(s32[384]{0:T(512)S(1)} %get-tuple-element.243) | copy-start | bytes 4612
  24.6 243.2 %copy-start.64 = (s32[144,2]{0,1:T(2,128)}, s32[144,2]{0,1:T(2,128)S(1)}, u32[]{:S(2)}) copy-start(s32[144,2]{0,1:T(2,128)S(1)} %eq.165) | copy-start | bytes 3460
  30.1 12.9 %all-to-all-start.1 = ((bf16[8,128,128]{2,1,0:T(8,128)(2,1)}), bf16[8,128,128]{2,1,0:T(8,128)(2,1)S(1)}, u32[]{:S(2)}, u32[]{:S(2)}) async-start(bf16[8,128,128]{2,1,0:T(8,128)(2,1)} %broadcast_in_dim.174), calls=%async_computation.1 | async-start | bytes 524288 | tf_op jit(solution)/shard_map/all_to_all | solution.py:175
  105.9 23.4 %all-to-all-start.2 = ((bf16[16,216,128]{2,1,0:T(8,128)(2,1)}), bf16[16,216,128]{2,1,0:T(8,128)(2,1)S(1)}, u32[]{:S(2)}, u32[]{:S(2)}) async-start(bf16[16,216,128]{2,1,0:T(8,128)(2,1)} %fusion.147), calls=%async_computation.2 | async-start | bytes 1769472 | tf_op jit(solution)/shard_map/all_to_all | solution.py:175
  137.6 15.8 %all-to-all-start.3 = ((bf16[16,72,128]{2,1,0:T(8,128)(2,1)}), bf16[16,72,128]{2,1,0:T(8,128)(2,1)S(1)}, u32[]{:S(2)}, u32[]{:S(2)}) async-start(bf16[16,72,128]{2,1,0:T(8,128)(2,1)} %bitcast.33), calls=%async_computation.3 | async-start | bytes 589824 | tf_op jit(solution)/shard_map/all_to_all | solution.py:175
  199.0 33.5 %all-to-all-start.4 = ((bf16[16,216,128]{2,1,0:T(8,128)(2,1)}), bf16[16,216,128]{2,1,0:T(8,128)(2,1)}, u32[]{:S(2)}, u32[]{:S(2)}) async-start(bf16[16,216,128]{2,1,0:T(8,128)(2,1)} %fusion.148), calls=%async_computation.4 | async-start | bytes 1769472 | tf_op jit(solution)/shard_map/all_to_all | solution.py:175
  243.4 14.0 %all-to-all-start.5 = ((bf16[16,72,128]{2,1,0:T(8,128)(2,1)}), bf16[16,72,128]{2,1,0:T(8,128)(2,1)S(1)}, u32[]{:S(2)}, u32[]{:S(2)}) async-start(bf16[16,72,128]{2,1,0:T(8,128)(2,1)} %bitcast.62), calls=%async_computation.5 | async-start | bytes 589824 | tf_op jit(solution)/shard_map/all_to_all | solution.py:175
  272.2 19.9 %all-to-all-start.6 = ((bf16[8,80,768]{2,1,0:T(8,128)(2,1)}), bf16[8,80,768]{2,1,0:T(8,128)(2,1)}, u32[]{:S(2)}, u32[]{:S(2)}) async-start(bf16[8,80,768]{2,1,0:T(8,128)(2,1)} %bitcast.348), calls=%async_computation.6 | async-start | bytes 1966080 | tf_op jit(solution)/shard_map/all_to_all | solution.py:175
  313.4 19.5 %all-to-all-start.7 = ((bf16[8,80,768]{2,1,0:T(8,128)(2,1)}), bf16[8,80,768]{2,1,0:T(8,128)(2,1)}, u32[]{:S(2)}, u32[]{:S(2)}) async-start(bf16[8,80,768]{2,1,0:T(8,128)(2,1)} %pad_maximum_fusion.4), calls=%async_computation.7 | async-start | bytes 1966080 | tf_op jit(solution)/shard_map/all_to_all | solution.py:175
  349.2 12.8 %all-to-all-start.8 = ((bf16[16,72,128]{2,1,0:T(8,128)(2,1)}), bf16[16,72,128]{2,1,0:T(8,128)(2,1)S(1)}, u32[]{:S(2)}, u32[]{:S(2)}) async-start(bf16[16,72,128]{2,1,0:T(8,128)(2,1)} %pad.49), calls=%async_computation.8 | async-start | bytes 589824 | tf_op jit(solution)/shard_map/all_to_all | solution.py:175
  376.9 19.0 %all-to-all-start.9 = ((bf16[16,216,128]{2,1,0:T(8,128)(2,1)}), bf16[16,216,128]{2,1,0:T(8,128)(2,1)}, u32[]{:S(2)}, u32[]{:S(2)}) async-start(bf16[16,216,128]{2,1,0:T(8,128)(2,1)} %pad_maximum_fusion.5), calls=%async_computation.9 | async-start | bytes 1769472 | tf_op jit(solution)/shard_map/all_to_all | solution.py:175
  381.2 230.6 %reduce-scatter.4.cloned.1.call-start = ((), (), s32[]{:S(2)}) async-start(), calls=%async_computation.19 | async-start | bytes 18173952
  381.4 6.4 %collective-permute-start.3 = (bf16[144,1152]{1,0:T(8,128)(2,1)S(1)}, bf16[144,1152]{1,0:T(8,128)(2,1)S(1)}, u32[]{:S(2)}, u32[]{:S(2)}) collective-permute-start(bf16[144,1152]{1,0:T(8,128)(2,1)S(1)} %pad_maximum_fusion.15), channel_id=1, source_target_pairs={{0,16},{16,0},{1,17},{17,1},{2,18},{18,2},{3,19},{19,3},{4,20},{20... | collective-permute-start | bytes 995336 | tf_op jit(solution)/shard_map/ppermute | solution.py:249
  441.0 6.3 collective-permute-start.2
  441.2 4.2 collective-permute-start.6
  442.9 1.9 collective-permute-start.5
  443.1 10.2 %collective-permute-start.4 = (bf16[144,3456]{1,0:T(8,128)(2,1)S(1)}, bf16[144,3456]{1,0:T(8,128)(2,1)S(1)}, u32[]{:S(2)}, u32[]{:S(2)}) collective-permute-start(bf16[144,3456]{1,0:T(8,128)(2,1)S(1)} %pad_maximum_fusion.3), channel_id=1, source_target_pairs={{0,16},{16,0},{1,17},{17,1},{2,18},{18,2},{3,19},{19,3},{4,20},{20... | collective-permute-start | bytes 2985992 | tf_op jit(solution)/shard_map/ppermute | solution.py:249
  478.3 17.1 %all-to-all-start.10 = ((bf16[16,72,128]{2,1,0:T(8,128)(2,1)}), bf16[16,72,128]{2,1,0:T(8,128)(2,1)S(1)}, u32[]{:S(2)}, u32[]{:S(2)}) async-start(bf16[16,72,128]{2,1,0:T(8,128)(2,1)} %pad.50), calls=%async_computation.10 | async-start | bytes 589824 | tf_op jit(solution)/shard_map/all_to_all | solution.py:175
  506.7 28.8 %all-to-all-start.11 = ((bf16[16,216,128]{2,1,0:T(8,128)(2,1)}), bf16[16,216,128]{2,1,0:T(8,128)(2,1)S(1)}, u32[]{:S(2)}, u32[]{:S(2)}) async-start(bf16[16,216,128]{2,1,0:T(8,128)(2,1)} %pad_maximum_fusion.6), calls=%async_computation.11 | async-start | bytes 1769472 | tf_op jit(solution)/shard_map/all_to_all | solution.py:175
  545.8 2.4 collective-permute-start
  546.3 1.9 collective-permute-start.1
  555.9 53.6 %all-to-all-start.12 = ((bf16[64,24,768]{2,1,0:T(8,128)(2,1)}), bf16[64,24,768]{2,1,0:T(8,128)(2,1)S(1)}, u32[]{:S(2)}, u32[]{:S(2)}) async-start(bf16[64,24,768]{2,1,0:T(8,128)(2,1)} %fusion.32), calls=%async_computation.12 | async-start | bytes 4718592 | tf_op jit(solution)/shard_map/all_to_all | solution.py:175
  615.4 11.3 %all-to-all-start.13 = ((bf16[4,80,768]{2,1,0:T(8,128)(2,1)}), bf16[4,80,768]{2,1,0:T(8,128)(2,1)S(1)}, u32[]{:S(2)}, u32[]{:S(2)}) async-start(bf16[4,80,768]{2,1,0:T(8,128)(2,1)} %pad.53.clone), calls=%async_computation.13 | async-start | bytes 983040 | tf_op jit(solution)/shard_map/all_to_all | solution.py:175
  (139 other events, 1333.8 us)
Sparse Core Ops, SparseCore 0:
  12.4 83.5 all-gather.6
  99.6 72.5 all-gather.8
  174.3 61.0 all-gather.10
  237.3 54.2 all-gather.12
  469.9 138.7 reduce-scatter.3

commit v3 on v2

--- a/solution.py
+++ b/solution.py
@@ -59,7 +59,17 @@
     return jax.nn.gelu(u, approximate=True)
 
 
-def forward_kernel(qk0_ref, qk1_ref, v_ref, bias_ref, start_ref, o_ref, lse_ref):
+LIMIT = pltpu.CompilerParams(vmem_limit_bytes=48 * 1024 * 1024)
+
+
+def split_blocks(blocks_ref, targets):
+    whole = blocks_ref[...].astype(f32)
+    for j, target in enumerate(targets):
+        target[...] = whole[:, j * TOK : (j + 1) * TOK].reshape(GROUP, 2 * HEAD_DIM).astype(bf16)
+
+
+def forward_kernel(blocks_ref, bias_ref, start_ref, o_ref, lse_ref, qk0_ref, qk1_ref, v_ref):
+    split_blocks(blocks_ref, (qk0_ref, qk1_ref, v_ref))
     for m, qk_ref in enumerate((qk0_ref, qk1_ref)):
         lanes = slice(m * HEAD_DIM, (m + 1) * HEAD_DIM)
         keys = qk_ref[:, HEAD_DIM:]
@@ -80,9 +90,10 @@
 
 
 def backward_kernel(
-    qk0_ref, qk1_ref, v_ref, do_ref, bias_ref, start_ref, lse_ref,
-    dqk0_ref, dqk1_ref, dv_ref, table_ref, dk_acc, dv_acc,
+    blocks_ref, do_ref, bias_ref, start_ref, lse_ref, grads_ref, table_ref,
+    qk0_ref, qk1_ref, v_ref, dqk0_ref, dqk1_ref, dv_ref, dk_acc, dv_acc,
 ):
+    split_blocks(blocks_ref, (qk0_ref, qk1_ref, v_ref))
     table_ref[...] = jnp.zeros_like(table_ref)
     for m, (qk_ref, dqk_ref) in enumerate(((qk0_ref, dqk0_ref), (qk1_ref, dqk1_ref))):
         lanes = slice(m * HEAD_DIM, (m + 1) * HEAD_DIM)
@@ -104,45 +115,165 @@
             inner = jnp.sum(weighted, axis=-1, keepdims=True)
             grad_scores = (weighted - probs * inner).astype(bf16)
             table_ref[:, GROUP - width :] += grad_scores.astype(f32)
-            dqk_ref[rows, :HEAD_DIM] = (dot(grad_scores, keys[:width]) * SCALE).astype(bf16)
+            dqk_ref[rows, :HEAD_DIM] = dot(grad_scores, keys[:width]) * SCALE
             dk_acc[:width] += dot_outer(grad_scores, query)
             dv_acc[:width] += dot_outer(probs.astype(bf16), grad_o)
-        dqk_ref[:, HEAD_DIM:] = dk_acc[...].astype(bf16)
-        dv_ref[:, lanes] = dv_acc[...].astype(bf16)
-
-
-LIMIT = pltpu.CompilerParams(vmem_limit_bytes=48 * 1024 * 1024)
-
-
-def head_forward(qk0, qk1, v, bias, start):
+        dqk_ref[:, HEAD_DIM:] = dk_acc[...]
+        dv_ref[:, lanes] = dv_acc[...]
+    parts = [r[...].reshape(SLOTS, TOK, 2 * HEAD_DIM) for r in (dqk0_ref, dqk1_ref, dv_ref)]
+    grads_ref[...] = jnp.concatenate(parts, axis=1).astype(bf16)
+
+
+def swap(values):
+    return pltpu.roll(values, HEAD_DIM, 1)
+
+
+def low_half(rows):
+    return lax.broadcasted_iota(jnp.int32, (rows, 2 * HEAD_DIM), 1) < HEAD_DIM
+
+
+def interleave(first, second):
+    low = low_half(first.shape[0])
+    return jnp.where(low, first, swap(second)), jnp.where(low, swap(first), second)
+
+
+def pair_lanes(pair, offset=0):
+    return slice(offset + pair * 2 * HEAD_DIM, offset + (pair + 1) * 2 * HEAD_DIM)
+
+
+def pack_qkv_kernel(qkv_ref, out_ref):
+    for pair in range(HEADS // 2):
+        q = qkv_ref[:, pair_lanes(pair)] * SCALE
+        k = qkv_ref[:, pair_lanes(pair, WIDTH)]
+        v = qkv_ref[:, pair_lanes(pair, 2 * WIDTH)]
+        heads = interleave(q, k)
+        values = interleave(v[:TOK], v[TOK:])
+        for j in range(2):
+            out_ref[2 * pair + j] = jnp.concatenate([heads[j], values[j]], axis=0).astype(bf16)
+    for slot in range(HEADS, SLOTS):
+        out_ref[slot] = jnp.zeros_like(out_ref[slot])
+
+
+def unpack_qkv_kernel(in_ref, out_ref):
+    for pair in range(HEADS // 2):
+        even, odd = in_ref[2 * pair].astype(f32), in_ref[2 * pair + 1].astype(f32)
+        q, k = interleave(even[:ROWS], odd[:ROWS])
+        v = jnp.concatenate(interleave(even[ROWS:], odd[ROWS:]), axis=0)
+        for j, value in enumerate((q, k, v)):
+            out_ref[:, pair_lanes(pair, j * WIDTH)] = value.astype(bf16)
+
+
+def pack_one_kernel(in_ref, out_ref):
+    for pair in range(HEADS // 2):
+        values = in_ref[:, pair_lanes(pair)]
+        for j, value in enumerate(interleave(values[:TOK], values[TOK:])):
+            out_ref[2 * pair + j] = value.astype(bf16)
+    for slot in range(HEADS, SLOTS):
+        out_ref[slot] = jnp.zeros_like(out_ref[slot])
+
+
+def unpack_one_kernel(in_ref, out_ref):
+    for pair in range(HEADS // 2):
+        even, odd = in_ref[2 * pair].astype(f32), in_ref[2 * pair + 1].astype(f32)
+        values = jnp.concatenate(interleave(even, odd), axis=0)
+        out_ref[:, pair_lanes(pair)] = values.astype(bf16)
+
+
+def repack(kernel, shape, values):
+    return pl.pallas_call(
+        kernel,
+        out_shape=jax.ShapeDtypeStruct(shape, bf16),
+        compiler_params=LIMIT,
+        cost_estimate=pl.CostEstimate(flops=1000000, bytes_accessed=1500000, transcendentals=0),
+    )(values)
+
+
+def products_kernel(
+    a_qkv, b_q, b_k, b_v, a_out, b_out, a_in, b_in0, b_in1, b_in2, b_in3, a_zero, b_zero, a_second, b_second,
+    a_rows, b_due0, b_due1, b_due2, b_due3, a_hidden, b_rows, out_ref,
+):
+    def rows(a, b, count):
+        return dot_outer(a[...], b[...]).reshape(SLOTS, count, -1)
+
+    def put(first, parts):
+        value = jnp.concatenate(parts, axis=1).astype(bf16)
+        out_ref[:, first : first + value.shape[1]] = value
+
+    put(0, [rows(a_qkv, b, 24) for b in (b_q, b_k, b_v)] + [rows(a_out, b_out, 24)])
+    put(96, [rows(a_in, b, 24) for b in (b_in0, b_in1, b_in2, b_in3)])
+    zero = rows(a_zero, b_zero, 24)
+    put(192, [zero, jnp.zeros_like(zero[:, :8])])
+    second = dot_outer(a_second[...], b_second[...]).reshape(12, SLOTS, 8, -1)
+    put(224, [second[j] for j in range(12)])
+    put(320, [rows(a_rows, b, 48) for b in (b_due0, b_due1, b_due2, b_due3)])
+    put(512, [rows(a_hidden, b_rows, 192)])
+
+
+def products(qkv, out, dense_in, zero, second, expert_in, expert_out):
+    step = 256
+    operands, specs = [], []
+
+    def whole(a):
+        operands.append(a)
+        specs.append(pl.BlockSpec(a.shape, lambda n: (0, 0)))
+
+    def columns(b, count):
+        for j in range(count):
+            operands.append(b)
+            specs.append(pl.BlockSpec((b.shape[0], step), lambda n, j=j: (0, n + j * (WIDTH // step))))
+
+    for (a, b), count in zip((qkv, out, dense_in, zero, second, expert_in, expert_out), (3, 1, 4, 1, 1, 4, 1)):
+        whole(a)
+        columns(b, count)
+    return pl.pallas_call(
+        products_kernel,
+        grid=(WIDTH // step,),
+        in_specs=specs,
+        out_specs=pl.BlockSpec((SLOTS, 704, step), lambda n: (0, 0, n)),
+        out_shape=jax.ShapeDtypeStruct((SLOTS, 704, WIDTH), bf16),
+        compiler_params=LIMIT,
+        cost_estimate=pl.CostEstimate(flops=5200000000, bytes_accessed=30000000, transcendentals=0),
+    )(*operands)
+
+
+def staging(dtype, count):
+    return [pltpu.VMEM((GROUP, 2 * HEAD_DIM), dtype)] * count
+
+
+def head_forward(blocks, bias, start):
     return pl.pallas_call(
         forward_kernel,
         out_shape=(
             jax.ShapeDtypeStruct((GROUP, 2 * HEAD_DIM), bf16),
             jax.ShapeDtypeStruct((GROUP, MICRO), f32),
         ),
+        scratch_shapes=staging(bf16, 3),
         compiler_params=LIMIT,
         cost_estimate=pl.CostEstimate(
             flops=4 * MICRO * GROUP * GROUP * HEAD_DIM // 2,
             bytes_accessed=6 * GROUP * 256,
             transcendentals=MICRO * GROUP * GROUP // 2,
         ),
-    )(qk0, qk1, v, bias, start)
-
-
-def head_backward(qk0, qk1, v, grad_o, bias, start, lse):
-    shape = jax.ShapeDtypeStruct((GROUP, 2 * HEAD_DIM), bf16)
+    )(blocks, bias, start)
+
+
+def head_backward(blocks, grad_o, bias, start, lse):
     return pl.pallas_call(
         backward_kernel,
-        out_shape=(shape, shape, shape, jax.ShapeDtypeStruct((BLOCK, GROUP), f32)),
-        scratch_shapes=[pltpu.VMEM((GROUP, HEAD_DIM), f32), pltpu.VMEM((GROUP, HEAD_DIM), f32)],
+        out_shape=(
+            jax.ShapeDtypeStruct((SLOTS, 3 * TOK, 2 * HEAD_DIM), bf16),
+            jax.ShapeDtypeStruct((BLOCK, GROUP), f32),
+        ),
+        scratch_shapes=staging(bf16, 3)
+        + staging(f32, 3)
+        + [pltpu.VMEM((GROUP, HEAD_DIM), f32), pltpu.VMEM((GROUP, HEAD_DIM), f32)],
         compiler_params=LIMIT,
         cost_estimate=pl.CostEstimate(
             flops=10 * MICRO * GROUP * GROUP * HEAD_DIM // 2,
             bytes_accessed=12 * GROUP * 256,
             transcendentals=MICRO * GROUP * GROUP // 2,
         ),
-    )(qk0, qk1, v, grad_o, bias, start, lse)
+    )(blocks, grad_o, bias, start, lse)
 
 
 def tile_distance():
@@ -175,37 +306,6 @@
     return lax.all_to_all(blocks, axes, split_axis=0, concat_axis=0, tiled=True)
 
 
-def pad_heads(blocks):
-    return jnp.pad(blocks, ((0, SLOTS - HEADS), (0, 0), (0, 0)))
-
-
-def by_head_single(values):
-    parts = values.reshape(MICRO, TOK, HEADS, HEAD_DIM).transpose(2, 1, 0, 3)
-    return parts.reshape(HEADS, TOK, MICRO * HEAD_DIM)
-
-
-def from_head_single(blocks):
-    parts = blocks.reshape(HEADS, TOK, MICRO, HEAD_DIM).transpose(2, 1, 0, 3)
-    return parts.reshape(ROWS, WIDTH)
-
-
-def send_heads(q, k, v):
-    pair = jnp.stack([q.reshape(ROWS, HEADS, HEAD_DIM), k.reshape(ROWS, HEADS, HEAD_DIM)], axis=2)
-    pair = pair.reshape(ROWS, HEADS, 2 * HEAD_DIM).transpose(1, 0, 2)
-    blocks = exchange(pad_heads(jnp.concatenate([pair, by_head_single(v)], axis=1)), LINE)
-    return tuple(
-        blocks[:, j * TOK : (j + 1) * TOK].reshape(GROUP, 2 * HEAD_DIM) for j in range(3)
-    )
-
-
-def return_heads(dqk0, dqk1, dv):
-    blocks = jnp.concatenate([a.reshape(SLOTS, TOK, 2 * HEAD_DIM) for a in (dqk0, dqk1, dv)], axis=1)
-    blocks = exchange(blocks, LINE)[:HEADS]
-    pair = blocks[:, :ROWS].reshape(HEADS, ROWS, 2, HEAD_DIM).transpose(2, 1, 0, 3)
-    pair = pair.reshape(2, ROWS, WIDTH)
-    return pair[0], pair[1], from_head_single(blocks[:, ROWS:])
-
-
 def spread_matrix():
     out = lax.broadcasted_iota(jnp.int32, (WIDTH, 1024), 1)
     source = lax.broadcasted_iota(jnp.int32, (WIDTH, 1024), 0)
@@ -220,26 +320,26 @@
     return dot_back(values.astype(bf16), places)
 
 
+HEAD_SHAPE = (SLOTS, 3 * TOK, 2 * HEAD_DIM)
+ONE_SHAPE = (SLOTS, TOK, 2 * HEAD_DIM)
+
+
 def attend_forward(x, scales, w_qkv, w_out, places, bias, start):
     normed, inv = normalize(x, scales)
-    qkv = dot(spread(normed, places), w_qkv)
-    q = (qkv[:, :WIDTH] * SCALE).astype(bf16)
-    k = qkv[:, WIDTH : 2 * WIDTH].astype(bf16)
-    v = qkv[:, 2 * WIDTH :].astype(bf16)
-    qk0, qk1, vv = send_heads(q, k, v)
-    o, lse = head_forward(qk0, qk1, vv, bias, start)
-    attended = from_head_single(exchange(o.reshape(SLOTS, TOK, 2 * HEAD_DIM), LINE)[:HEADS])
+    blocks = exchange(repack(pack_qkv_kernel, HEAD_SHAPE, dot(spread(normed, places), w_qkv)), LINE)
+    o, lse = head_forward(blocks, bias, start)
+    attended = repack(unpack_one_kernel, (ROWS, WIDTH), exchange(o.reshape(ONE_SHAPE), LINE))
     x = x + dot(spread(attended, places), w_out)
-    return x, (normed, inv, qk0, qk1, vv, lse, attended)
+    return x, (normed, inv, blocks, lse, attended)
 
 
 def attend_backward(grad, x, scales, w_qkv, w_out, places, bias, start, saved):
-    normed, inv, qk0, qk1, vv, lse, attended = saved
+    normed, inv, blocks, lse, attended = saved
     branch = grad.astype(bf16)
-    grad_attended = gather_back(dot_back(branch, w_out), places).astype(bf16)
-    grad_o = exchange(pad_heads(by_head_single(grad_attended)), LINE).reshape(GROUP, 2 * HEAD_DIM)
-    dqk0, dqk1, dv, tile = head_backward(qk0, qk1, vv, grad_o, bias, start, lse)
-    heads = jnp.concatenate(return_heads(dqk0, dqk1, dv), axis=1)
+    grad_attended = gather_back(dot_back(branch, w_out), places)
+    grad_o = exchange(repack(pack_one_kernel, ONE_SHAPE, grad_attended), LINE)
+    grad_heads, tile = head_backward(blocks, grad_o.reshape(GROUP, 2 * HEAD_DIM), bias, start, lse)
+    heads = repack(unpack_qkv_kernel, (ROWS, 3 * WIDTH), exchange(grad_heads, LINE))
     grad_normed = gather_back(dot_back(heads, w_qkv), places)
     grad_x, grad_scales = normalize_back(grad_normed, x, inv, scales)
     return grad + grad_x, grad_scales, branch, heads, tile
@@ -274,17 +374,15 @@
         jnp.concatenate([qkv_weights[l, 0], qkv_weights[l, 1], qkv_weights[l, 2], out_weights[l]], axis=1)
         for l in range(2)
     ]
-    first_pack = jnp.pad(jnp.concatenate([attention[0], ffn_in_units], axis=1), ((0, 2), (0, 0)))
-    first_pack = jnp.concatenate([first_pack, ffn_out[:8], ffn_out[8:16], ffn_out[16:]], axis=1)
-    second_pack = jnp.pad(attention[1], ((0, 2), (0, 0)))
-    first = lax.all_gather(first_pack, ALL, axis=0, tiled=True)
-    second = lax.all_gather(second_pack, ALL, axis=0, tiled=True)
+    pack = jnp.pad(jnp.concatenate(attention + [ffn_in_units], axis=1), ((0, 2), (0, 0)))
+    pack = jnp.concatenate([pack, ffn_out[:8], ffn_out[8:16], ffn_out[16:]], axis=1)
+    shared = lax.all_gather(pack, ALL, axis=0, tiled=True)
     w_expert_in = lax.all_gather(expert_in[0], LINE, axis=0, tiled=True)
     w_expert_out = lax.all_gather(expert_out[0], LINE, axis=0, tiled=True)
-    qkv_zero, out_zero = first[:, : 3 * WIDTH], first[:, 3 * WIDTH : 4 * WIDTH]
-    qkv_one, out_one = second[:, : 3 * WIDTH], second[:, 3 * WIDTH :]
-    w_in = first[:, 4 * WIDTH : 8 * WIDTH]
-    w_out = [first[:, (8 + g) * WIDTH : (9 + g) * WIDTH] for g in range(3)]
+    qkv_zero, out_zero = shared[:, : 3 * WIDTH], shared[:, 3 * WIDTH : 4 * WIDTH]
+    qkv_one, out_one = shared[:, 4 * WIDTH : 7 * WIDTH], shared[:, 7 * WIDTH : 8 * WIDTH]
+    w_in = shared[:, 8 * WIDTH : 12 * WIDTH]
+    w_out = [shared[:, (12 + g) * WIDTH : (13 + g) * WIDTH] for g in range(3)]
 
     small = jnp.concatenate([norm_gains.reshape(24), router.reshape(48), rel_table])
     small = jnp.pad(small, (0, 128 - 75))[None, None, :]
@@ -346,11 +444,6 @@
     picked = [collected[ROWS : 2 * ROWS], collected[2 * ROWS :]]
     hidden_out = x3 + gates[:, :1] * picked[0] + gates[:, 1:] * picked[1]
 
-    expert_parts = [
-        dot_outer(expert_rows, due[:, j * WIDTH : (j + 1) * WIDTH]).astype(bf16).reshape(SLOTS, 48, WIDTH)
-        for j in range(4)
-    ] + [dot_outer(he, grad_rows).astype(bf16).reshape(SLOTS, 192, WIDTH)]
-
     dgates = jnp.stack([jnp.sum(grad_four * p, axis=-1) for p in picked], axis=1)
     dchosen = gates * (dgates - jnp.sum(gates * dgates, axis=-1, keepdims=True))
     dlogits = jnp.sum(marks * dchosen[:, :, None], axis=1)
@@ -378,8 +471,8 @@
     grad_two, gain_three, branch_three, heads_three, tile_three = attend_backward(
         grad_three, x2, gains[2], qkv_one, out_one, places, bias[1], start, saved_three
     )
-    parts = chunks(*share(saved_three[0], heads_three, True), SLOTS)
-    parts += chunks(*share(saved_three[6], branch_three, True), SLOTS)
+    pair_qkv = share(saved_three[0], heads_three, True)
+    pair_out = share(saved_three[4], branch_three, True)
 
     branch_two = grad_two.astype(bf16)
     grad_h = jnp.concatenate([dot_back(branch_two, w) for w in w_out], axis=1)
@@ -388,22 +481,21 @@
     grad_c = gather_back(dot_back(du, w_in), places)
     grad_x, gain_two = normalize_back(grad_c, x1, inv_c, gains[1])
     grad_one = grad_two + grad_x
-    parts += chunks(*share(c, du, True), SLOTS)
-    parts += chunks(*share(saved_one[6], grad_one.astype(bf16), True), SLOTS)
+    pair_in = share(c, du, True)
+    pair_zero = share(saved_one[4], grad_one.astype(bf16), True)
     halves = h.reshape(ROWS, 12, 2, BLOCK)
     mine = lax.dynamic_index_in_dim(halves, core, axis=2, keepdims=False).reshape(ROWS, FF // 2)
     theirs = lax.dynamic_index_in_dim(halves, 1 - core, axis=2, keepdims=False).reshape(ROWS, FF // 2)
     got = other_core(jnp.concatenate([theirs, branch_two], axis=1))
     mine = jnp.concatenate([mine, got[:, : FF // 2]], axis=0)
-    second_grad = dot_outer(mine, jnp.concatenate([branch_two, got[:, FF // 2 :]], axis=0))
-    second_grad = second_grad.astype(bf16).reshape(12, SLOTS, 8, WIDTH).transpose(1, 0, 2, 3)
-    parts.append(second_grad.reshape(SLOTS, 96, WIDTH))
+    pair_second = (mine, jnp.concatenate([branch_two, got[:, FF // 2 :]], axis=0))
+    summed = products(
+        pair_qkv, pair_out, pair_in, pair_zero, pair_second, (expert_rows, due), (he, grad_rows)
+    )
     early_sum = lax.optimization_barrier(
-        lax.psum_scatter(
-            jnp.concatenate(parts + expert_parts, axis=1), LINE, scatter_dimension=0, tiled=False
-        )
+        lax.psum_scatter(summed, LINE, scatter_dimension=0, tiled=False)
     )
-    expert_sum = early_sum[312:]
+    expert_sum = early_sum[320:]
 
     grad_zero, gain_one, branch_one, heads_one, tile_one = attend_backward(
         grad_one, x0, gains[0], qkv_zero, out_zero, places, bias[0], start, saved_one
@@ -426,7 +518,7 @@
     tiny = late_sum[18, :75]
 
     early_rows = early_sum[:216].reshape(9, 4, 6, WIDTH).transpose(1, 0, 2, 3).reshape(4, 54, WIDTH)
-    ffn_out_rows = early_sum[216:312].reshape(3, 4, 8, WIDTH).transpose(1, 0, 2, 3).reshape(4, 24, WIDTH)
+    ffn_out_rows = early_sum[224:320].reshape(3, 4, 8, WIDTH).transpose(1, 0, 2, 3).reshape(4, 24, WIDTH)
     last = jnp.concatenate([ffn_out_rows, early_rows], axis=1)
     last = exchange(jnp.pad(last, ((0, 0), (0, 2), (0, 0))), ("z",))
     last = jnp.sum(last.astype(f32), axis=0)

time: 648 us -> 587 us (0.906)
  local copies, waits for them, and re-layouts: 132 us -> 47.5 us
  waiting for transfers between devices: 197 us -> 242 us
  matrix products: 129 us -> 96.4 us
  Pallas kernels: 34.8 us -> 56.7 us
  other arithmetic: 56.9 us -> 49.7 us
    dot_general x20 -> x5, matrix products: 33.3 us -> 6.88 us  [dot_outer(): lax.dot_general(a, b, (((0,), (0,)), ((), ())), preferred_element_type=f32)]
    pallas_call x2 -> x11, Pallas kernels: 18.5 us -> 40.3 us  [the longest x2 20.8 us: head_backward(): pl.pallas_call(backward_kernel, out_shape=(jax.ShapeDtypeStruct((SLOTS, 3...]
    unnamed x6 -> x5, waiting for transfers between devices: 1.25 us -> 22.2 us
    slice x23 -> x3, local copies, waits for them, and re-layouts: 22.5 us -> 1.99 us  [the longest x1 0.92 us: on_device(): early_sum[224:320].reshape(3, 4, 8, WIDTH).transpose(1, 0, 2, 3)]
    reshape x23 -> x1, local copies, waits for them, and re-layouts: 19.2 us -> 0.06 us  [on_device(): early_sum[224:320].reshape(3, 4, 8, WIDTH).transpose(1, 0, 2, 3)]
    unnamed x319 -> x305, local copies, waits for them, and re-layouts: 29.9 us -> 12.4 us
    all_to_all x14, waiting for transfers between devices: 141 us -> 153 us  [exchange(): return lax.all_to_all(blocks, axes, split_axis=0, concat_axis=0, tiled=True)]
    all_gather x2 -> x1, waiting for transfers between devices: 52.4 us -> 62.8 us  [on_device(): shared = lax.all_gather(pack, ALL, axis=0, tiled=True)]
  transfers between devices with their start and end apart: 26 -> 25, of which waited for: 16 -> 21; matrix products, arithmetic and copies ran while one was open for 31% -> 22% of each run, Pallas kernels for 4% -> 5%
where the time goes in v3:
time: 587 us; the launch traced here: 576 us
  waiting for transfers between devices  242 us (41%)
  matrix products  96.4 us (16%)
  starting transfers between devices  67.6 us (12%)
  Pallas kernels  56.7 us (10%)
  other arithmetic  49.7 us (8%)
  local copies, waits for them, and re-layouts  47.5 us (8%)
  between operations  16.6 us (3%)
    all_to_all x14, waiting for transfers between devices, exchange(): return lax.all_to_all(blocks, axes, split_axis=0, concat_axis=0, tiled=True)  153 us
    all_to_all x14, starting transfers between devices, exchange(): return lax.all_to_all(blocks, axes, split_axis=0, concat_axis=0, tiled=True)  65.9 us
    all_gather x1, waiting for transfers between devices, on_device(): shared = lax.all_gather(pack, ALL, axis=0, tiled=True)  62.8 us
    dot_general x22, matrix products, dot(): lax.dot_general(a, b, (((1,), (0,)), ((), ())), preferred_element_type=f32)  48.1 us
    dot_general x11, matrix products, dot_back(): lax.dot_general(a, b, (((1,), (1,)), ((), ())), preferred_element_type=f32)  41.4 us
    unnamed x5, waiting for transfers between devices  22.2 us
    pallas_call x2, Pallas kernels, head_backward(): pl.pallas_call(backward_kernel, out_shape=(jax.ShapeDtypeStruct((SLOTS, 3...  20.8 us
    select_n x2, other arithmetic, bias_tile(): result = jnp.where(distance >= first, entries[b], result)  20.4 us
  transfers between devices with their start and end apart: 25, of which 21 were waited for; matrix products, arithmetic and copies ran while one was open for 22% of the time, Pallas kernels for 5%

profile of v3, /device:TPU:0, one launch (start us, length us, event | category | flops | bytes accessed | tf_op | source)
XLA Modules:
  0.0 576.0 jit_solution(17684947798821811185)
XLA Ops:
  14.0 7.1 %all-to-all-start = ((bf16[16,8,128]{2,1,0:T(8,128)(2,1)}), bf16[16,8,128]{2,1,0:T(8,128)(2,1)S(1)}, u32[]{:S(2)}, u32[]{:S(2)}) async-start(bf16[16,8,128]{2,1,0:T(8,128)(2,1)} %broadcast_in_dim.172), calls=%async_computation | async-start | bytes 65536 | tf_op jit(solution)/shard_map/all_to_all | solution.py:306
  29.5 5.3 all-to-all-start.1
  35.2 7.3 %all-to-all-done.1 = bf16[8,128,128]{2,1,0:T(8,128)(2,1)S(1)} async-done(((bf16[8,128,128]{2,1,0:T(8,128)(2,1)}), bf16[8,128,128]{2,1,0:T(8,128)(2,1)S(1)}, u32[]{:S(2)}, u32[]{:S(2)}) %all-to-all-start.1) | async-done | bytes 262176 | tf_op jit(solution)/shard_map/all_to_all | solution.py:306
  43.1 62.8 %all-gather.6.cloned.1.call-done = bf16[1024,11520]{1,0:T(8,128)(2,1)} async-done(((bf16[8,11520]{1,0:T(8,128)(2,1)}), bf16[1024,11520]{1,0:T(8,128)(2,1)}) %all-gather.6.cloned.1.call-update) | async-done | bytes 23592976 | tf_op jit(solution)/shard_map/all_gather | solution.py:379
  111.2 6.9 %all-to-all-start.2 = ((bf16[16,216,128]{2,1,0:T(8,128)(2,1)}), bf16[16,216,128]{2,1,0:T(8,128)(2,1)S(1)}, u32[]{:S(2)}, u32[]{:S(2)}) async-start(bf16[16,216,128]{2,1,0:T(8,128)(2,1)} %shard_map.248), calls=%async_computation.2 | async-start | bytes 1769472 | tf_op jit(solution)/shard_map/all_to_all | solution.py:306
  119.3 10.1 %select_select_fusion.2.bias_ref = f32[128,1152]{1,0:T(8,128)S(1)} fusion(f32[]{:T(128)} %bitcast.28, f32[]{:T(128)} %bitcast.27, f32[]{:T(128)} %bitcast.26, f32[]{:T(128)} %bitcast.25, f32[]{:T(128)} %bitcast.24, f32[]{:T(128)} %bitcast.23, f32[]{:T(128)} %bitcast.22, f32[]{:T(128)} %bitcast.21, f32[]{:T(128)} %bitcast.20, f32[]{:T(128)} %bitcast.19, ...), kind=kLoop, calls=%fused_computation.192 | loop fusion | flops 5013504 | bytes 589888 | tf_op jit(solution)/shard_map/jit(_where)/select_n | solution.py:293
  129.4 8.6 %all-to-all-done.2.blocks_ref = bf16[16,216,128]{2,1,0:T(8,128)(2,1)S(1)} async-done(((bf16[16,216,128]{2,1,0:T(8,128)(2,1)}), bf16[16,216,128]{2,1,0:T(8,128)(2,1)S(1)}, u32[]{:S(2)}, u32[]{:S(2)}) %all-to-all-start.2) | async-done | bytes 884768 | tf_op jit(solution)/shard_map/all_to_all | solution.py:306
  138.1 8.2 %shard_map.249 = (bf16[1152,128]{1,0:T(8,128)(2,1)}, f32[1152,2]{1,0:T(8,128)S(1)}) custom-call(bf16[16,216,128]{2,1,0:T(8,128)(2,1)S(1)} %all-to-all-done.2.blocks_ref, f32[128,1152]{1,0:T(8,128)S(1)} %select_select_fusion.2.bias_ref, s32[1152,2]{1,0:T(8,128)S(1)} %copy.232.start_ref), custom_call_target="tpu_custom_call" | custom-call | flops 339738624 | bytes 1769472 | tf_op jit(solution)/shard_map/pallas_call | solution.py:244
  151.5 11.7 %all-to-all-done.3.in_ref = bf16[16,72,128]{2,1,0:T(8,128)(2,1)S(1)} async-done(((bf16[16,72,128]{2,1,0:T(8,128)(2,1)}), bf16[16,72,128]{2,1,0:T(8,128)(2,1)S(1)}, u32[]{:S(2)}, u32[]{:S(2)}) %all-to-all-start.3) | async-done | bytes 294944 | tf_op jit(solution)/shard_map/all_to_all | solution.py:306
  166.9 6.3 %multiply_convert_fusion.1 = (bf16[144,3072]{1,0:T(8,128)(2,1)S(1)}, f32[144,3072]{1,0:T(8,128)}) fusion(bf16[1024,11520]{1,0:T(8,128)(2,1)} %all-gather.6.cloned.1.call-done, bf16[144,768]{1,0:T(8,128)(2,1)S(1)} %multiply_convert_fusion.4, s32[1024]{0:T(1024)S(1)} %get-tuple-element.218, s32[1024]{0:T(1024)S(1)} %get-tuple-element.221, ...), kind=kOutput, calls=%fused_computation.60 | convolution fusion | flops 1142095872 | bytes 9185280 | tf_op jit(solution)/shard_map/dot_general | solution.py:34
  193.2 10.3 %select_select_fusion.1.bias_ref = f32[128,1152]{1,0:T(8,128)S(1)} fusion(f32[]{:T(128)} %bitcast.46, f32[]{:T(128)} %bitcast.45, f32[]{:T(128)} %bitcast.44, f32[]{:T(128)} %bitcast.43, f32[]{:T(128)} %bitcast.42, f32[]{:T(128)} %bitcast.41, f32[]{:T(128)} %bitcast.40, f32[]{:T(128)} %bitcast.39, f32[]{:T(128)} %bitcast.38, f32[]{:T(128)} %bitcast.37, ...), kind=kLoop, calls=%fused_computation.191 | loop fusion | flops 5013504 | bytes 589888 | tf_op jit(solution)/shard_map/jit(_where)/select_n | solution.py:293
  206.3 8.2 %shard_map.252 = (bf16[1152,128]{1,0:T(8,128)(2,1)}, f32[1152,2]{1,0:T(8,128)S(1)}) custom-call(bf16[16,216,128]{2,1,0:T(8,128)(2,1)S(1)} %all-to-all-done.4.blocks_ref, f32[128,1152]{1,0:T(8,128)S(1)} %select_select_fusion.1.bias_ref, s32[1152,2]{1,0:T(8,128)S(1)} %copy.232.start_ref), custom_call_target="tpu_custom_call" | custom-call | flops 339738624 | bytes 1769472 | tf_op jit(solution)/shard_map/pallas_call | solution.py:244
  221.1 10.4 %all-to-all-done.5.in_ref = bf16[16,72,128]{2,1,0:T(8,128)(2,1)S(1)} async-done(((bf16[16,72,128]{2,1,0:T(8,128)(2,1)}), bf16[16,72,128]{2,1,0:T(8,128)(2,1)S(1)}, u32[]{:S(2)}, u32[]{:S(2)}) %all-to-all-start.5) | async-done | bytes 294944 | tf_op jit(solution)/shard_map/all_to_all | solution.py:306
  238.3 4.6 all-to-all-start.6
  247.7 10.4 %all-to-all-done.6 = bf16[8,80,768]{2,1,0:T(8,128)(2,1)} async-done(((bf16[8,80,768]{2,1,0:T(8,128)(2,1)}), bf16[8,80,768]{2,1,0:T(8,128)(2,1)}, u32[]{:S(2)}, u32[]{:S(2)}) %all-to-all-start.6) | async-done | bytes 983072 | tf_op jit(solution)/shard_map/all_to_all | solution.py:306
  259.4 7.3 %multiply_convert_fusion = (bf16[320,3072]{1,0:T(8,128)(2,1)}, f32[320,3072]{1,0:T(8,128)}) fusion(bf16[320,768]{1,0:T(8,128)(2,1)S(1)} %bitcast.223, bf16[1,768,3072]{2,1,0:T(8,128)(2,1)} %all-gather.8.cloned.1.call-done), kind=kOutput, calls=%fused_computation.37 | convolution fusion | flops 1518796800 | bytes 11108352 | tf_op jit(solution)/shard_map/dot_general | solution.py:34
  266.7 7.5 %fusion.27.b_due0.b_due1.b_due2.b_due3 = bf16[320,3072]{1,0:T(8,128)(2,1)S(1)} fusion(f32[320,3072]{1,0:T(8,128)} %get-tuple-element.209, bf16[320,768]{1,0:T(8,128)(2,1)S(1)} %bitcast.221, bf16[1,3072,768]{2,1,0:T(8,128)(2,1)} %all-gather.10.cloned.1.call-done), kind=kOutput, calls=%fused_computation.36 | convolution fusion | flops 1529610240 | bytes 11108352 | tf_op jit(solution)/shard_map/dot_general | solution.py:38
  285.1 6.8 %dynamic-slice_reduce_fusion.1 = (bf16[144,12,128]{2,1,0:T(8,128)(2,1)S(1)}, bf16[144,12,128]{2,1,0:T(8,128)(2,1)S(1)}) fusion(bf16[144,12,2,128]{3,2,1,0:T(2,128)(2,1)} %reshape.502, s32[]{:T(128)S(6)} %select_n.328, s32[]{:T(128)S(6)} %select_n.329), kind=kLoop, calls=%fused_computation.167 | loop fusion | bytes 1769480 | tf_op jit(solution)/shard_map/jit(dynamic_index_in_dim)/dynamic_slice | solution.py:487
  315.9 8.6 %all-to-all-done.8 = bf16[16,72,128]{2,1,0:T(8,128)(2,1)S(1)} async-done(((bf16[16,72,128]{2,1,0:T(8,128)(2,1)}), bf16[16,72,128]{2,1,0:T(8,128)(2,1)S(1)}, u32[]{:S(2)}, u32[]{:S(2)}) %all-to-all-start.8) | async-done | bytes 294944 | tf_op jit(solution)/shard_map/all_to_all | solution.py:306
  326.6 10.4 %shard_map.255 = (bf16[16,216,128]{2,1,0:T(8,128)(2,1)}, f32[128,1152]{1,0:T(8,128)S(1)}) custom-call(bf16[16,216,128]{2,1,0:T(8,128)(2,1)S(1)} %all-to-all-done.4.blocks_ref, bf16[1152,128]{1,0:T(8,128)(2,1)S(1)} %bitcast.226, f32[128,1152]{1,0:T(8,128)S(1)} %copy-done.7, s32[1152,2]{1,0:T(8,128)S(1)} %copy.232.start_ref, f32[1152,2]{1,0:T(8,128)S(1)} %copy-done.16), custom_call_target="tpu_custom_call" | custom-call | flops 849346560 | bytes 3538944 | tf_op jit(solution)/shard_map/pallas_call | solution.py:261
  343.8 12.5 %all-to-all-done.9.in_ref = bf16[16,216,128]{2,1,0:T(8,128)(2,1)S(1)} async-done(((bf16[16,216,128]{2,1,0:T(8,128)(2,1)}), bf16[16,216,128]{2,1,0:T(8,128)(2,1)S(1)}, u32[]{:S(2)}, u32[]{:S(2)}) %all-to-all-start.9) | async-done | bytes 884768 | tf_op jit(solution)/shard_map/all_to_all | solution.py:306
  356.6 6.2 %multiply_reduce_fusion.1 = (f32[768]{0:T(1024)}, f32[144]{0:T(256)S(1)}, f32[144,768]{1,0:T(8,128)}) fusion(f32[144,768]{1,0:T(8,128)} %get-tuple-element.205, f32[144]{0:T(256)S(1)} %copy-done.69, f32[768]{0:T(1024)S(1)} %mul.600, s32[1024]{0:T(1024)S(1)} %copy-done.78, s32[1024]{0:T(1024)S(1)} %copy-done.93, s32[1024]{0:T(1024)S(1)} %copy-done.83, ...), kind=kOutput, calls=%fused_computation.227 | convolution fusion | flops 912284800 | bytes 6292608 | tf_op jit(solution)/shard_map/dot_general | solution.py:38
  373.5 6.8 %multiply_reduce_fusion.2 = (f32[768]{0:T(1024)S(1)}, f32[144]{0:T(256)S(1)}, f32[144,768]{1,0:T(8,128)}) fusion(f32[144,768]{1,0:T(8,128)S(1)} %copy-done.22, f32[144]{0:T(256)S(1)} %copy-done.67, f32[768]{0:T(1024)S(1)} %mul.590, s32[1024]{0:T(1024)S(1)} %copy-done.78, s32[1024]{0:T(1024)S(1)} %copy-done.93, s32[1024]{0:T(1024)S(1)} %copy-done.83, ...), kind=kOutput, calls=%fused_computation.228 | convolution fusion | flops 1138777216 | bytes 8086656 | tf_op jit(solution)/shard_map/dot_general | solution.py:38
  388.0 14.7 %shard_map.260 = bf16[16,704,768]{2,1,0:T(8,128)(2,1)} custom-call(bf16[288,384]{1,0:T(8,128)(2,1)S(1)} %pad_maximum_fusion.18.a_qkv, bf16[288,2304]{1,0:T(8,128)(2,1)S(1)} %pad_maximum_fusion.2.b_q.b_k.b_v, bf16[288,2304]{1,0:T(8,128)(2,1)S(1)} %pad_maximum_fusion.2.b_q.b_k.b_v, bf16[288,2304]{1,0:T(8,128)(2,1)S(1)} %pad_maximum_fusion.2.b_q.b_k.b_v, ...), custom_call_target="tpu_custom_call" | custom-call | flops 5200000000 | bytes 30000000 | tf_op jit(solution)/shard_map/pallas_call | solution.py:228
  416.1 8.6 %all-to-all-done.10 = bf16[16,72,128]{2,1,0:T(8,128)(2,1)S(1)} async-done(((bf16[16,72,128]{2,1,0:T(8,128)(2,1)}), bf16[16,72,128]{2,1,0:T(8,128)(2,1)S(1)}, u32[]{:S(2)}, u32[]{:S(2)}) %all-to-all-start.10) | async-done | bytes 294944 | tf_op jit(solution)/shard_map/all_to_all | solution.py:306
  424.7 10.4 %shard_map.258 = (bf16[16,216,128]{2,1,0:T(8,128)(2,1)}, f32[128,1152]{1,0:T(8,128)S(1)}) custom-call(bf16[16,216,128]{2,1,0:T(8,128)(2,1)S(1)} %copy-done.1, bf16[1152,128]{1,0:T(8,128)(2,1)S(1)} %bitcast.225, f32[128,1152]{1,0:T(8,128)S(1)} %copy-done.5, s32[1152,2]{1,0:T(8,128)S(1)} %copy-done.3, f32[1152,2]{1,0:T(8,128)S(1)} %copy-done.14), custom_call_target="tpu_custom_call" | custom-call | flops 849346560 | bytes 3538944 | tf_op jit(solution)/shard_map/pallas_call | solution.py:261
  443.4 21.6 %all-to-all-done.11.in_ref = bf16[16,216,128]{2,1,0:T(8,128)(2,1)S(1)} async-done(((bf16[16,216,128]{2,1,0:T(8,128)(2,1)}), bf16[16,216,128]{2,1,0:T(8,128)(2,1)S(1)}, u32[]{:S(2)}, u32[]{:S(2)}) %all-to-all-start.11) | async-done | bytes 884768 | tf_op jit(solution)/shard_map/all_to_all | solution.py:306
  465.4 5.6 multiply_reduce_fusion.3
  482.3 5.0 all-to-all-start.12
  488.3 35.9 %all-to-all-done.12 = bf16[64,24,768]{2,1,0:T(8,128)(2,1)S(1)} async-done(((bf16[64,24,768]{2,1,0:T(8,128)(2,1)}), bf16[64,24,768]{2,1,0:T(8,128)(2,1)S(1)}, u32[]{:S(2)}, u32[]{:S(2)}) %all-to-all-start.12) | async-done | bytes 2359328 | tf_op jit(solution)/shard_map/all_to_all | solution.py:306
  526.6 20.8 %reduce-scatter.4.cloned.1.call-done = bf16[1,704,768]{2,1,0:T(8,128)(2,1)} async-done(((bf16[16,704,768]{2,1,0:T(8,128)(2,1)}), bf16[1,704,768]{2,1,0:T(8,128)(2,1)}) %reduce-scatter.4.cloned.1.call-update) | async-done | bytes 1081360
  557.7 6.3 %all-to-all-done.13 = bf16[4,80,768]{2,1,0:T(8,128)(2,1)S(1)} async-done(((bf16[4,80,768]{2,1,0:T(8,128)(2,1)}), bf16[4,80,768]{2,1,0:T(8,128)(2,1)S(1)}, u32[]{:S(2)}, u32[]{:S(2)}) %all-to-all-start.13) | async-done | bytes 491552 | tf_op jit(solution)/shard_map/all_to_all | solution.py:306
  (557 shorter events, 186.2 us)
Async XLA Ops:
  7.2 98.8 %all-gather.6.cloned.1.call-start = ((), (), s32[]{:S(2)}) async-start(), calls=%async_computation.15 | async-start | bytes 23777280 | tf_op jit(solution)/shard_map/all_gather | solution.py:379
  12.3 247.0 %all-gather.8.cloned.1.call-start = ((), (), s32[]{:S(2)}) async-start(), calls=%async_computation.16 | async-start | bytes 5013504 | tf_op jit(solution)/shard_map/all_gather | solution.py:380
  14.0 14.7 %all-to-all-start = ((bf16[16,8,128]{2,1,0:T(8,128)(2,1)}), bf16[16,8,128]{2,1,0:T(8,128)(2,1)S(1)}, u32[]{:S(2)}, u32[]{:S(2)}) async-start(bf16[16,8,128]{2,1,0:T(8,128)(2,1)} %broadcast_in_dim.172), calls=%async_computation | async-start | bytes 65536 | tf_op jit(solution)/shard_map/all_to_all | solution.py:306
  21.1 245.6 %all-gather.10.cloned.1.call-start = ((), (), s32[]{:S(2)}) async-start(), calls=%async_computation.17 | async-start | bytes 5013504 | tf_op jit(solution)/shard_map/all_gather | solution.py:381
  25.2 156.3 %copy-start.117 = (pred[1024]{0:T(1024)(128)(4,1)}, pred[1024]{0:T(1024)(128)(4,1)S(1)}, u32[]{:S(2)}) copy-start(pred[1024]{0:T(1024)(128)(4,1)S(1)} %get-tuple-element.214) | copy-start | bytes 3076
  25.2 156.3 %copy-start.122 = (pred[1024]{0:T(1024)(128)(4,1)}, pred[1024]{0:T(1024)(128)(4,1)S(1)}, u32[]{:S(2)}) copy-start(pred[1024]{0:T(1024)(128)(4,1)S(1)} %get-tuple-element.215) | copy-start | bytes 3076
  29.5 13.1 %all-to-all-start.1 = ((bf16[8,128,128]{2,1,0:T(8,128)(2,1)}), bf16[8,128,128]{2,1,0:T(8,128)(2,1)S(1)}, u32[]{:S(2)}, u32[]{:S(2)}) async-start(bf16[8,128,128]{2,1,0:T(8,128)(2,1)} %broadcast_in_dim.174), calls=%async_computation.1 | async-start | bytes 524288 | tf_op jit(solution)/shard_map/all_to_all | solution.py:306
  35.2 289.3 %copy-start.2 = (s32[1152,2]{1,0:T(8,128)}, s32[1152,2]{1,0:T(8,128)S(1)}, u32[]{:S(2)}) copy-start(s32[1152,2]{1,0:T(8,128)S(1)} %copy.232.start_ref) | copy-start | bytes 27652
  35.2 146.3 %copy-start.75 = (s32[1024]{0:T(1024)}, s32[1024]{0:T(1024)S(1)}, u32[]{:S(2)}) copy-start(s32[1024]{0:T(1024)S(1)} %get-tuple-element.218) | copy-start | bytes 12292
  35.2 146.3 %copy-start.80 = (s32[1024]{0:T(1024)}, s32[1024]{0:T(1024)S(1)}, u32[]{:S(2)}) copy-start(s32[1024]{0:T(1024)S(1)} %get-tuple-element.219) | copy-start | bytes 12292
  35.2 146.3 %copy-start.85 = (s32[1024]{0:T(1024)}, s32[1024]{0:T(1024)S(1)}, u32[]{:S(2)}) copy-start(s32[1024]{0:T(1024)S(1)} %get-tuple-element.220) | copy-start | bytes 12292
  35.2 146.3 %copy-start.90 = (s32[1024]{0:T(1024)}, s32[1024]{0:T(1024)S(1)}, u32[]{:S(2)}) copy-start(s32[1024]{0:T(1024)S(1)} %get-tuple-element.221) | copy-start | bytes 12292
  111.2 26.9 %all-to-all-start.2 = ((bf16[16,216,128]{2,1,0:T(8,128)(2,1)}), bf16[16,216,128]{2,1,0:T(8,128)(2,1)S(1)}, u32[]{:S(2)}, u32[]{:S(2)}) async-start(bf16[16,216,128]{2,1,0:T(8,128)(2,1)} %shard_map.248), calls=%async_computation.2 | async-start | bytes 1769472 | tf_op jit(solution)/shard_map/all_to_all | solution.py:306
  146.2 16.9 %all-to-all-start.3 = ((bf16[16,72,128]{2,1,0:T(8,128)(2,1)}), bf16[16,72,128]{2,1,0:T(8,128)(2,1)S(1)}, u32[]{:S(2)}, u32[]{:S(2)}) async-start(bf16[16,72,128]{2,1,0:T(8,128)(2,1)} %bitcast.30), calls=%async_computation.3 | async-start | bytes 589824 | tf_op jit(solution)/shard_map/all_to_all | solution.py:306
  187.0 19.3 %all-to-all-start.4 = ((bf16[16,216,128]{2,1,0:T(8,128)(2,1)}), bf16[16,216,128]{2,1,0:T(8,128)(2,1)S(1)}, u32[]{:S(2)}, u32[]{:S(2)}) async-start(bf16[16,216,128]{2,1,0:T(8,128)(2,1)} %shard_map.251), calls=%async_computation.4 | async-start | bytes 1769472 | tf_op jit(solution)/shard_map/all_to_all | solution.py:306
  214.4 17.0 %all-to-all-start.5 = ((bf16[16,72,128]{2,1,0:T(8,128)(2,1)}), bf16[16,72,128]{2,1,0:T(8,128)(2,1)S(1)}, u32[]{:S(2)}, u32[]{:S(2)}) async-start(bf16[16,72,128]{2,1,0:T(8,128)(2,1)} %bitcast.47), calls=%async_computation.5 | async-start | bytes 589824 | tf_op jit(solution)/shard_map/all_to_all | solution.py:306
  238.3 19.8 %all-to-all-start.6 = ((bf16[8,80,768]{2,1,0:T(8,128)(2,1)}), bf16[8,80,768]{2,1,0:T(8,128)(2,1)}, u32[]{:S(2)}, u32[]{:S(2)}) async-start(bf16[8,80,768]{2,1,0:T(8,128)(2,1)} %bitcast.242), calls=%async_computation.6 | async-start | bytes 1966080 | tf_op jit(solution)/shard_map/all_to_all | solution.py:306
  280.6 19.7 %all-to-all-start.7 = ((bf16[8,80,768]{2,1,0:T(8,128)(2,1)}), bf16[8,80,768]{2,1,0:T(8,128)(2,1)}, u32[]{:S(2)}, u32[]{:S(2)}) async-start(bf16[8,80,768]{2,1,0:T(8,128)(2,1)} %pad_maximum_fusion.4), calls=%async_computation.7 | async-start | bytes 1966080 | tf_op jit(solution)/shard_map/all_to_all | solution.py:306
  311.5 13.0 %all-to-all-start.8 = ((bf16[16,72,128]{2,1,0:T(8,128)(2,1)}), bf16[16,72,128]{2,1,0:T(8,128)(2,1)S(1)}, u32[]{:S(2)}, u32[]{:S(2)}) async-start(bf16[16,72,128]{2,1,0:T(8,128)(2,1)} %shard_map.254), calls=%async_computation.8 | async-start | bytes 589824 | tf_op jit(solution)/shard_map/all_to_all | solution.py:306
  337.8 18.4 %all-to-all-start.9 = ((bf16[16,216,128]{2,1,0:T(8,128)(2,1)}), bf16[16,216,128]{2,1,0:T(8,128)(2,1)S(1)}, u32[]{:S(2)}, u32[]{:S(2)}) async-start(bf16[16,216,128]{2,1,0:T(8,128)(2,1)} %get-tuple-element.22), calls=%async_computation.9 | async-start | bytes 1769472 | tf_op jit(solution)/shard_map/all_to_all | solution.py:306
  341.6 205.8 %reduce-scatter.4.cloned.1.call-start = ((), (), s32[]{:S(2)}) async-start(), calls=%async_computation.18 | async-start | bytes 18382848
  341.7 1.9 collective-permute-start.3
  380.3 4.9 collective-permute-start.2
  382.3 1.7 collective-permute-start.5
  382.5 2.5 collective-permute-start.6
  383.6 2.9 collective-permute-start.4
  407.7 17.0 %all-to-all-start.10 = ((bf16[16,72,128]{2,1,0:T(8,128)(2,1)}), bf16[16,72,128]{2,1,0:T(8,128)(2,1)S(1)}, u32[]{:S(2)}, u32[]{:S(2)}) async-start(bf16[16,72,128]{2,1,0:T(8,128)(2,1)} %shard_map.257), calls=%async_computation.10 | async-start | bytes 589824 | tf_op jit(solution)/shard_map/all_to_all | solution.py:306
  435.1 29.9 %all-to-all-start.11 = ((bf16[16,216,128]{2,1,0:T(8,128)(2,1)}), bf16[16,216,128]{2,1,0:T(8,128)(2,1)S(1)}, u32[]{:S(2)}, u32[]{:S(2)}) async-start(bf16[16,216,128]{2,1,0:T(8,128)(2,1)} %get-tuple-element.24), calls=%async_computation.11 | async-start | bytes 1769472 | tf_op jit(solution)/shard_map/all_to_all | solution.py:306
  471.5 2.4 collective-permute-start
  472.0 1.9 collective-permute-start.1
  482.3 41.9 %all-to-all-start.12 = ((bf16[64,24,768]{2,1,0:T(8,128)(2,1)}), bf16[64,24,768]{2,1,0:T(8,128)(2,1)S(1)}, u32[]{:S(2)}, u32[]{:S(2)}) async-start(bf16[64,24,768]{2,1,0:T(8,128)(2,1)} %fusion.32), calls=%async_computation.12 | async-start | bytes 4718592 | tf_op jit(solution)/shard_map/all_to_all | solution.py:306
  550.9 13.1 %all-to-all-start.13 = ((bf16[4,80,768]{2,1,0:T(8,128)(2,1)}), bf16[4,80,768]{2,1,0:T(8,128)(2,1)S(1)}, u32[]{:S(2)}, u32[]{:S(2)}) async-start(bf16[4,80,768]{2,1,0:T(8,128)(2,1)} %pad.30.clone), calls=%async_computation.13 | async-start | bytes 983040 | tf_op jit(solution)/shard_map/all_to_all | solution.py:306
  (138 other events, 1334.1 us)
Sparse Core Ops, SparseCore 0:
  12.5 93.4 all-gather.5
  108.1 62.9 all-gather.7
  173.2 62.9 all-gather.9
  402.8 144.5 reduce-scatter.3

commit v4 on v3

--- a/solution.py
+++ b/solution.py
@@ -53,6 +53,14 @@
     grad_x = inv * scaled - x * (inv * inv * inv) * mean
     grad_scales = jnp.sum(grad * x * inv, axis=0)
     return grad_x, grad_scales
+
+
+def gelu_pair(u):
+    root = 0.7978845608028654
+    squared = u * u
+    t = jnp.tanh(root * u * (1.0 + 0.044715 * squared))
+    half = 0.5 * (1.0 + t)
+    return u * half, half + 0.5 * u * (1.0 - t * t) * root * (1.0 + 3 * 0.044715 * squared)
 
 
 def gelu(u):
@@ -188,52 +196,142 @@
     )(values)
 
 
-def products_kernel(
+LINE_ROWS = 704
+EXPERT_ROWS = 384
+STEP = 256
+
+
+def rows_of(a, b, count):
+    return dot_outer(a[...], b[...]).reshape(SLOTS, count, -1)
+
+
+def put(out_ref, first, parts):
+    value = jnp.concatenate(parts, axis=1).astype(bf16)
+    out_ref[:, first : first + value.shape[1]] = value
+
+
+def expert_products_kernel(a_rows, b_due0, b_due1, b_due2, b_due3, a_hidden, b_rows, out_ref):
+    put(out_ref, 0, [rows_of(a_rows, b, 48) for b in (b_due0, b_due1, b_due2, b_due3)])
+    put(out_ref, 192, [rows_of(a_hidden, b_rows, 192)])
+
+
+def shared_products_kernel(
     a_qkv, b_q, b_k, b_v, a_out, b_out, a_in, b_in0, b_in1, b_in2, b_in3, a_zero, b_zero, a_second, b_second,
-    a_rows, b_due0, b_due1, b_due2, b_due3, a_hidden, b_rows, out_ref,
+    buffer_ref, out_ref, staged,
 ):
-    def rows(a, b, count):
-        return dot_outer(a[...], b[...]).reshape(SLOTS, count, -1)
-
-    def put(first, parts):
-        value = jnp.concatenate(parts, axis=1).astype(bf16)
-        out_ref[:, first : first + value.shape[1]] = value
-
-    put(0, [rows(a_qkv, b, 24) for b in (b_q, b_k, b_v)] + [rows(a_out, b_out, 24)])
-    put(96, [rows(a_in, b, 24) for b in (b_in0, b_in1, b_in2, b_in3)])
-    zero = rows(a_zero, b_zero, 24)
-    put(192, [zero, jnp.zeros_like(zero[:, :8])])
-    second = dot_outer(a_second[...], b_second[...]).reshape(12, SLOTS, 8, -1)
-    put(224, [second[j] for j in range(12)])
-    put(320, [rows(a_rows, b, 48) for b in (b_due0, b_due1, b_due2, b_due3)])
-    put(512, [rows(a_hidden, b_rows, 192)])
-
-
-def products(qkv, out, dense_in, zero, second, expert_in, expert_out):
-    step = 256
-    operands, specs = [], []
-
-    def whole(a):
+    block = pl.program_id(1)
+
+    @pl.when(block == 0)
+    def _():
+        put(staged, 0, [rows_of(a_qkv, b, 24) for b in (b_q, b_k, b_v)] + [rows_of(a_out, b_out, 24)])
+        put(staged, 96, [rows_of(a_in, b, 24) for b in (b_in0, b_in1, b_in2, b_in3)])
+        zero = rows_of(a_zero, b_zero, 24)
+        put(staged, 192, [zero, jnp.zeros_like(zero[:, :8])])
+        second = dot_outer(a_second[...], b_second[...]).reshape(12, SLOTS, 8, -1)
+        put(staged, 224, [second[j] for j in range(12)])
+
+    out_ref[...] = staged[:, pl.ds(pl.multiple_of(block * 64, 64), 64), :]
+
+
+def product_operands(pairs, counts):
+    operands, specs, flops = [], [], 0
+    for (a, b), count in zip(pairs, counts):
         operands.append(a)
-        specs.append(pl.BlockSpec(a.shape, lambda n: (0, 0)))
-
-    def columns(b, count):
+        specs.append(pl.BlockSpec(a.shape, lambda n, *rest: (0, 0)))
+        flops += 2 * a.size * b.shape[1]
         for j in range(count):
             operands.append(b)
-            specs.append(pl.BlockSpec((b.shape[0], step), lambda n, j=j: (0, n + j * (WIDTH // step))))
-
-    for (a, b), count in zip((qkv, out, dense_in, zero, second, expert_in, expert_out), (3, 1, 4, 1, 1, 4, 1)):
-        whole(a)
-        columns(b, count)
+            specs.append(
+                pl.BlockSpec((b.shape[0], STEP), lambda n, *rest, j=j: (0, n + j * (WIDTH // STEP)))
+            )
+    return operands, specs, flops
+
+
+def expert_products(expert_in, expert_out):
+    operands, specs, flops = product_operands((expert_in, expert_out), (4, 1))
     return pl.pallas_call(
-        products_kernel,
-        grid=(WIDTH // step,),
+        expert_products_kernel,
+        grid=(WIDTH // STEP,),
         in_specs=specs,
-        out_specs=pl.BlockSpec((SLOTS, 704, step), lambda n: (0, 0, n)),
-        out_shape=jax.ShapeDtypeStruct((SLOTS, 704, WIDTH), bf16),
+        out_specs=pl.BlockSpec((SLOTS, EXPERT_ROWS, STEP), lambda n: (0, 0, n)),
+        out_shape=jax.ShapeDtypeStruct((SLOTS, LINE_ROWS, WIDTH), bf16),
         compiler_params=LIMIT,
-        cost_estimate=pl.CostEstimate(flops=5200000000, bytes_accessed=30000000, transcendentals=0),
+        cost_estimate=pl.CostEstimate(flops=flops, bytes_accessed=15000000, transcendentals=0),
     )(*operands)
+
+
+def shared_products(pairs, buffer):
+    operands, specs, flops = product_operands(pairs, (3, 1, 4, 1, 1))
+    return pl.pallas_call(
+        shared_products_kernel,
+        grid=(WIDTH // STEP, (LINE_ROWS - EXPERT_ROWS) // 64),
+        in_specs=specs + [pl.BlockSpec(memory_space=pl.ANY)],
+        out_specs=pl.BlockSpec((SLOTS, 64, STEP), lambda n, r: (0, EXPERT_ROWS // 64 + r, n)),
+        out_shape=jax.ShapeDtypeStruct((SLOTS, LINE_ROWS, WIDTH), bf16),
+        scratch_shapes=[pltpu.VMEM((SLOTS, LINE_ROWS - EXPERT_ROWS, STEP), bf16)],
+        input_output_aliases={len(operands): 0},
+        compiler_params=LIMIT,
+        cost_estimate=pl.CostEstimate(flops=flops, bytes_accessed=15000000, transcendentals=0),
+    )(*operands, buffer)
+
+
+def expert_kernel(
+    arrived_ref, w_in_ref, w_out_ref, produced_ref, rows_ref, grads_ref, hidden_ref, due_ref, forward_acc, back_acc
+):
+    step = pl.program_id(0)
+
+    @pl.when(step == 0)
+    def _():
+        whole = arrived_ref[...].astype(f32)
+        rows_ref[...] = whole[:, :40].reshape(320, WIDTH).astype(bf16)
+        grads_ref[...] = whole[:, 40:].reshape(320, WIDTH).astype(bf16)
+        forward_acc[...] = jnp.zeros_like(forward_acc)
+        back_acc[...] = jnp.zeros_like(back_acc)
+
+    u = dot(rows_ref[...], w_in_ref[...])
+    grad_hidden = dot_back(grads_ref[...], w_out_ref[...])
+    hidden, slope = gelu_pair(u)
+    hidden = hidden.astype(bf16)
+    due = (grad_hidden * slope).astype(bf16)
+    hidden_ref[...] = hidden
+    due_ref[...] = due
+    forward_acc[...] += dot(hidden, w_out_ref[...])
+    back_acc[...] += dot_back(due, w_in_ref[...])
+
+    @pl.when(step == pl.num_programs(0) - 1)
+    def _():
+        parts = [a[...].reshape(EXPERTS, 40, WIDTH) for a in (forward_acc, back_acc)]
+        produced_ref[...] = jnp.concatenate(parts, axis=1).astype(bf16)
+
+
+def expert_block(arrived, w_in, w_out):
+    def fixed(shape):
+        return pl.BlockSpec(shape, lambda n: (0,) * len(shape))
+
+    rows = jax.ShapeDtypeStruct((320, WIDTH), bf16)
+    units = jax.ShapeDtypeStruct((320, FF), bf16)
+    return pl.pallas_call(
+        expert_kernel,
+        grid=(FF // 512,),
+        in_specs=[
+            fixed((EXPERTS, 80, WIDTH)),
+            pl.BlockSpec((WIDTH, 512), lambda n: (0, n)),
+            pl.BlockSpec((512, WIDTH), lambda n: (n, 0)),
+        ],
+        out_specs=(
+            fixed((EXPERTS, 80, WIDTH)),
+            fixed((320, WIDTH)),
+            fixed((320, WIDTH)),
+            pl.BlockSpec((320, 512), lambda n: (0, n)),
+            pl.BlockSpec((320, 512), lambda n: (0, n)),
+        ),
+        out_shape=(jax.ShapeDtypeStruct((EXPERTS, 80, WIDTH), bf16), rows, rows, units, units),
+        scratch_shapes=[pltpu.VMEM((320, WIDTH), f32), pltpu.VMEM((320, WIDTH), f32)],
+        compiler_params=LIMIT,
+        cost_estimate=pl.CostEstimate(
+            flops=8 * 320 * WIDTH * FF, bytes_accessed=15000000, transcendentals=320 * FF
+        ),
+    )(arrived, w_in, w_out)
 
 
 def staging(dtype, count):
@@ -430,15 +528,8 @@
     picked_grads = [(gates[:, k : k + 1] * grad_four).astype(bf16) for k in range(2)]
     sent = dot(scatter, jnp.concatenate([e] + picked_grads, axis=0)).astype(bf16)
     arrived = exchange(sent.reshape(EXPERTS, 80, WIDTH), ROW)
-    expert_rows = arrived[:, :40].reshape(320, WIDTH)
-    grad_rows = arrived[:, 40:].reshape(320, WIDTH)
-    ue = dot(expert_rows, w_expert_in)
-    he, gelu_back = jax.vjp(gelu, ue)
-    he = he.astype(bf16)
-    ye = dot(he, w_expert_out).astype(bf16)
-    due = gelu_back(dot_back(grad_rows, w_expert_out))[0].astype(bf16)
-    grad_sent = dot_back(due, w_expert_in).astype(bf16)
-    produced = jnp.concatenate([ye.reshape(EXPERTS, 40, WIDTH), grad_sent.reshape(EXPERTS, 40, WIDTH)], axis=1)
+    produced, expert_rows, grad_rows, he, due = expert_block(arrived, w_expert_in, w_expert_out)
+    buffer = expert_products((expert_rows, due), (he, grad_rows))
     returned = exchange(produced, ROW).reshape(EXPERTS * 80, WIDTH)
     collected = dot_outer(collect, returned)
     picked = [collected[ROWS : 2 * ROWS], collected[2 * ROWS :]]
@@ -450,7 +541,7 @@
     grad_router = dot_outer(e, dlogits.astype(bf16))
     grad_e = collected[:ROWS] + dot_back(dlogits.astype(bf16), w_router)
     grad_x, gain_four = normalize_back(grad_e, x3, inv_e, gains[3])
-    grad_three = grad_four + grad_x
+    grad_three = grad_four + grad_x + 0.0 * buffer[0, 0, 0].astype(f32)
 
 
     def share(a, b, line_first):
@@ -489,13 +580,11 @@
     got = other_core(jnp.concatenate([theirs, branch_two], axis=1))
     mine = jnp.concatenate([mine, got[:, : FF // 2]], axis=0)
     pair_second = (mine, jnp.concatenate([branch_two, got[:, FF // 2 :]], axis=0))
-    summed = products(
-        pair_qkv, pair_out, pair_in, pair_zero, pair_second, (expert_rows, due), (he, grad_rows)
-    )
+    summed = shared_products((pair_qkv, pair_out, pair_in, pair_zero, pair_second), buffer)
     early_sum = lax.optimization_barrier(
         lax.psum_scatter(summed, LINE, scatter_dimension=0, tiled=False)
     )
-    expert_sum = early_sum[320:]
+    expert_sum, early_sum = early_sum[:EXPERT_ROWS], early_sum[EXPERT_ROWS:]
 
     grad_zero, gain_one, branch_one, heads_one, tile_one = attend_backward(
         grad_one, x0, gains[0], qkv_zero, out_zero, places, bias[0], start, saved_one

time: 587 us -> 568 us (0.968)
  matrix products: 96.4 us -> 75.7 us
  waiting for transfers between devices: 242 us -> 222 us
  Pallas kernels: 56.7 us -> 72.6 us
    unnamed x5, waiting for transfers between devices: 22.2 us -> 1.41 us
    pallas_call x1 -> x3, Pallas kernels: 14.7 us -> 30.4 us  [the longest x1 11.6 us: shared_products(): pl.pallas_call(shared_products_kernel, grid=(WIDTH // STEP, (LINE_ROWS -...]
    dot_general x22 -> x20, matrix products: 48.1 us -> 36.9 us  [dot(): lax.dot_general(a, b, (((1,), (0,)), ((), ())), preferred_element_type=f32)]
    dot_general x11 -> x9, matrix products: 41.4 us -> 31.8 us  [dot_back(): lax.dot_general(a, b, (((1,), (1,)), ((), ())), preferred_element_type=f32)]
    unnamed x305 -> x349, local copies, waits for them, and re-layouts: 12.4 us -> 16.3 us
  transfers between devices with their start and end apart: 25 -> 25, of which waited for: 21 -> 20; matrix products, arithmetic and copies ran while one was open for 22% -> 20% of each run, Pallas kernels for 5% -> 7%
where the time goes in v4:
time: 568 us; the launch traced here: 557 us
  waiting for transfers between devices  222 us (39%)
  matrix products  75.7 us (13%)
  Pallas kernels  72.6 us (13%)
  starting transfers between devices  68.7 us (12%)
  local copies, waits for them, and re-layouts  51.9 us (9%)
  other arithmetic  48.7 us (9%)
  between operations  17.7 us (3%)
    all_to_all x14, waiting for transfers between devices, exchange(): return lax.all_to_all(blocks, axes, split_axis=0, concat_axis=0, tiled=True)  153 us
    all_to_all x14, starting transfers between devices, exchange(): return lax.all_to_all(blocks, axes, split_axis=0, concat_axis=0, tiled=True)  66.7 us
    all_gather x1, waiting for transfers between devices, on_device(): shared = lax.all_gather(pack, ALL, axis=0, tiled=True)  62.8 us
    dot_general x20, matrix products, dot(): lax.dot_general(a, b, (((1,), (0,)), ((), ())), preferred_element_type=f32)  36.9 us
    dot_general x9, matrix products, dot_back(): lax.dot_general(a, b, (((1,), (1,)), ((), ())), preferred_element_type=f32)  31.8 us
    pallas_call x2, Pallas kernels, head_backward(): pl.pallas_call(backward_kernel, out_shape=(jax.ShapeDtypeStruct((SLOTS, 3...  20.8 us
    select_n x2, other arithmetic, bias_tile(): result = jnp.where(distance >= first, entries[b], result)  20.2 us
    pallas_call x2, Pallas kernels, head_forward(): pl.pallas_call(forward_kernel, out_shape=(jax.ShapeDtypeStruct((GROUP, 2...  16.4 us
  transfers between devices with their start and end apart: 25, of which 20 were waited for; matrix products, arithmetic and copies ran while one was open for 20% of the time, Pallas kernels for 7%

profile of v4, /device:TPU:0, one launch (start us, length us, event | category | flops | bytes accessed | tf_op | source)
XLA Modules:
  0.0 557.0 jit_solution(18100931115632112433)
XLA Ops:
  14.7 7.1 %all-to-all-start = ((bf16[16,8,128]{2,1,0:T(8,128)(2,1)}), bf16[16,8,128]{2,1,0:T(8,128)(2,1)S(1)}, u32[]{:S(2)}, u32[]{:S(2)}) async-start(bf16[16,8,128]{2,1,0:T(8,128)(2,1)} %broadcast_in_dim.172), calls=%async_computation | async-start | bytes 65536 | tf_op jit(solution)/shard_map/all_to_all | solution.py:404
  24.9 4.5 all-to-all-done
  30.2 5.3 all-to-all-start.1
  36.2 7.1 %all-to-all-done.1 = bf16[8,128,128]{2,1,0:T(8,128)(2,1)S(1)} async-done(((bf16[8,128,128]{2,1,0:T(8,128)(2,1)}), bf16[8,128,128]{2,1,0:T(8,128)(2,1)S(1)}, u32[]{:S(2)}, u32[]{:S(2)}) %all-to-all-start.1) | async-done | bytes 262176 | tf_op jit(solution)/shard_map/all_to_all | solution.py:404
  43.8 62.8 %all-gather.6.cloned.1.call-done = bf16[1024,11520]{1,0:T(8,128)(2,1)} async-done(((bf16[8,11520]{1,0:T(8,128)(2,1)}), bf16[1024,11520]{1,0:T(8,128)(2,1)}) %all-gather.6.cloned.1.call-update) | async-done | bytes 23592976 | tf_op jit(solution)/shard_map/all_gather | solution.py:477
  111.8 6.8 %all-to-all-start.2 = ((bf16[16,216,128]{2,1,0:T(8,128)(2,1)}), bf16[16,216,128]{2,1,0:T(8,128)(2,1)S(1)}, u32[]{:S(2)}, u32[]{:S(2)}) async-start(bf16[16,216,128]{2,1,0:T(8,128)(2,1)} %shard_map.248), calls=%async_computation.2 | async-start | bytes 1769472 | tf_op jit(solution)/shard_map/all_to_all | solution.py:404
  120.3 10.3 %select_select_fusion.2.bias_ref = f32[128,1152]{1,0:T(8,128)S(1)} fusion(f32[]{:T(128)} %bitcast.28, f32[]{:T(128)} %bitcast.27, f32[]{:T(128)} %bitcast.26, f32[]{:T(128)} %bitcast.25, f32[]{:T(128)} %bitcast.24, f32[]{:T(128)} %bitcast.23, f32[]{:T(128)} %bitcast.22, f32[]{:T(128)} %bitcast.21, f32[]{:T(128)} %bitcast.20, f32[]{:T(128)} %bitcast.19, ...), kind=kLoop, calls=%fused_computation.171 | loop fusion | flops 5013504 | bytes 589888 | tf_op jit(solution)/shard_map/jit(_where)/select_n | solution.py:391
  130.6 8.5 %all-to-all-done.2.blocks_ref = bf16[16,216,128]{2,1,0:T(8,128)(2,1)S(1)} async-done(((bf16[16,216,128]{2,1,0:T(8,128)(2,1)}), bf16[16,216,128]{2,1,0:T(8,128)(2,1)S(1)}, u32[]{:S(2)}, u32[]{:S(2)}) %all-to-all-start.2) | async-done | bytes 884768 | tf_op jit(solution)/shard_map/all_to_all | solution.py:404
  139.0 8.2 %shard_map.249 = (bf16[1152,128]{1,0:T(8,128)(2,1)}, f32[1152,2]{1,0:T(8,128)S(1)}) custom-call(bf16[16,216,128]{2,1,0:T(8,128)(2,1)S(1)} %all-to-all-done.2.blocks_ref, f32[128,1152]{1,0:T(8,128)S(1)} %select_select_fusion.2.bias_ref, s32[1152,2]{1,0:T(8,128)S(1)} %copy.233.start_ref), custom_call_target="tpu_custom_call" | custom-call | flops 339738624 | bytes 1769472 | tf_op jit(solution)/shard_map/pallas_call | solution.py:342
  153.0 11.0 %all-to-all-done.3.in_ref = bf16[16,72,128]{2,1,0:T(8,128)(2,1)S(1)} async-done(((bf16[16,72,128]{2,1,0:T(8,128)(2,1)}), bf16[16,72,128]{2,1,0:T(8,128)(2,1)S(1)}, u32[]{:S(2)}, u32[]{:S(2)}) %all-to-all-start.3) | async-done | bytes 294944 | tf_op jit(solution)/shard_map/all_to_all | solution.py:404
  167.6 6.4 %multiply_convert_fusion = (bf16[144,3072]{1,0:T(8,128)(2,1)S(1)}, f32[144,3072]{1,0:T(8,128)}) fusion(bf16[1024,11520]{1,0:T(8,128)(2,1)} %all-gather.6.cloned.1.call-done, bf16[144,768]{1,0:T(8,128)(2,1)S(1)} %multiply_convert_fusion.3, s32[1024]{0:T(1024)S(1)} %get-tuple-element.224, s32[1024]{0:T(1024)S(1)} %get-tuple-element.227, ...), kind=kOutput, calls=%fused_computation.42 | convolution fusion | flops 1142095872 | bytes 9185280 | tf_op jit(solution)/shard_map/dot_general | solution.py:34
  190.8 10.0 %select_select_fusion.1.bias_ref = f32[128,1152]{1,0:T(8,128)S(1)} fusion(f32[]{:T(128)} %bitcast.46, f32[]{:T(128)} %bitcast.45, f32[]{:T(128)} %bitcast.44, f32[]{:T(128)} %bitcast.43, f32[]{:T(128)} %bitcast.42, f32[]{:T(128)} %bitcast.41, f32[]{:T(128)} %bitcast.40, f32[]{:T(128)} %bitcast.39, f32[]{:T(128)} %bitcast.38, f32[]{:T(128)} %bitcast.37, ...), kind=kLoop, calls=%fused_computation.170 | loop fusion | flops 5013504 | bytes 589888 | tf_op jit(solution)/shard_map/jit(_where)/select_n | solution.py:391
  205.6 8.3 %shard_map.252 = (bf16[1152,128]{1,0:T(8,128)(2,1)}, f32[1152,2]{1,0:T(8,128)S(1)}) custom-call(bf16[16,216,128]{2,1,0:T(8,128)(2,1)S(1)} %all-to-all-done.4.blocks_ref, f32[128,1152]{1,0:T(8,128)S(1)} %select_select_fusion.1.bias_ref, s32[1152,2]{1,0:T(8,128)S(1)} %copy.233.start_ref), custom_call_target="tpu_custom_call" | custom-call | flops 339738624 | bytes 1769472 | tf_op jit(solution)/shard_map/pallas_call | solution.py:342
  213.9 7.2 %all-to-all-start.5 = ((bf16[16,72,128]{2,1,0:T(8,128)(2,1)}), bf16[16,72,128]{2,1,0:T(8,128)(2,1)S(1)}, u32[]{:S(2)}, u32[]{:S(2)}) async-start(bf16[16,72,128]{2,1,0:T(8,128)(2,1)} %bitcast.47), calls=%async_computation.5 | async-start | bytes 589824 | tf_op jit(solution)/shard_map/all_to_all | solution.py:404
  222.9 10.7 %all-to-all-done.5.in_ref = bf16[16,72,128]{2,1,0:T(8,128)(2,1)S(1)} async-done(((bf16[16,72,128]{2,1,0:T(8,128)(2,1)}), bf16[16,72,128]{2,1,0:T(8,128)(2,1)S(1)}, u32[]{:S(2)}, u32[]{:S(2)}) %all-to-all-start.5) | async-done | bytes 294944 | tf_op jit(solution)/shard_map/all_to_all | solution.py:404
  244.6 5.3 dynamic-slice_reduce_fusion.1
  253.7 6.0 %all-to-all-done.6.arrived_ref = bf16[8,80,768]{2,1,0:T(8,128)(2,1)S(1)} async-done(((bf16[8,80,768]{2,1,0:T(8,128)(2,1)}), bf16[8,80,768]{2,1,0:T(8,128)(2,1)S(1)}, u32[]{:S(2)}, u32[]{:S(2)}) %all-to-all-start.6) | async-done | bytes 983072 | tf_op jit(solution)/shard_map/all_to_all | solution.py:404
  259.7 11.1 %shard_map.254 = (bf16[8,80,768]{2,1,0:T(8,128)(2,1)S(1)}, bf16[320,768]{1,0:T(8,128)(2,1)S(1)}, bf16[320,768]{1,0:T(8,128)(2,1)S(1)}, bf16[320,3072]{1,0:T(8,128)(2,1)S(1)}, bf16[320,3072]{1,0:T(8,128)(2,1)}) custom-call(bf16[8,80,768]{2,1,0:T(8,128)(2,1)S(1)} %all-to-all-done.6.arrived_ref, bf16[768,3072]{1,0:T(8,128)(2,1)} %bitcast.245, ...), custom_call_target="tpu_custom_call" | custom-call | flops 6039797760 | bytes 15000000 | tf_op jit(solution)/shard_map/pallas_call | solution.py:313
  280.8 7.7 %shard_map.255.buffer_ref = bf16[16,704,768]{2,1,0:T(8,128)(2,1)} custom-call(bf16[320,768]{1,0:T(8,128)(2,1)S(1)} %copy-done.11, bf16[320,3072]{1,0:T(8,128)(2,1)S(1)} %copy-done, bf16[320,3072]{1,0:T(8,128)(2,1)S(1)} %copy-done, bf16[320,3072]{1,0:T(8,128)(2,1)S(1)} %copy-done, bf16[320,3072]{1,0:T(8,128)(2,1)S(1)} %copy-done, ...), custom_call_target="tpu_custom_call" | custom-call | flops 3019898880 | bytes 15000000 | tf_op jit(solution)/shard_map/pallas_call | solution.py:252
  306.9 8.6 %all-to-all-done.8 = bf16[16,72,128]{2,1,0:T(8,128)(2,1)S(1)} async-done(((bf16[16,72,128]{2,1,0:T(8,128)(2,1)}), bf16[16,72,128]{2,1,0:T(8,128)(2,1)S(1)}, u32[]{:S(2)}, u32[]{:S(2)}) %all-to-all-start.8) | async-done | bytes 294944 | tf_op jit(solution)/shard_map/all_to_all | solution.py:404
  316.6 10.5 %shard_map.257 = (bf16[16,216,128]{2,1,0:T(8,128)(2,1)}, f32[128,1152]{1,0:T(8,128)S(1)}) custom-call(bf16[16,216,128]{2,1,0:T(8,128)(2,1)S(1)} %copy-done.5, bf16[1152,128]{1,0:T(8,128)(2,1)S(1)} %bitcast.199, f32[128,1152]{1,0:T(8,128)S(1)} %copy-done.9, s32[1152,2]{1,0:T(8,128)S(1)} %copy.233.start_ref, f32[1152,2]{1,0:T(8,128)S(1)} %copy-done.21), custom_call_target="tpu_custom_call" | custom-call | flops 849346560 | bytes 3538944 | tf_op jit(solution)/shard_map/pallas_call | solution.py:359
  333.2 12.3 %all-to-all-done.9.in_ref = bf16[16,216,128]{2,1,0:T(8,128)(2,1)S(1)} async-done(((bf16[16,216,128]{2,1,0:T(8,128)(2,1)}), bf16[16,216,128]{2,1,0:T(8,128)(2,1)S(1)}, u32[]{:S(2)}, u32[]{:S(2)}) %all-to-all-start.9) | async-done | bytes 884768 | tf_op jit(solution)/shard_map/all_to_all | solution.py:404
  345.8 6.2 %multiply_reduce_fusion.1 = (f32[768]{0:T(1024)}, f32[144]{0:T(256)S(1)}, f32[144,768]{1,0:T(8,128)}) fusion(f32[144,768]{1,0:T(8,128)} %copy-done.28, f32[144]{0:T(256)S(1)} %copy-done.82, f32[768]{0:T(1024)S(1)} %copy-done.68, s32[1024]{0:T(1024)S(1)} %copy-done.102, s32[1024]{0:T(1024)S(1)} %copy-done.98, s32[1024]{0:T(1024)S(1)} %copy-done.106, ...), kind=kOutput, calls=%fused_computation.207 | convolution fusion | flops 912284800 | bytes 6292608 | tf_op jit(solution)/shard_map/dot_general | solution.py:38
  363.5 7.4 %multiply_reduce_fusion.2 = (f32[768]{0:T(1024)}, f32[144]{0:T(256)S(1)}, f32[144,768]{1,0:T(8,128)}) fusion(f32[144,768]{1,0:T(8,128)S(1)} %copy-done.27, f32[144]{0:T(256)S(1)} %copy-done.80, f32[768]{0:T(1024)S(1)} %mul.552, s32[1024]{0:T(1024)S(1)} %copy-done.102, s32[1024]{0:T(1024)S(1)} %copy-done.98, s32[1024]{0:T(1024)S(1)} %copy-done.106, ...), kind=kOutput, calls=%fused_computation.208 | convolution fusion | flops 1138777216 | bytes 8086656 | tf_op jit(solution)/shard_map/dot_general | solution.py:38
  379.8 11.6 %shard_map.262 = bf16[16,704,768]{2,1,0:T(8,128)(2,1)} custom-call(bf16[288,384]{1,0:T(8,128)(2,1)S(1)} %pad_maximum_fusion.17.a_qkv, bf16[288,2304]{1,0:T(8,128)(2,1)S(1)} %pad_maximum_fusion.2.b_q.b_k.b_v, bf16[288,2304]{1,0:T(8,128)(2,1)S(1)} %pad_maximum_fusion.2.b_q.b_k.b_v, ...), custom_call_target="tpu_custom_call", output_to_operand_aliasing={{}: (15, {})} | custom-call | flops 2208301056 | bytes 15000000 | tf_op jit(solution)/shard_map/pallas_call | solution.py:265
  404.2 9.3 %all-to-all-done.10 = bf16[16,72,128]{2,1,0:T(8,128)(2,1)S(1)} async-done(((bf16[16,72,128]{2,1,0:T(8,128)(2,1)}), bf16[16,72,128]{2,1,0:T(8,128)(2,1)S(1)}, u32[]{:S(2)}, u32[]{:S(2)}) %all-to-all-start.10) | async-done | bytes 294944 | tf_op jit(solution)/shard_map/all_to_all | solution.py:404
  416.2 10.3 %shard_map.260 = (bf16[16,216,128]{2,1,0:T(8,128)(2,1)}, f32[128,1152]{1,0:T(8,128)S(1)}) custom-call(bf16[16,216,128]{2,1,0:T(8,128)(2,1)S(1)} %copy-done.3, bf16[1152,128]{1,0:T(8,128)(2,1)S(1)} %bitcast.198, f32[128,1152]{1,0:T(8,128)S(1)} %copy-done.7, s32[1152,2]{1,0:T(8,128)S(1)} %copy.233.start_ref, f32[1152,2]{1,0:T(8,128)S(1)} %copy-done.19), custom_call_target="tpu_custom_call" | custom-call | flops 849346560 | bytes 3538944 | tf_op jit(solution)/shard_map/pallas_call | solution.py:359
  434.6 21.4 %all-to-all-done.11.in_ref = bf16[16,216,128]{2,1,0:T(8,128)(2,1)S(1)} async-done(((bf16[16,216,128]{2,1,0:T(8,128)(2,1)}), bf16[16,216,128]{2,1,0:T(8,128)(2,1)S(1)}, u32[]{:S(2)}, u32[]{:S(2)}) %all-to-all-start.11) | async-done | bytes 884768 | tf_op jit(solution)/shard_map/all_to_all | solution.py:404
  456.4 6.1 %multiply_reduce_fusion.3 = (f32[768]{0:T(1024)S(1)}, f32[144]{0:T(256)}, f32[144,768]{1,0:T(8,128)}) fusion(f32[144]{0:T(256)S(1)} %copy-done.78, bf16[2,72,768]{2,1,0:T(8,128)(2,1)S(1)} %copy-done.32, f32[768]{0:T(1024)S(1)} %mul.544, s32[1024]{0:T(1024)S(1)} %copy-done.103, s32[1024]{0:T(1024)S(1)} %copy-done.99, s32[1024]{0:T(1024)S(1)} %copy-done.107, ...), kind=kOutput, calls=%fused_computation.209 | convolution fusion | flops 912505984 | bytes 6292608 | tf_op jit(solution)/shard_map/dot_general | solution.py:38
  474.5 5.6 %all-to-all-start.12 = ((bf16[64,24,768]{2,1,0:T(8,128)(2,1)}), bf16[64,24,768]{2,1,0:T(8,128)(2,1)S(1)}, u32[]{:S(2)}, u32[]{:S(2)}) async-start(bf16[64,24,768]{2,1,0:T(8,128)(2,1)} %fusion.15), calls=%async_computation.12 | async-start | bytes 4718592 | tf_op jit(solution)/shard_map/all_to_all | solution.py:404
  482.1 45.0 %all-to-all-done.12 = bf16[64,24,768]{2,1,0:T(8,128)(2,1)S(1)} async-done(((bf16[64,24,768]{2,1,0:T(8,128)(2,1)}), bf16[64,24,768]{2,1,0:T(8,128)(2,1)S(1)}, u32[]{:S(2)}, u32[]{:S(2)}) %all-to-all-start.12) | async-done | bytes 2359328 | tf_op jit(solution)/shard_map/all_to_all | solution.py:404
  538.9 5.8 %all-to-all-done.13 = bf16[4,80,768]{2,1,0:T(8,128)(2,1)S(1)} async-done(((bf16[4,80,768]{2,1,0:T(8,128)(2,1)}), bf16[4,80,768]{2,1,0:T(8,128)(2,1)S(1)}, u32[]{:S(2)}, u32[]{:S(2)}) %all-to-all-start.13) | async-done | bytes 491552 | tf_op jit(solution)/shard_map/all_to_all | solution.py:404
  (597 shorter events, 175.0 us)
Async XLA Ops:
  7.2 99.5 %all-gather.6.cloned.1.call-start = ((), (), s32[]{:S(2)}) async-start(), calls=%async_computation.15 | async-start | bytes 23777280 | tf_op jit(solution)/shard_map/all_gather | solution.py:477
  13.0 240.7 %all-gather.8.cloned.1.call-start = ((), (), s32[]{:S(2)}) async-start(), calls=%async_computation.16 | async-start | bytes 5013504 | tf_op jit(solution)/shard_map/all_gather | solution.py:478
  14.7 14.7 %all-to-all-start = ((bf16[16,8,128]{2,1,0:T(8,128)(2,1)}), bf16[16,8,128]{2,1,0:T(8,128)(2,1)S(1)}, u32[]{:S(2)}, u32[]{:S(2)}) async-start(bf16[16,8,128]{2,1,0:T(8,128)(2,1)} %broadcast_in_dim.172), calls=%async_computation | async-start | bytes 65536 | tf_op jit(solution)/shard_map/all_to_all | solution.py:404
  21.8 231.9 %all-gather.10.cloned.1.call-start = ((), (), s32[]{:S(2)}) async-start(), calls=%async_computation.17 | async-start | bytes 5013504 | tf_op jit(solution)/shard_map/all_gather | solution.py:479
  22.6 158.2 %copy-start.96 = (s32[1024]{0:T(1024)}, s32[1024]{0:T(1024)S(1)}, u32[]{:S(2)}) copy-start(s32[1024]{0:T(1024)S(1)} %get-tuple-element.227) | copy-start | bytes 12292
  22.6 211.2 %copy-start.93 = (s32[1024]{0:T(1024)}, s32[1024]{0:T(1024)S(1)}, u32[]{:S(2)}) copy-start(s32[1024]{0:T(1024)S(1)} %get-tuple-element.226) | copy-start | bytes 12292
  22.6 158.2 %copy-start.100 = (s32[1024]{0:T(1024)}, s32[1024]{0:T(1024)S(1)}, u32[]{:S(2)}) copy-start(s32[1024]{0:T(1024)S(1)} %get-tuple-element.224) | copy-start | bytes 12292
  22.6 158.2 %copy-start.104 = (s32[1024]{0:T(1024)}, s32[1024]{0:T(1024)S(1)}, u32[]{:S(2)}) copy-start(s32[1024]{0:T(1024)S(1)} %get-tuple-element.225) | copy-start | bytes 12292
  24.9 155.9 %copy-start.135 = (pred[1024]{0:T(1024)(128)(4,1)}, pred[1024]{0:T(1024)(128)(4,1)S(1)}, u32[]{:S(2)}) copy-start(pred[1024]{0:T(1024)(128)(4,1)S(1)} %get-tuple-element.220) | copy-start | bytes 3076
  24.9 155.9 %copy-start.139 = (pred[1024]{0:T(1024)(128)(4,1)}, pred[1024]{0:T(1024)(128)(4,1)S(1)}, u32[]{:S(2)}) copy-start(pred[1024]{0:T(1024)(128)(4,1)S(1)} %get-tuple-element.221) | copy-start | bytes 3076
  30.2 13.1 %all-to-all-start.1 = ((bf16[8,128,128]{2,1,0:T(8,128)(2,1)}), bf16[8,128,128]{2,1,0:T(8,128)(2,1)S(1)}, u32[]{:S(2)}, u32[]{:S(2)}) async-start(bf16[8,128,128]{2,1,0:T(8,128)(2,1)} %broadcast_in_dim.174), calls=%async_computation.1 | async-start | bytes 524288 | tf_op jit(solution)/shard_map/all_to_all | solution.py:404
  35.7 202.3 %copy-start.69 = (s32[144,2]{0,1:T(2,128)}, s32[144,2]{0,1:T(2,128)S(1)}, u32[]{:S(2)}) copy-start(s32[144,2]{0,1:T(2,128)S(1)} %eq.165) | copy-start | bytes 3460
  111.8 27.2 %all-to-all-start.2 = ((bf16[16,216,128]{2,1,0:T(8,128)(2,1)}), bf16[16,216,128]{2,1,0:T(8,128)(2,1)S(1)}, u32[]{:S(2)}, u32[]{:S(2)}) async-start(bf16[16,216,128]{2,1,0:T(8,128)(2,1)} %shard_map.248), calls=%async_computation.2 | async-start | bytes 1769472 | tf_op jit(solution)/shard_map/all_to_all | solution.py:404
  147.2 16.8 %all-to-all-start.3 = ((bf16[16,72,128]{2,1,0:T(8,128)(2,1)}), bf16[16,72,128]{2,1,0:T(8,128)(2,1)S(1)}, u32[]{:S(2)}, u32[]{:S(2)}) async-start(bf16[16,72,128]{2,1,0:T(8,128)(2,1)} %bitcast.30), calls=%async_computation.3 | async-start | bytes 589824 | tf_op jit(solution)/shard_map/all_to_all | solution.py:404
  186.2 19.4 %all-to-all-start.4 = ((bf16[16,216,128]{2,1,0:T(8,128)(2,1)}), bf16[16,216,128]{2,1,0:T(8,128)(2,1)S(1)}, u32[]{:S(2)}, u32[]{:S(2)}) async-start(bf16[16,216,128]{2,1,0:T(8,128)(2,1)} %shard_map.251), calls=%async_computation.4 | async-start | bytes 1769472 | tf_op jit(solution)/shard_map/all_to_all | solution.py:404
  213.9 19.7 %all-to-all-start.5 = ((bf16[16,72,128]{2,1,0:T(8,128)(2,1)}), bf16[16,72,128]{2,1,0:T(8,128)(2,1)S(1)}, u32[]{:S(2)}, u32[]{:S(2)}) async-start(bf16[16,72,128]{2,1,0:T(8,128)(2,1)} %bitcast.47), calls=%async_computation.5 | async-start | bytes 589824 | tf_op jit(solution)/shard_map/all_to_all | solution.py:404
  240.7 19.0 %all-to-all-start.6 = ((bf16[8,80,768]{2,1,0:T(8,128)(2,1)}), bf16[8,80,768]{2,1,0:T(8,128)(2,1)S(1)}, u32[]{:S(2)}, u32[]{:S(2)}) async-start(bf16[8,80,768]{2,1,0:T(8,128)(2,1)} %bitcast.60), calls=%async_computation.6 | async-start | bytes 1966080 | tf_op jit(solution)/shard_map/all_to_all | solution.py:404
  273.4 19.6 %all-to-all-start.7 = ((bf16[8,80,768]{2,1,0:T(8,128)(2,1)}), bf16[8,80,768]{2,1,0:T(8,128)(2,1)}, u32[]{:S(2)}, u32[]{:S(2)}) async-start(bf16[8,80,768]{2,1,0:T(8,128)(2,1)} %copy-done.1), calls=%async_computation.7 | async-start | bytes 1966080 | tf_op jit(solution)/shard_map/all_to_all | solution.py:404
  302.7 12.8 %all-to-all-start.8 = ((bf16[16,72,128]{2,1,0:T(8,128)(2,1)}), bf16[16,72,128]{2,1,0:T(8,128)(2,1)S(1)}, u32[]{:S(2)}, u32[]{:S(2)}) async-start(bf16[16,72,128]{2,1,0:T(8,128)(2,1)} %shard_map.256), calls=%async_computation.8 | async-start | bytes 589824 | tf_op jit(solution)/shard_map/all_to_all | solution.py:404
  327.1 18.4 %all-to-all-start.9 = ((bf16[16,216,128]{2,1,0:T(8,128)(2,1)}), bf16[16,216,128]{2,1,0:T(8,128)(2,1)S(1)}, u32[]{:S(2)}, u32[]{:S(2)}) async-start(bf16[16,216,128]{2,1,0:T(8,128)(2,1)} %get-tuple-element.32), calls=%async_computation.9 | async-start | bytes 1769472 | tf_op jit(solution)/shard_map/all_to_all | solution.py:404
  330.8 198.6 %reduce-scatter.4.cloned.1.call-start = ((), (), s32[]{:S(2)}) async-start(), calls=%async_computation.18 | async-start | bytes 18382848
  330.9 2.1 collective-permute-start.3
  373.1 1.7 collective-permute-start.5
  374.2 2.1 collective-permute-start.6
  374.2 3.2 collective-permute-start.2
  374.8 4.0 collective-permute-start.4
  396.5 17.0 %all-to-all-start.10 = ((bf16[16,72,128]{2,1,0:T(8,128)(2,1)}), bf16[16,72,128]{2,1,0:T(8,128)(2,1)S(1)}, u32[]{:S(2)}, u32[]{:S(2)}) async-start(bf16[16,72,128]{2,1,0:T(8,128)(2,1)} %shard_map.259), calls=%async_computation.10 | async-start | bytes 589824 | tf_op jit(solution)/shard_map/all_to_all | solution.py:404
  426.5 29.5 %all-to-all-start.11 = ((bf16[16,216,128]{2,1,0:T(8,128)(2,1)}), bf16[16,216,128]{2,1,0:T(8,128)(2,1)S(1)}, u32[]{:S(2)}, u32[]{:S(2)}) async-start(bf16[16,216,128]{2,1,0:T(8,128)(2,1)} %get-tuple-element.34), calls=%async_computation.11 | async-start | bytes 1769472 | tf_op jit(solution)/shard_map/all_to_all | solution.py:404
  463.0 2.4 collective-permute-start
  463.3 2.2 collective-permute-start.1
  474.5 52.6 %all-to-all-start.12 = ((bf16[64,24,768]{2,1,0:T(8,128)(2,1)}), bf16[64,24,768]{2,1,0:T(8,128)(2,1)S(1)}, u32[]{:S(2)}, u32[]{:S(2)}) async-start(bf16[64,24,768]{2,1,0:T(8,128)(2,1)} %fusion.15), calls=%async_computation.12 | async-start | bytes 4718592 | tf_op jit(solution)/shard_map/all_to_all | solution.py:404
  532.9 11.8 %all-to-all-start.13 = ((bf16[4,80,768]{2,1,0:T(8,128)(2,1)}), bf16[4,80,768]{2,1,0:T(8,128)(2,1)S(1)}, u32[]{:S(2)}, u32[]{:S(2)}) async-start(bf16[4,80,768]{2,1,0:T(8,128)(2,1)} %pad.30.clone), calls=%async_computation.13 | async-start | bytes 983040 | tf_op jit(solution)/shard_map/all_to_all | solution.py:404
  (159 other events, 1091.9 us)
Sparse Core Ops, SparseCore 0:
  13.2 93.4 all-gather.5
  108.8 62.7 all-gather.7
  173.7 63.1 all-gather.9
  391.6 135.6 reduce-scatter.3
